TPU v7x, 32 devices: a whole 2x2x4 slice. The times are simulated.
32 devices in a mesh: band: 16 (over z, y, x), shell: 2 (over core).
Axes of the slice: x: 2, y: 2, z: 4, core: 2. Of those that a mesh axis runs over, the one named last changes fastest.
Arguments:
- spectrum: float32 [2, 3, 2, 512, 512], P('shell', None, None, 'band'), parts along dimension 0, may hold values from -6 to 6
- capture_rate: float32 [2, 1024, 2048], P('shell', 'band'), parts along dimension 0, may hold values from 0.5 to 1500, as said below
- row_latitude: int32 [1024], replicated, may hold values from 0 to 1023, each once
- slot_wavenumber: int32 [512], replicated, may hold values from 0 to 511, each once
Outputs:
- transport: float32 [2, 3, 2, 512, 512], P('shell', None, None, 'band'), parts along dimension 0
There are 2 independent parts, one for each index of `shell`. A program takes and returns all parts, laid end to end along the dimension named above; an argument that names none is the same for every part. Nothing has to cross between parts.
Inputs may be any that keep to these rules, and one draw needn't show every extreme that they name: `row_latitude`: each latitude index appears once. `slot_wavenumber`: each wavenumber appears once. `capture_rate`: positive.
All inputs are finite; a program needn't handle non-finite values.
Results may differ from a plain program's by a relative error of at most 0.0013.
Values sent between devices are 32-bit elements; how exact they have to be, the bound alone decides.
No kernel may reach another device: no remote copies, remote signals or barrier semaphores. Data moves between devices by JAX's collectives and lax.ppermute only.
A program may use at most 128 MiB of HBM per device.

v0:
```python
import functools
import math

import jax
import jax.numpy as jnp
import numpy as np
from jax import lax
from jax.experimental import pallas as pl
from jax.experimental.pallas import tpu as pltpu
from jax.sharding import PartitionSpec as P

DEG = 512
NLAT = 1024
NLON = 2048
FIELDS = 3
HALF = NLAT // 2
CHAN = 2 * FIELDS
BLK = 8
ROWS = CHAN * BLK
CHUNK = 64
LANES = 128
KTILE = 256
BF = jnp.bfloat16
F32 = jnp.float32


def split_two(value):
    high = value.astype(BF)
    low = (value - high.astype(F32)).astype(BF)
    return high, low


def dot(lhs, rhs, contract_rhs=0):
    return lax.dot_general(
        lhs, rhs, (((1,), (contract_rhs,)), ((), ())), preferred_element_type=F32
    )


def latitude_rows():
    theta = np.pi * (np.arange(HALF) + 0.5) / NLAT
    index = np.arange(DEG, dtype=np.float64)
    log_terms = np.zeros(DEG)
    log_terms[1:] = 0.5 * np.log2((2.0 * index[1:] + 1.0) / (2.0 * index[1:]))
    rows = np.zeros((8, DEG))
    rows[0], rows[1], rows[2] = np.cos(theta), np.log2(np.sin(theta)), log_terms
    return rows.astype(np.float32)


def spread_matrix():
    spread = np.zeros((LANES, 2, 2, CHUNK // 2, BLK), np.float32)
    for half in range(2):
        for parity in range(2):
            for step in range(CHUNK // 2):
                spread[half * CHUNK + 2 * step + parity, half, parity, step, :] = 1.0
    return spread.reshape(LANES, 2 * 2 * (CHUNK // 2) * BLK).astype(BF)


def block_orders(slots_ref, first):
    sublane = lax.broadcasted_iota(jnp.int32, (BLK, LANES), 0)
    orders = jnp.zeros((BLK, LANES), jnp.int32)
    lowest = jnp.int32(DEG)
    for i in range(BLK):
        order = slots_ref[first + i]
        orders = jnp.where(sublane == i, order, orders)
        lowest = jnp.minimum(lowest, order)
    return orders[:, :1], lowest


def recursion_tables(order, rows_ref, alpha_ref, beta_ref):
    degree = lax.broadcasted_iota(jnp.int32, (BLK, DEG), 1).astype(F32)
    order_sq = order * order
    denominator = degree * degree - order_sq
    safe = jnp.where(denominator > 0, denominator, 1.0)
    alpha = jnp.sqrt((4.0 * degree * degree - 1.0) / safe)
    back = jnp.maximum((degree - 1.0) * (degree - 1.0) - order_sq, 0.0)
    beta = jnp.sqrt(back * (2.0 * degree + 1.0) / (safe * jnp.maximum(2.0 * degree - 3.0, 1.0)))
    alpha_ref[...] = jnp.where(degree > order, alpha, 0.0)
    beta_ref[...] = jnp.where(degree > order, beta, -1.0)
    terms = jnp.where(degree <= order, rows_ref[2:3, :], 0.0)
    norm = jnp.where(order > 0, 0.5 + jnp.sum(terms, axis=1, keepdims=True), 0.0)
    return norm + order * rows_ref[1:2, :]


def run_chunk(step, carry, cosine, alpha_ref, beta_ref, emit, beside):
    current, previous, log_scale = carry
    tile = pl.ds(pl.multiple_of(step // 2 * LANES, LANES), LANES)
    shift = (step % 2) * CHUNK
    alpha = pltpu.roll(alpha_ref[:, tile], shift, 1)
    beta = pltpu.roll(beta_ref[:, tile], shift, 1)
    scale = None
    for i in range(CHUNK):
        if i % 16 == 0:
            large = jnp.abs(current) > 2.0**60
            factor = jnp.where(large, 2.0**-60, 1.0)
            current = current * factor
            previous = previous * factor
            log_scale = jnp.where(large, log_scale + 60.0, log_scale)
            scale = jnp.exp2(jnp.maximum(log_scale, -200.0))
        newest = (alpha[:, i : i + 1] * cosine) * current - beta[:, i : i + 1] * previous
        current, previous = newest, current
        emit(i, newest * scale)
        if i % (CHUNK // len(beside)) == 1:
            beside[i // (CHUNK // len(beside))]()
    return current, previous, log_scale


def start_state(log_start):
    ones = jnp.ones((BLK, HALF), F32)
    return ones, ones, log_start


def fold_matrix(latitude_ref, fold_ref):
    latitude = latitude_ref[...]
    north = jnp.where(latitude < HALF, latitude, NLAT - 1 - latitude)
    sublane = lax.broadcasted_iota(jnp.int32, (HALF, NLAT), 0)
    fold_ref[...] = jnp.where(sublane == north, 1.0, 0.0).astype(BF)


def synth_kernel(
    dims, slots_ref, place_ref, spec_ref, rows_ref, spread_ref, latitude_ref, out_ref,
    alpha_ref, beta_ref, lhs_ref, high_a, low_a, high_b, low_b, acc_ref, fold_ref, coeff_ref,
):
    bands, row_count, modes, first_block, blocks, tiles = dims
    fold_matrix(latitude_ref, fold_ref)
    base = lax.axis_index("band") * modes + first_block * BLK
    south = latitude_ref[...] >= HALF
    spread_width = 4 * (CHUNK // 2) * BLK
    lane = lax.broadcasted_iota(jnp.int32, (2 * ROWS, spread_width), 1)
    sub = lax.broadcasted_iota(jnp.int32, (2 * ROWS, spread_width), 0)
    diagonal = (lane % BLK) == (sub % BLK)
    width = (CHUNK // 2) * BLK

    def one_block(block, unused):
        orders, lowest = block_orders(slots_ref, base + block * BLK)
        order = orders.astype(F32)
        log_start = recursion_tables(order, rows_ref, alpha_ref, beta_ref)
        for i in range(BLK):
            source = pl.ds(place_ref[base + block * BLK + i], 1)
            coeff_ref[:, i : i + 1, :] = spec_ref[:, source, :]
        degree = lax.broadcasted_iota(jnp.int32, (BLK, DEG), 1)
        coeffs = jnp.where((degree >= orders)[None], coeff_ref[...], 0.0)
        coeff_high, coeff_low = split_two(coeffs.reshape(ROWS, DEG))
        stacked = jnp.concatenate([coeff_high, coeff_low], 0)
        for t in range(DEG // LANES):
            wide = dot(stacked[:, t * LANES : (t + 1) * LANES], spread_ref[...])
            wide = jnp.where(diagonal, wide, 0.0).astype(BF)
            for half in range(2):
                lhs_ref[2 * t + half] = wide[:, half * 2 * width : (half + 1) * 2 * width]
        acc_ref[...] = jnp.zeros_like(acc_ref)
        cosine = jnp.broadcast_to(rows_ref[0:1, :], (BLK, HALF))

        def recur(step, carry, high_ref, low_ref, beside):
            held = {}

            def emit(i, value):
                if i % 4 < 2:
                    held[i] = value
                else:
                    pair = jnp.concatenate([held.pop(i - 2), value], 0)
                    high, low = split_two(pair)
                    at = (i // 4) * 2 * BLK
                    high_ref[i % 2, at : at + 2 * BLK, :] = high
                    low_ref[i % 2, at : at + 2 * BLK, :] = low

            return run_chunk(step, carry, cosine, alpha_ref, beta_ref, emit, beside)

        def add_products(step, high_ref, low_ref):
            def part(parity, columns):
                lhs = lhs_ref[step, :, parity * width : (parity + 1) * width]
                first = dot(lhs, high_ref[parity, :, columns])
                second = dot(lhs[:ROWS], low_ref[parity, :, columns])
                acc_ref[parity, :, columns] += first[:ROWS] + first[ROWS:] + second

            return [
                functools.partial(part, parity, slice(at, at + KTILE))
                for parity in range(2)
                for at in range(0, HALF, KTILE)
            ]

        def two_chunks(pair, carry):
            step = 2 * pair
            beside = add_products(jnp.maximum(step - 1, 0), high_b, low_b)
            carry = recur(step, carry, high_a, low_a, beside)
            beside = add_products(step, high_a, low_a)
            return recur(step + 1, carry, high_b, low_b, beside)

        high_b[...] = jnp.zeros_like(high_b)
        low_b[...] = jnp.zeros_like(low_b)
        chunks = DEG // CHUNK
        lax.fori_loop(lowest // (2 * CHUNK), chunks // 2, two_chunks, start_state(log_start))
        for part in add_products(chunks - 1, high_b, low_b):
            part()
        both = acc_ref[...].reshape(2 * ROWS, HALF)
        high, low = split_two(both)
        moved = dot(jnp.concatenate([high, low], 0), fold_ref[...])
        moved = moved[: 2 * ROWS] + moved[2 * ROWS :]
        sign = jnp.tile(1.0 - 2.0 * (orders % 2).astype(F32), (CHAN, 1))
        even, odd = moved[:ROWS], moved[ROWS:]
        values = jnp.where(south, sign * (even - odd), even + odd)
        for d in range(bands):
            parts = []
            for kind in range(2):
                for field in range(FIELDS):
                    c = field * 2 + kind
                    parts.append(
                        values[c * BLK : (c + 1) * BLK, d * row_count : (d + 1) * row_count]
                    )
            if CHAN * row_count < tiles * LANES:
                parts.append(jnp.zeros((BLK, tiles * LANES - CHAN * row_count), F32))
            joined = jnp.concatenate(parts, 1)
            for t in range(tiles):
                at = pl.ds(pl.multiple_of(t * blocks * BLK + block * BLK, BLK), BLK)
                out_ref[d, at, :] = joined[:, t * LANES : (t + 1) * LANES]
        return unused

    lax.fori_loop(0, blocks, one_block, 0)


def analyze_kernel(
    dims, total_row, slots_ref, place_ref, data_ref, total_ref, rows_ref, latitude_ref, out_ref,
    alpha_ref, beta_ref, high_a, low_a, high_b, low_b, weight_ref, result_ref, fold_ref, coeff_ref,
):
    bands, row_count, modes, first_block, blocks, tiles = dims
    fold_matrix(latitude_ref, fold_ref)
    base = lax.axis_index("band") * modes + first_block * BLK
    south = latitude_ref[...] >= HALF
    total = total_ref[0, total_row : total_row + 8]
    for d in range(1, bands):
        total = total + total_ref[d, total_row : total_row + 8]
    inverse = (1.0 / total)[:, :1]
    lane = lax.broadcasted_iota(jnp.int32, (KTILE, LANES), 1)
    sub = lax.broadcasted_iota(jnp.int32, (KTILE, LANES), 0)
    keep = (lane % BLK == sub % BLK) & (lane // ROWS == sub // BLK % 2)

    def one_block(block, unused):
        orders, lowest = block_orders(slots_ref, base + block * BLK)
        order = orders.astype(F32)
        log_start = recursion_tables(order, rows_ref, alpha_ref, beta_ref)
        sign = 1.0 - 2.0 * (orders % 2).astype(F32)
        evens, odds = [], []
        for c in range(CHAN):
            offset = ((c % 2) * FIELDS + c // 2) * row_count
            t, at = offset // LANES, offset % LANES
            rows = pl.ds(pl.multiple_of(t * blocks * BLK + block * BLK, BLK), BLK)
            values = jnp.concatenate(
                [data_ref[d, rows, :][:, at : at + row_count] for d in range(bands)], 1
            )
            flipped = sign * values
            evens.append(jnp.where(south, flipped, values))
            odds.append(jnp.where(south, -flipped, values))
        high, low = split_two(jnp.concatenate(evens + odds, 0))
        folded = dot(jnp.concatenate([high, low], 0), fold_ref[...], 1)
        folded = folded[: 2 * ROWS] + folded[2 * ROWS :]
        padded = jnp.concatenate([folded, jnp.zeros((LANES - 2 * ROWS, HALF), F32)], 0)
        high, low = split_two(padded.T)
        weight_ref[:, :LANES] = high
        weight_ref[:, LANES:] = low
        result_ref[...] = jnp.zeros_like(result_ref)
        cosine = jnp.broadcast_to(rows_ref[0:1, :], (BLK, HALF))

        def recur(step, carry, high_ref, low_ref, beside):
            held = {}

            def emit(i, value):
                if i % 2 == 0:
                    held[i] = value
                else:
                    pair = jnp.concatenate([held.pop(i - 1), value], 0)
                    high, low = split_two(pair)
                    at = (i // 2) * 2 * BLK
                    high_ref[at : at + 2 * BLK, :] = high
                    low_ref[at : at + 2 * BLK, :] = low

            return run_chunk(step, carry, cosine, alpha_ref, beta_ref, emit, beside)

        def store_products(step, high_ref, low_ref):
            def part(at):
                rows = slice(at, at + KTILE)
                first = dot(high_ref[rows, :], weight_ref[...])
                second = dot(low_ref[rows, :], weight_ref[:, :LANES])
                full = first[:, :LANES] + first[:, LANES:] + second
                picked = jnp.where(keep, full, 0.0).reshape(KTILE // BLK, BLK, LANES)
                to = pl.ds(pl.multiple_of(step * CHUNK + at // BLK, KTILE // BLK), KTILE // BLK)
                result_ref[to, :] = jnp.sum(picked, axis=1)

            return [functools.partial(part, at) for at in range(0, CHUNK * BLK, KTILE)]

        def two_chunks(pair, carry):
            step = 2 * pair
            beside = store_products(jnp.maximum(step - 1, 0), high_b, low_b)
            carry = recur(step, carry, high_a, low_a, beside)
            beside = store_products(step, high_a, low_a)
            return recur(step + 1, carry, high_b, low_b, beside)

        high_b[...] = jnp.zeros_like(high_b)
        low_b[...] = jnp.zeros_like(low_b)
        chunks = DEG // CHUNK
        lax.fori_loop(lowest // (2 * CHUNK), chunks // 2, two_chunks, start_state(log_start))
        for part in store_products(chunks - 1, high_b, low_b):
            part()
        turned = result_ref[...].T
        turned = turned[:ROWS] + turned[ROWS : 2 * ROWS]
        degree = lax.broadcasted_iota(jnp.int32, (BLK, DEG), 1)
        for c in range(CHAN):
            part = jnp.where(degree >= orders, turned[c * BLK : (c + 1) * BLK], 0.0)
            if c // 2 == FIELDS - 1:
                part = part * inverse
            coeff_ref[c] = part
        for i in range(BLK):
            target = pl.ds(place_ref[base + block * BLK + i], 1)
            out_ref[:, target, :] = coeff_ref[:, i : i + 1, :]
        return unused

    lax.fori_loop(0, blocks, one_block, 0)


def base_trig(order, first):
    lane = lax.broadcasted_iota(jnp.int32, order.shape, 1) + first
    phase = (order * lane) & (NLON - 1)
    quarter = (phase + NLON // 8) >> 9
    rest = (phase - quarter * (NLON // 4)).astype(F32) * (2.0 * math.pi / NLON)
    square = rest * rest
    sine = 1.0 / 362880.0
    for coef in (-1.0 / 5040.0, 1.0 / 120.0, -1.0 / 6.0, 1.0):
        sine = sine * square + coef
    sine = sine * rest
    cosine = 1.0 / 40320.0
    for coef in (-1.0 / 720.0, 1.0 / 24.0, -0.5, 1.0):
        cosine = cosine * square + coef
    swap = (quarter & 1) == 1
    cos_out = jnp.where(swap, sine, cosine)
    sin_out = jnp.where(swap, cosine, sine)
    cos_out = jnp.where(((quarter + 1) & 2) == 2, -cos_out, cos_out)
    sin_out = jnp.where((quarter & 2) == 2, -sin_out, sin_out)
    return cos_out, sin_out


def grid_kernel(
    dims, *refs,
):
    bands, row_count, modes, pieces, tiles, slots = dims
    data_refs = refs[:pieces]
    orders_ref, rate_ref, sine_ref = refs[pieces : pieces + 3]
    out_refs = refs[pieces + 3 : 2 * pieces + 3]
    (lhs_ref, cos_ref, sin_ref, turn_cos, turn_sin, high_ref, low_ref, weight_ref, acc_ref) = refs[
        2 * pieces + 3 :
    ]
    piece_modes = modes // pieces
    piece_slots = bands * piece_modes
    group = FIELDS * row_count
    padded = weight_ref.shape[0] // 2

    for p in range(pieces):
        columns = []
        for t in range(tiles):
            part = data_refs[p][:, t * piece_modes : (t + 1) * piece_modes, :]
            columns.append(part.reshape(piece_slots, LANES).T)
        turned = jnp.concatenate(columns, 0)
        for kind in range(2):
            high, low = split_two(turned[kind * group : (kind + 1) * group])
            at = kind * slots + p * piece_slots
            lhs_ref[:group, at : at + piece_slots] = high
            lhs_ref[group:, at : at + piece_slots] = low

    def prepare(step, unused):
        at = pl.ds(pl.multiple_of(step * 64, 64), 64)
        order = orders_ref[at, :]
        for t in range(KTILE // LANES):
            cosine, sine = base_trig(order, t * LANES)
            cos_ref[at, t * LANES : (t + 1) * LANES] = cosine
            sin_ref[at, t * LANES : (t + 1) * LANES] = sine
        eighth = order & 7
        root = math.sqrt(0.5)
        odd = (eighth & 1) == 1
        turned_cos = jnp.where(odd, root, jnp.where((eighth & 2) == 0, 1.0, 0.0))
        turned_sin = jnp.where(odd, root, jnp.where((eighth & 2) == 2, 1.0, 0.0))
        turn_cos[at, :] = jnp.where((eighth >= 3) & (eighth <= 5), -turned_cos, turned_cos)
        turn_sin[at, :] = jnp.where(eighth > 4, -turned_sin, turned_sin)
        return unused

    lax.fori_loop(0, slots // 64, prepare, 0)
    acc_ref[...] = jnp.zeros_like(acc_ref)
    weight_ref[...] = jnp.zeros_like(weight_ref)
    flux_scale = math.pi / (2.0 * NLAT * NLON * DEG)

    def one_tile(step, total):
        for s in range(0, slots, 64):
            rows_at = slice(s, s + 64)
            more_cos = jnp.tile(turn_cos[rows_at, :], (1, KTILE // LANES))
            more_sin = jnp.tile(turn_sin[rows_at, :], (1, KTILE // LANES))
            cosine, sine = cos_ref[rows_at, :], sin_ref[rows_at, :]
            cos_ref[rows_at, :] = cosine * more_cos - sine * more_sin
            sin_ref[rows_at, :] = sine * more_cos + cosine * more_sin
            high, low = split_two(cosine)
            high_ref[rows_at, :], low_ref[rows_at, :] = high, low
            high, low = split_two(sine)
            high_ref[slots + s : slots + s + 64, :] = high
            low_ref[slots + s : slots + s + 64, :] = low
        first = dot(lhs_ref[...], high_ref[...])
        second = dot(lhs_ref[:group, :], low_ref[...])
        fields = first[:group] + first[group:] + second
        weight = jnp.tile(sine_ref[...], (1, KTILE // LANES))
        columns = pl.ds(pl.multiple_of(step * KTILE, KTILE), KTILE)
        weighted_rate = rate_ref[:, columns] * weight
        scaled = fields[:row_count] * (weight * flux_scale)
        values = jnp.concatenate(
            [
                fields[row_count : 2 * row_count] * scaled,
                fields[2 * row_count :] * scaled,
                weighted_rate * fields[:row_count],
            ],
            0,
        )
        high, low = split_two(values)
        weight_ref[:group, :] = high
        weight_ref[padded : padded + group, :] = low
        first = dot(high_ref[...], weight_ref[...], 1)
        second = dot(low_ref[...], weight_ref[:padded, :], 1)
        acc_ref[...] += first[:, :padded] + first[:, padded:] + second
        return total + jnp.sum(weighted_rate.reshape(row_count // 8, 8, KTILE), axis=0)

    total = lax.fori_loop(0, NLON // KTILE, one_tile, jnp.zeros((8, KTILE), F32))
    out_refs[0][:, tiles * piece_modes :, :] = jnp.broadcast_to(jnp.sum(total), (bands, 8, LANES))
    for p in range(pieces):
        at = p * piece_slots
        joined = [
            acc_ref[at : at + piece_slots, :group],
            acc_ref[slots + at : slots + at + piece_slots, :group],
        ]
        if 2 * group < tiles * LANES:
            joined.append(jnp.zeros((piece_slots, tiles * LANES - 2 * group), F32))
        joined = jnp.concatenate(joined, 1)
        for t in range(tiles):
            part = joined[:, t * LANES : (t + 1) * LANES]
            out_refs[p][:, t * piece_modes : (t + 1) * piece_modes, :] = part.reshape(
                bands, piece_modes, LANES
            )


VMEM = pl.BlockSpec(memory_space=pltpu.VMEM)
SMEM = pl.BlockSpec(memory_space=pltpu.SMEM)
PIECES = 1


def per_device(spectrum, capture_rate, row_latitude, slot_wavenumber):
    bands = lax.axis_size("band")
    modes = spectrum.shape[3]
    row_count = capture_rate.shape[1]
    slots = slot_wavenumber.shape[0]
    blocks = modes // BLK
    pieces = min(PIECES, blocks)
    per_piece = blocks // pieces
    tiles = -(-CHAN * row_count // LANES)
    band_index = lax.axis_index("band")
    table = slot_wavenumber.reshape(bands, modes)
    rank = jnp.sum((table[:, None, :] < table[:, :, None]).astype(jnp.int32), 2)
    match = rank[:, None, :] == jnp.arange(modes, dtype=jnp.int32)[None, :, None]
    ordered = jnp.sum(jnp.where(match, table[:, None, :], 0), 2).reshape(slots)
    place_row = jnp.arange(modes, dtype=jnp.int32)[None, None, :]
    places = jnp.sum(jnp.where(match, place_row, 0), 2).reshape(slots)
    rows = jnp.asarray(latitude_rows())
    spread = jnp.asarray(spread_matrix())
    latitude = row_latitude.reshape(1, NLAT)
    coeffs = spectrum.reshape(CHAN, modes, DEG)
    params = pltpu.CompilerParams(vmem_limit_bytes=40 * 2**20)
    cost = pl.CostEstimate(
        flops=6 * 10**9 * per_piece, bytes_accessed=2**20, transcendentals=0
    )
    chunk_rows = tiles * per_piece * BLK

    def synth(p):
        dims = (bands, row_count, modes, p * per_piece, per_piece, tiles)
        return pl.pallas_call(
            lambda *refs: synth_kernel(dims, *refs),
            out_shape=jax.ShapeDtypeStruct((bands, chunk_rows, LANES), F32),
            in_specs=[SMEM, SMEM, VMEM, VMEM, VMEM, VMEM],
            out_specs=VMEM,
            scratch_shapes=[
                pltpu.VMEM((BLK, DEG), F32),
                pltpu.VMEM((BLK, DEG), F32),
                pltpu.VMEM((DEG // CHUNK, 2 * ROWS, CHUNK * BLK), BF),
                pltpu.VMEM((2, CHUNK // 2 * BLK, HALF), BF),
                pltpu.VMEM((2, CHUNK // 2 * BLK, HALF), BF),
                pltpu.VMEM((2, CHUNK // 2 * BLK, HALF), BF),
                pltpu.VMEM((2, CHUNK // 2 * BLK, HALF), BF),
                pltpu.VMEM((2, ROWS, HALF), F32),
                pltpu.VMEM((HALF, NLAT), BF),
                pltpu.VMEM((CHAN, BLK, DEG), F32),
            ],
            compiler_params=params,
            cost_estimate=cost,
            name="synth",
        )(
            ordered, places, coeffs, rows, spread, latitude,
        )

    def analyze(p, data, total):
        dims = (bands, row_count, modes, p * per_piece, per_piece, tiles)
        return pl.pallas_call(
            lambda *refs: analyze_kernel(dims, chunk_rows, *refs),
            out_shape=jax.ShapeDtypeStruct((CHAN, per_piece * BLK, DEG), F32),
            in_specs=[SMEM, SMEM, VMEM, VMEM, VMEM, VMEM],
            out_specs=VMEM,
            scratch_shapes=[
                pltpu.VMEM((BLK, DEG), F32),
                pltpu.VMEM((BLK, DEG), F32),
                pltpu.VMEM((CHUNK * BLK, HALF), BF),
                pltpu.VMEM((CHUNK * BLK, HALF), BF),
                pltpu.VMEM((CHUNK * BLK, HALF), BF),
                pltpu.VMEM((CHUNK * BLK, HALF), BF),
                pltpu.VMEM((HALF, 2 * LANES), BF),
                pltpu.VMEM((DEG, LANES), F32),
                pltpu.VMEM((HALF, NLAT), BF),
                pltpu.VMEM((CHAN, BLK, DEG), F32),
            ],
            compiler_params=params,
            cost_estimate=cost,
            name="analyze",
        )(ordered, places, data, total, rows, latitude)

    def exchange(value):
        return lax.all_to_all(value, "band", split_axis=0, concat_axis=0, tiled=True)

    received = [exchange(synth(p)) for p in range(pieces)]

    my_latitudes = lax.dynamic_slice_in_dim(row_latitude, band_index * row_count, row_count)
    row_sine = jnp.sin(jnp.pi * (my_latitudes.astype(F32) + 0.5) / NLAT)
    row_sine = jnp.broadcast_to(row_sine[:, None], (row_count, LANES))
    orders = ordered.reshape(bands, pieces, per_piece * BLK).transpose(1, 0, 2)
    orders = jnp.broadcast_to(orders.reshape(slots, 1), (slots, LANES))
    group = FIELDS * row_count
    padded = -(-group // LANES) * LANES
    dims = (bands, row_count, modes, pieces, tiles, slots)
    outs = pl.pallas_call(
        lambda *refs: grid_kernel(dims, *refs),
        out_shape=[
            jax.ShapeDtypeStruct((bands, chunk_rows + (8 if p == 0 else 0), LANES), F32)
            for p in range(pieces)
        ],
        in_specs=[VMEM] * (pieces + 3),
        out_specs=[VMEM] * pieces,
        scratch_shapes=[
            pltpu.VMEM((2 * group, 2 * slots), BF),
            pltpu.VMEM((slots, KTILE), F32),
            pltpu.VMEM((slots, KTILE), F32),
            pltpu.VMEM((slots, LANES), F32),
            pltpu.VMEM((slots, LANES), F32),
            pltpu.VMEM((2 * slots, KTILE), BF),
            pltpu.VMEM((2 * slots, KTILE), BF),
            pltpu.VMEM((2 * padded, KTILE), BF),
            pltpu.VMEM((2 * slots, padded), F32),
        ],
        compiler_params=params,
        name="grid",
    )(*received, orders, capture_rate.reshape(row_count, NLON), row_sine)
    returned = [exchange(out) for out in outs]
    parts = [analyze(p, returned[p], returned[0]) for p in range(pieces)]
    result = parts[0] if pieces == 1 else jnp.concatenate(parts, 1)
    return result.reshape(1, FIELDS, 2, modes, DEG)


def solution(mesh):
    return jax.shard_map(
        per_device,
        mesh=mesh,
        in_specs=(P("shell", None, None, "band", None), P("shell", "band", None), P(), P()),
        out_specs=P("shell", None, None, "band", None),
        check_vma=False,
    )
```

profile of v0, /device:TPU:0, one launch (start us, length us, event | category | flops | bytes accessed | tf_op | source)
XLA Modules:
  0.0 107.5 jit_solution(3522870664415307190)
XLA Ops:
  0.0 0.8 lt.18
  0.8 0.5 convert_reduce_fusion
  1.2 0.6 select_reduce_fusion
  1.8 0.0 copy-start.4
  1.9 0.1 reshape.24.refs_1_
  1.9 0.0 copy-start.2
  1.9 0.1 reshape.23.refs_0_
  2.0 0.6 copy-done.4
  2.6 0.1 copy-done.2
  2.6 0.0 copy-start.1
  2.6 1.0 copy-done.1
  3.6 0.0 copy-start.3
  3.6 0.9 copy-done.3
  4.6 14.9 %synth.1 = f32[16,96,128]{2,1,0:T(8,128)} custom-call(s32[512]{0:T(512)S(1)} %reshape.23.refs_0_, s32[512]{0:T(512)S(1)} %reshape.24.refs_1_, f32[6,32,512]{2,1,0:T(8,128)S(1)} %bitcast.5, f32[8,512]{1,0:T(8,128)S(1)} %copy-done.4, bf16[128,1024]{1,0:T(8,128)(2,1)S(1)} %copy-done.3, s32[1,1024]{1,0:T(1,128)S(1)} %bitcast.6), custom_call_target="tpu_custom_call" | custom-call | flops 24000000000 | bytes 1048576 | tf_op jit(solution)/shard_map/synth/pallas_call | solution.py:473
  19.5 0.0 copy-start
  19.5 10.2 %all-to-all-start = ((f32[16,96,128]{2,1,0:T(8,128)}), f32[16,96,128]{2,1,0:T(8,128)S(1)}, u32[]{:S(2)}, u32[]{:S(2)}) async-start(f32[16,96,128]{2,1,0:T(8,128)} %synth.1), calls=%async_computation | async-start | bytes 1572864 | tf_op jit(solution)/shard_map/all_to_all | solution.py:522
  29.7 0.1 multiply_sine_fusion
  29.8 19.6 %all-to-all-done.refs_0_ = f32[16,96,128]{2,1,0:T(8,128)S(1)} async-done(((f32[16,96,128]{2,1,0:T(8,128)}), f32[16,96,128]{2,1,0:T(8,128)S(1)}, u32[]{:S(2)}, u32[]{:S(2)}) %all-to-all-start) | async-done | bytes 786464 | tf_op jit(solution)/shard_map/all_to_all | solution.py:522
  49.4 0.1 broadcast_in_dim.37.refs_3_
  49.5 0.1 broadcast_in_dim.36.refs_1_
  49.6 0.0 copy-done
  49.6 14.4 %grid.1 = f32[16,104,128]{2,1,0:T(8,128)S(1)} custom-call(f32[16,96,128]{2,1,0:T(8,128)S(1)} %all-to-all-done.refs_0_, s32[512,128]{1,0:T(8,128)S(1)} %broadcast_in_dim.36.refs_1_, f32[64,2048]{1,0:T(8,128)S(1)} %bitcast.4, f32[64,128]{1,0:T(8,128)S(1)} %broadcast_in_dim.37.refs_3_), custom_call_target="tpu_custom_call" | custom-call | tf_op jit(solution)/shard_map/grid/pallas_call | solution.py:534
  64.0 26.2 %all_to_all.10.refs_2_.refs_3_ = f32[16,104,128]{2,1,0:T(8,128)S(1)} all-to-all(f32[16,104,128]{2,1,0:T(8,128)S(1)} %grid.1), channel_id=1, replica_groups=mesh['band'=16,'shell'=2] {'band'}, dimensions={0} | all-to-all | bytes 1703936 | tf_op jit(solution)/shard_map/all_to_all | solution.py:522
  90.2 17.3 %analyze.1 = f32[6,32,512]{2,1,0:T(8,128)} custom-call(s32[512]{0:T(512)S(1)} %reshape.23.refs_0_, s32[512]{0:T(512)S(1)} %reshape.24.refs_1_, f32[16,104,128]{2,1,0:T(8,128)S(1)} %all_to_all.10.refs_2_.refs_3_, f32[16,104,128]{2,1,0:T(8,128)S(1)} %all_to_all.10.refs_2_.refs_3_, f32[8,512]{1,0:T(8,128)S(1)} %copy-done.4, s32[1,1024]{1,0:T(1,128)S(1)} %bitcast.7), custom_call_target="tpu_custom_call" | custom-call | flops 24000000000 | bytes 1048576 | tf_op jit(solution)/shard_map/analyze/pallas_call | solution.py:499
Async XLA Ops:
  1.8 0.7 copy-start.4
  1.9 0.7 copy-start.2
  2.6 1.0 copy-start.1
  3.6 0.9 copy-start.3
  19.5 30.2 %copy-start = (f32[1,64,2048]{2,1,0:T(8,128)S(1)}, f32[1,64,2048]{2,1,0:T(8,128)}, u32[]{:S(2)}) copy-start(f32[1,64,2048]{2,1,0:T(8,128)} %param.7) | copy-start | bytes 1572868
  19.5 29.9 %all-to-all-start = ((f32[16,96,128]{2,1,0:T(8,128)}), f32[16,96,128]{2,1,0:T(8,128)S(1)}, u32[]{:S(2)}, u32[]{:S(2)}) async-start(f32[16,96,128]{2,1,0:T(8,128)} %synth.1), calls=%async_computation | async-start | bytes 1572864 | tf_op jit(solution)/shard_map/all_to_all | solution.py:522
where the time goes:
time: 109 us; the launch traced here: 107 us
  Pallas kernels  46.6 us (43%)
  blocking collectives  26.2 us (24%)
  waiting for transfers between devices  19.6 us (18%)
  starting transfers between devices  10.2 us (9%)
  local copies, waits for them, and re-layouts  3.67 us (3%)
  other arithmetic  1.19 us (1%)
    all_to_all x1, blocking collectives, exchange(): lax.all_to_all(value, 'band', split_axis=0, concat_axis=0, tiled=True)  26.2 us
    all_to_all x1, waiting for transfers between devices, exchange(): lax.all_to_all(value, 'band', split_axis=0, concat_axis=0, tiled=True)  19.6 us
    pallas_call x1, Pallas kernels, analyze(): pl.pallas_call(lambda *refs: analyze_kernel(dims, chunk_rows, *refs), out...  17.3 us
    pallas_call x1, Pallas kernels, synth(): pl.pallas_call(lambda *refs: synth_kernel(dims, *refs), out_shape=jax.Sha...  14.9 us
    pallas_call x1, Pallas kernels, per_device(): pl.pallas_call(lambda *refs: grid_kernel(dims, *refs), out_shape=[jax.Sha...  14.4 us
    all_to_all x1, starting transfers between devices, exchange(): lax.all_to_all(value, 'band', split_axis=0, concat_axis=0, tiled=True)  10.2 us
    unnamed x10, local copies, waits for them, and re-layouts  2.56 us
  transfers between devices with their start and end apart: 1, of which 1 were waited for; matrix products, arithmetic and copies ran while one was open for 0% of the time, Pallas kernels for 0%

commit v1 on v0

--- a/solution.py
+++ b/solution.py
@@ -117,7 +117,7 @@
 
 
 def synth_kernel(
-    dims, slots_ref, place_ref, spec_ref, rows_ref, spread_ref, latitude_ref, out_ref,
+    dims, slots_ref, place_ref, spec_ref, rows_ref, spread_ref, latitude_ref, out_refs,
     alpha_ref, beta_ref, lhs_ref, high_a, low_a, high_b, low_b, acc_ref, fold_ref, coeff_ref,
 ):
     bands, row_count, modes, first_block, blocks, tiles = dims
@@ -210,23 +210,23 @@
             joined = jnp.concatenate(parts, 1)
             for t in range(tiles):
                 at = pl.ds(pl.multiple_of(t * blocks * BLK + block * BLK, BLK), BLK)
-                out_ref[d, at, :] = joined[:, t * LANES : (t + 1) * LANES]
+                out_refs[d][at, :] = joined[:, t * LANES : (t + 1) * LANES]
         return unused
 
     lax.fori_loop(0, blocks, one_block, 0)
 
 
 def analyze_kernel(
-    dims, total_row, slots_ref, place_ref, data_ref, total_ref, rows_ref, latitude_ref, out_ref,
+    dims, total_row, data_refs, slots_ref, place_ref, rows_ref, latitude_ref, out_ref,
     alpha_ref, beta_ref, high_a, low_a, high_b, low_b, weight_ref, result_ref, fold_ref, coeff_ref,
 ):
     bands, row_count, modes, first_block, blocks, tiles = dims
     fold_matrix(latitude_ref, fold_ref)
     base = lax.axis_index("band") * modes + first_block * BLK
     south = latitude_ref[...] >= HALF
-    total = total_ref[0, total_row : total_row + 8]
+    total = data_refs[0][total_row : total_row + 8]
     for d in range(1, bands):
-        total = total + total_ref[d, total_row : total_row + 8]
+        total = total + data_refs[d][total_row : total_row + 8]
     inverse = (1.0 / total)[:, :1]
     lane = lax.broadcasted_iota(jnp.int32, (KTILE, LANES), 1)
     sub = lax.broadcasted_iota(jnp.int32, (KTILE, LANES), 0)
@@ -243,7 +243,7 @@
             t, at = offset // LANES, offset % LANES
             rows = pl.ds(pl.multiple_of(t * blocks * BLK + block * BLK, BLK), BLK)
             values = jnp.concatenate(
-                [data_ref[d, rows, :][:, at : at + row_count] for d in range(bands)], 1
+                [data_refs[d][rows, :][:, at : at + row_count] for d in range(bands)], 1
             )
             flipped = sign * values
             evens.append(jnp.where(south, flipped, values))
@@ -338,29 +338,25 @@
 def grid_kernel(
     dims, *refs,
 ):
-    bands, row_count, modes, pieces, tiles, slots = dims
-    data_refs = refs[:pieces]
-    orders_ref, rate_ref, sine_ref = refs[pieces : pieces + 3]
-    out_refs = refs[pieces + 3 : 2 * pieces + 3]
+    bands, row_count, modes, tiles, slots = dims
+    data_refs = refs[:bands]
+    orders_ref, rate_ref, sine_ref = refs[bands : bands + 3]
+    out_refs = refs[bands + 3 : 2 * bands + 3]
     (lhs_ref, cos_ref, sin_ref, turn_cos, turn_sin, high_ref, low_ref, weight_ref, acc_ref) = refs[
-        2 * pieces + 3 :
+        2 * bands + 3 :
     ]
-    piece_modes = modes // pieces
-    piece_slots = bands * piece_modes
     group = FIELDS * row_count
     padded = weight_ref.shape[0] // 2
 
-    for p in range(pieces):
-        columns = []
-        for t in range(tiles):
-            part = data_refs[p][:, t * piece_modes : (t + 1) * piece_modes, :]
-            columns.append(part.reshape(piece_slots, LANES).T)
-        turned = jnp.concatenate(columns, 0)
-        for kind in range(2):
-            high, low = split_two(turned[kind * group : (kind + 1) * group])
-            at = kind * slots + p * piece_slots
-            lhs_ref[:group, at : at + piece_slots] = high
-            lhs_ref[group:, at : at + piece_slots] = low
+    columns = []
+    for t in range(tiles):
+        part = [data_refs[d][t * modes : (t + 1) * modes, :] for d in range(bands)]
+        columns.append(jnp.concatenate(part, 0).T)
+    turned = jnp.concatenate(columns, 0)
+    for kind in range(2):
+        high, low = split_two(turned[kind * group : (kind + 1) * group])
+        lhs_ref[:group, kind * slots : (kind + 1) * slots] = high
+        lhs_ref[group:, kind * slots : (kind + 1) * slots] = low
 
     def prepare(step, unused):
         at = pl.ds(pl.multiple_of(step * 64, 64), 64)
@@ -420,26 +416,20 @@
         return total + jnp.sum(weighted_rate.reshape(row_count // 8, 8, KTILE), axis=0)
 
     total = lax.fori_loop(0, NLON // KTILE, one_tile, jnp.zeros((8, KTILE), F32))
-    out_refs[0][:, tiles * piece_modes :, :] = jnp.broadcast_to(jnp.sum(total), (bands, 8, LANES))
-    for p in range(pieces):
-        at = p * piece_slots
-        joined = [
-            acc_ref[at : at + piece_slots, :group],
-            acc_ref[slots + at : slots + at + piece_slots, :group],
-        ]
-        if 2 * group < tiles * LANES:
-            joined.append(jnp.zeros((piece_slots, tiles * LANES - 2 * group), F32))
-        joined = jnp.concatenate(joined, 1)
+    total = jnp.broadcast_to(jnp.sum(total), (8, LANES))
+    joined = [acc_ref[:slots, :group], acc_ref[slots:, :group]]
+    if 2 * group < tiles * LANES:
+        joined.append(jnp.zeros((slots, tiles * LANES - 2 * group), F32))
+    joined = jnp.concatenate(joined, 1)
+    for d in range(bands):
         for t in range(tiles):
-            part = joined[:, t * LANES : (t + 1) * LANES]
-            out_refs[p][:, t * piece_modes : (t + 1) * piece_modes, :] = part.reshape(
-                bands, piece_modes, LANES
-            )
+            part = joined[d * modes : (d + 1) * modes, t * LANES : (t + 1) * LANES]
+            out_refs[d][t * modes : (t + 1) * modes, :] = part
+        out_refs[d][tiles * modes :, :] = total
 
 
 VMEM = pl.BlockSpec(memory_space=pltpu.VMEM)
 SMEM = pl.BlockSpec(memory_space=pltpu.SMEM)
-PIECES = 1
 
 
 def per_device(spectrum, capture_rate, row_latitude, slot_wavenumber):
@@ -448,8 +438,7 @@
     row_count = capture_rate.shape[1]
     slots = slot_wavenumber.shape[0]
     blocks = modes // BLK
-    pieces = min(PIECES, blocks)
-    per_piece = blocks // pieces
+    per_piece = blocks
     tiles = -(-CHAN * row_count // LANES)
     band_index = lax.axis_index("band")
     table = slot_wavenumber.reshape(bands, modes)
@@ -460,7 +449,13 @@
     places = jnp.sum(jnp.where(match, place_row, 0), 2).reshape(slots)
     rows = jnp.asarray(latitude_rows())
     spread = jnp.asarray(spread_matrix())
-    latitude = row_latitude.reshape(1, NLAT)
+
+    def partner_rows(table):
+        partner = band_index ^ jnp.arange(bands, dtype=jnp.int32)
+        chosen = partner[:, None] == jnp.arange(bands, dtype=jnp.int32)[None, :]
+        return jnp.sum(jnp.where(chosen[:, :, None], table[None], 0), 1)
+
+    latitude = partner_rows(row_latitude.reshape(bands, row_count)).reshape(1, NLAT)
     coeffs = spectrum.reshape(CHAN, modes, DEG)
     params = pltpu.CompilerParams(vmem_limit_bytes=40 * 2**20)
     cost = pl.CostEstimate(
@@ -471,10 +466,10 @@
     def synth(p):
         dims = (bands, row_count, modes, p * per_piece, per_piece, tiles)
         return pl.pallas_call(
-            lambda *refs: synth_kernel(dims, *refs),
-            out_shape=jax.ShapeDtypeStruct((bands, chunk_rows, LANES), F32),
+            lambda *refs: synth_kernel(dims, *refs[:6], refs[6 : 6 + bands], *refs[6 + bands :]),
+            out_shape=[jax.ShapeDtypeStruct((chunk_rows, LANES), F32)] * bands,
             in_specs=[SMEM, SMEM, VMEM, VMEM, VMEM, VMEM],
-            out_specs=VMEM,
+            out_specs=[VMEM] * bands,
             scratch_shapes=[
                 pltpu.VMEM((BLK, DEG), F32),
                 pltpu.VMEM((BLK, DEG), F32),
@@ -494,12 +489,12 @@
             ordered, places, coeffs, rows, spread, latitude,
         )
 
-    def analyze(p, data, total):
+    def analyze(p, data):
         dims = (bands, row_count, modes, p * per_piece, per_piece, tiles)
         return pl.pallas_call(
-            lambda *refs: analyze_kernel(dims, chunk_rows, *refs),
+            lambda *refs: analyze_kernel(dims, chunk_rows, refs[:bands], *refs[bands:]),
             out_shape=jax.ShapeDtypeStruct((CHAN, per_piece * BLK, DEG), F32),
-            in_specs=[SMEM, SMEM, VMEM, VMEM, VMEM, VMEM],
+            in_specs=[VMEM] * bands + [SMEM, SMEM, VMEM, VMEM],
             out_specs=VMEM,
             scratch_shapes=[
                 pltpu.VMEM((BLK, DEG), F32),
@@ -516,29 +511,30 @@
             compiler_params=params,
             cost_estimate=cost,
             name="analyze",
-        )(ordered, places, data, total, rows, latitude)
-
-    def exchange(value):
-        return lax.all_to_all(value, "band", split_axis=0, concat_axis=0, tiled=True)
-
-    received = [exchange(synth(p)) for p in range(pieces)]
+        )(*data, ordered, places, rows, latitude)
+
+    def exchange(chunks):
+        received = [chunks[0]]
+        for k in range(1, bands):
+            pairs = [(i, i ^ k) for i in range(bands)]
+            received.append(lax.ppermute(chunks[k], "band", pairs))
+        return received
+
+    received = exchange(synth(0))
 
     my_latitudes = lax.dynamic_slice_in_dim(row_latitude, band_index * row_count, row_count)
     row_sine = jnp.sin(jnp.pi * (my_latitudes.astype(F32) + 0.5) / NLAT)
     row_sine = jnp.broadcast_to(row_sine[:, None], (row_count, LANES))
-    orders = ordered.reshape(bands, pieces, per_piece * BLK).transpose(1, 0, 2)
-    orders = jnp.broadcast_to(orders.reshape(slots, 1), (slots, LANES))
+    orders = partner_rows(ordered.reshape(bands, modes)).reshape(slots, 1)
+    orders = jnp.broadcast_to(orders, (slots, LANES))
     group = FIELDS * row_count
     padded = -(-group // LANES) * LANES
-    dims = (bands, row_count, modes, pieces, tiles, slots)
+    dims = (bands, row_count, modes, tiles, slots)
     outs = pl.pallas_call(
         lambda *refs: grid_kernel(dims, *refs),
-        out_shape=[
-            jax.ShapeDtypeStruct((bands, chunk_rows + (8 if p == 0 else 0), LANES), F32)
-            for p in range(pieces)
-        ],
-        in_specs=[VMEM] * (pieces + 3),
-        out_specs=[VMEM] * pieces,
+        out_shape=[jax.ShapeDtypeStruct((chunk_rows + 8, LANES), F32)] * bands,
+        in_specs=[VMEM] * (bands + 3),
+        out_specs=[VMEM] * bands,
         scratch_shapes=[
             pltpu.VMEM((2 * group, 2 * slots), BF),
             pltpu.VMEM((slots, KTILE), F32),
@@ -553,9 +549,7 @@
         compiler_params=params,
         name="grid",
     )(*received, orders, capture_rate.reshape(row_count, NLON), row_sine)
-    returned = [exchange(out) for out in outs]
-    parts = [analyze(p, returned[p], returned[0]) for p in range(pieces)]
-    result = parts[0] if pieces == 1 else jnp.concatenate(parts, 1)
+    result = analyze(0, exchange(outs))
     return result.reshape(1, FIELDS, 2, modes, DEG)
 
 

time: 109 us -> 121 us (1.11)
  starting transfers between devices: 10.2 us -> 55.8 us
  blocking collectives: 26.2 us -> 0 us
  waiting for transfers between devices: 19.6 us -> 9.95 us
    ppermute x0 -> x30, starting transfers between devices: none -> 55.8 us  [exchange(): received.append(lax.ppermute(chunks[k], 'band', pairs))]
    all_to_all x1 -> x0, blocking collectives: 26.2 us -> none  [exchange(): lax.all_to_all(value, 'band', split_axis=0, concat_axis=0, tiled=True)]
    all_to_all x1 -> x0, waiting for transfers between devices: 19.6 us -> none  [exchange(): lax.all_to_all(value, 'band', split_axis=0, concat_axis=0, tiled=True)]
    all_to_all x1 -> x0, starting transfers between devices: 10.2 us -> none  [exchange(): lax.all_to_all(value, 'band', split_axis=0, concat_axis=0, tiled=True)]
    ppermute x0 -> x30, waiting for transfers between devices: none -> 9.95 us  [exchange(): received.append(lax.ppermute(chunks[k], 'band', pairs))]
    unnamed x10 -> x12, local copies, waits for them, and re-layouts: 2.56 us -> 3.68 us
  transfers between devices with their start and end apart: 1 -> 30, of which waited for: 1 -> 6; matrix products, arithmetic and copies ran while one was open for 0% -> 0% of each run, Pallas kernels for 0% -> 0%
where the time goes in v1:
time: 121 us; the launch traced here: 119 us
  starting transfers between devices  55.8 us (46%)
  Pallas kernels  47.7 us (39%)
  waiting for transfers between devices  9.95 us (8%)
  local copies, waits for them, and re-layouts  4.33 us (4%)
  other arithmetic  1.5 us (1%)
    ppermute x30, starting transfers between devices, exchange(): received.append(lax.ppermute(chunks[k], 'band', pairs))  55.8 us
    pallas_call x1, Pallas kernels, analyze(): pl.pallas_call(lambda *refs: analyze_kernel(dims, chunk_rows, refs[:bands...  18.3 us
    pallas_call x1, Pallas kernels, synth(): pl.pallas_call(lambda *refs: synth_kernel(dims, *refs[:6], refs[6:6 + ban...  14.9 us
    pallas_call x1, Pallas kernels, per_device(): pl.pallas_call(lambda *refs: grid_kernel(dims, *refs), out_shape=[jax.Sha...  14.5 us
    ppermute x30, waiting for transfers between devices, exchange(): received.append(lax.ppermute(chunks[k], 'band', pairs))  9.95 us
    unnamed x12, local copies, waits for them, and re-layouts  3.68 us
  transfers between devices with their start and end apart: 30, of which 6 were waited for; matrix products, arithmetic and copies ran while one was open for 0% of the time, Pallas kernels for 0%

profile of v1, /device:TPU:0, one launch (start us, length us, event | category | flops | bytes accessed | tf_op | source)
XLA Modules:
  0.0 119.4 jit_solution(11304072001196461547)
XLA Ops:
  1.2 0.6 select_reduce_fusion
  3.4 1.0 copy-done.1
  4.4 0.9 copy-done.2
  5.4 14.9 %synth.1 = (f32[96,128]{1,0:T(8,128)S(1)}, f32[96,128]{1,0:T(8,128)S(1)}, f32[96,128]{1,0:T(8,128)S(1)}, f32[96,128]{1,0:T(8,128)S(1)}, f32[96,128]{1,0:T(8,128)...) custom-call(s32[512]{0:T(512)S(1)} %reshape.50.refs_0_.refs_16_, ...), custom_call_target="tpu_custom_call" | custom-call | flops 24000000000 | bytes 1048576 | tf_op jit(solution)/shard_map/synth/pallas_call | solution.py:468
  20.2 3.9 %collective-permute-start = (f32[96,128]{1,0:T(8,128)S(1)}, f32[96,128]{1,0:T(8,128)S(1)}, u32[]{:S(2)}, u32[]{:S(2)}) collective-permute-start(f32[96,128]{1,0:T(8,128)S(1)} %get-tuple-element.38), channel_id=1, source_target_pairs={{0,2},{2,0},{4,6},{6,4},{8,10},{10,8},{12,14},{14,12},{16,18},{18,... | collective-permute-start | bytes 147464 | tf_op jit(solution)/shard_map/ppermute | solution.py:520
  24.1 2.4 %collective-permute-start.1 = (f32[96,128]{1,0:T(8,128)S(1)}, f32[96,128]{1,0:T(8,128)S(1)}, u32[]{:S(2)}, u32[]{:S(2)}) collective-permute-start(f32[96,128]{1,0:T(8,128)S(1)} %get-tuple-element.39), channel_id=1, source_target_pairs={{0,4},{2,6},{4,0},{6,2},{8,12},{10,14},{12,8},{14,10},{16,20},{18,... | collective-permute-start | bytes 147464 | tf_op jit(solution)/shard_map/ppermute | solution.py:520
  26.5 1.6 %collective-permute-start.3 = (f32[96,128]{1,0:T(8,128)S(1)}, f32[96,128]{1,0:T(8,128)S(1)}, u32[]{:S(2)}, u32[]{:S(2)}) collective-permute-start(f32[96,128]{1,0:T(8,128)S(1)} %get-tuple-element.41), channel_id=1, source_target_pairs={{0,8},{2,10},{4,12},{6,14},{8,0},{10,2},{12,4},{14,6},{16,24},{18,... | collective-permute-start | bytes 147464 | tf_op jit(solution)/shard_map/ppermute | solution.py:520
  28.1 1.3 %collective-permute-start.4 = (f32[96,128]{1,0:T(8,128)S(1)}, f32[96,128]{1,0:T(8,128)S(1)}, u32[]{:S(2)}, u32[]{:S(2)}) collective-permute-start(f32[96,128]{1,0:T(8,128)S(1)} %get-tuple-element.42), channel_id=1, source_target_pairs={{0,10},{2,8},{4,14},{6,12},{8,2},{10,0},{12,6},{14,4},{16,26},{18,... | collective-permute-start | bytes 147464 | tf_op jit(solution)/shard_map/ppermute | solution.py:520
  29.4 3.0 %collective-permute-start.5 = (f32[96,128]{1,0:T(8,128)S(1)}, f32[96,128]{1,0:T(8,128)S(1)}, u32[]{:S(2)}, u32[]{:S(2)}) collective-permute-start(f32[96,128]{1,0:T(8,128)S(1)} %get-tuple-element.43), channel_id=1, source_target_pairs={{0,12},{2,14},{4,8},{6,10},{8,4},{10,6},{12,0},{14,2},{16,28},{18,... | collective-permute-start | bytes 147464 | tf_op jit(solution)/shard_map/ppermute | solution.py:520
  32.5 2.6 %collective-permute-start.7 = (f32[96,128]{1,0:T(8,128)S(1)}, f32[96,128]{1,0:T(8,128)S(1)}, u32[]{:S(2)}, u32[]{:S(2)}) collective-permute-start(f32[96,128]{1,0:T(8,128)S(1)} %get-tuple-element.45), channel_id=1, source_target_pairs={{0,16},{2,18},{4,20},{6,22},{8,24},{10,26},{12,28},{14,30},{16,0},... | collective-permute-start | bytes 147464 | tf_op jit(solution)/shard_map/ppermute | solution.py:520
  35.1 1.3 %collective-permute-start.8 = (f32[96,128]{1,0:T(8,128)S(1)}, f32[96,128]{1,0:T(8,128)S(1)}, u32[]{:S(2)}, u32[]{:S(2)}) collective-permute-start(f32[96,128]{1,0:T(8,128)S(1)} %get-tuple-element.46), channel_id=1, source_target_pairs={{0,18},{2,16},{4,22},{6,20},{8,26},{10,24},{12,30},{14,28},{16,2},... | collective-permute-start | bytes 147464 | tf_op jit(solution)/shard_map/ppermute | solution.py:520
  36.4 3.9 %collective-permute-start.9 = (f32[96,128]{1,0:T(8,128)S(1)}, f32[96,128]{1,0:T(8,128)S(1)}, u32[]{:S(2)}, u32[]{:S(2)}) collective-permute-start(f32[96,128]{1,0:T(8,128)S(1)} %get-tuple-element.47), channel_id=1, source_target_pairs={{0,20},{2,22},{4,16},{6,18},{8,28},{10,30},{12,24},{14,26},{16,4},... | collective-permute-start | bytes 147464 | tf_op jit(solution)/shard_map/ppermute | solution.py:520
  40.5 3.3 %collective-permute-start.11 = (f32[96,128]{1,0:T(8,128)S(1)}, f32[96,128]{1,0:T(8,128)S(1)}, u32[]{:S(2)}, u32[]{:S(2)}) collective-permute-start(f32[96,128]{1,0:T(8,128)S(1)} %get-tuple-element.49), channel_id=1, source_target_pairs={{0,24},{2,26},{4,28},{6,30},{8,16},{10,18},{12,20},{14,22},{16,8},... | collective-permute-start | bytes 147464 | tf_op jit(solution)/shard_map/ppermute | solution.py:520
  43.8 1.4 %collective-permute-start.12 = (f32[96,128]{1,0:T(8,128)S(1)}, f32[96,128]{1,0:T(8,128)S(1)}, u32[]{:S(2)}, u32[]{:S(2)}) collective-permute-start(f32[96,128]{1,0:T(8,128)S(1)} %get-tuple-element.50), channel_id=1, source_target_pairs={{0,26},{2,24},{4,30},{6,28},{8,18},{10,16},{12,22},{14,20},{16,10}... | collective-permute-start | bytes 147464 | tf_op jit(solution)/shard_map/ppermute | solution.py:520
  45.2 4.0 %collective-permute-start.13 = (f32[96,128]{1,0:T(8,128)S(1)}, f32[96,128]{1,0:T(8,128)S(1)}, u32[]{:S(2)}, u32[]{:S(2)}) collective-permute-start(f32[96,128]{1,0:T(8,128)S(1)} %get-tuple-element.51), channel_id=1, source_target_pairs={{0,28},{2,30},{4,24},{6,26},{8,20},{10,22},{12,16},{14,18},{16,12}... | collective-permute-start | bytes 147464 | tf_op jit(solution)/shard_map/ppermute | solution.py:520
  49.2 0.9 collective-permute-start.14
  50.3 0.9 collective-permute-done.12.refs_13_
  51.2 1.2 %collective-permute-done.13.refs_14_ = f32[96,128]{1,0:T(8,128)S(1)} collective-permute-done((f32[96,128]{1,0:T(8,128)S(1)}, f32[96,128]{1,0:T(8,128)S(1)}, u32[]{:S(2)}, u32[]{:S(2)}) %collective-permute-start.13) | collective-permute-done | bytes 49184 | tf_op jit(solution)/shard_map/ppermute | solution.py:520
  52.4 4.4 %collective-permute-done.14.refs_15_ = f32[96,128]{1,0:T(8,128)S(1)} collective-permute-done((f32[96,128]{1,0:T(8,128)S(1)}, f32[96,128]{1,0:T(8,128)S(1)}, u32[]{:S(2)}, u32[]{:S(2)}) %collective-permute-start.14) | collective-permute-done | bytes 49184 | tf_op jit(solution)/shard_map/ppermute | solution.py:520
  57.1 14.5 %grid.1 = (f32[104,128]{1,0:T(8,128)S(1)}, f32[104,128]{1,0:T(8,128)S(1)}, f32[104,128]{1,0:T(8,128)S(1)}, f32[104,128]{1,0:T(8,128)S(1)}, f32[104,128]{1,0:T(8,...) custom-call(f32[96,128]{1,0:T(8,128)S(1)} %get-tuple-element.37.refs, ...), custom_call_target="tpu_custom_call" | custom-call | tf_op jit(solution)/shard_map/grid/pallas_call | solution.py:533
  71.5 1.5 %collective-permute-start.15 = (f32[104,128]{1,0:T(8,128)S(1)}, f32[104,128]{1,0:T(8,128)S(1)}, u32[]{:S(2)}, u32[]{:S(2)}) collective-permute-start(f32[104,128]{1,0:T(8,128)S(1)} %get-tuple-element.54), channel_id=1, source_target_pairs={{0,2},{2,0},{4,6},{6,4},{8,10},{10,8},{12,14},{14,12},{16,18},{18,... | collective-permute-start | bytes 159752 | tf_op jit(solution)/shard_map/ppermute | solution.py:520
  73.0 2.1 %collective-permute-start.17 = (f32[104,128]{1,0:T(8,128)S(1)}, f32[104,128]{1,0:T(8,128)S(1)}, u32[]{:S(2)}, u32[]{:S(2)}) collective-permute-start(f32[104,128]{1,0:T(8,128)S(1)} %get-tuple-element.56), channel_id=1, source_target_pairs={{0,6},{2,4},{4,2},{6,0},{8,14},{10,12},{12,10},{14,8},{16,22},{18,... | collective-permute-start | bytes 159752 | tf_op jit(solution)/shard_map/ppermute | solution.py:520
  75.1 2.9 %collective-permute-start.19 = (f32[104,128]{1,0:T(8,128)S(1)}, f32[104,128]{1,0:T(8,128)S(1)}, u32[]{:S(2)}, u32[]{:S(2)}) collective-permute-start(f32[104,128]{1,0:T(8,128)S(1)} %get-tuple-element.58), channel_id=1, source_target_pairs={{0,10},{2,8},{4,14},{6,12},{8,2},{10,0},{12,6},{14,4},{16,26},{18,... | collective-permute-start | bytes 159752 | tf_op jit(solution)/shard_map/ppermute | solution.py:520
  78.3 2.7 %collective-permute-start.21 = (f32[104,128]{1,0:T(8,128)S(1)}, f32[104,128]{1,0:T(8,128)S(1)}, u32[]{:S(2)}, u32[]{:S(2)}) collective-permute-start(f32[104,128]{1,0:T(8,128)S(1)} %get-tuple-element.60), channel_id=1, source_target_pairs={{0,14},{2,12},{4,10},{6,8},{8,6},{10,4},{12,2},{14,0},{16,30},{18,... | collective-permute-start | bytes 159752 | tf_op jit(solution)/shard_map/ppermute | solution.py:520
  81.0 3.8 %collective-permute-start.23 = (f32[104,128]{1,0:T(8,128)S(1)}, f32[104,128]{1,0:T(8,128)S(1)}, u32[]{:S(2)}, u32[]{:S(2)}) collective-permute-start(f32[104,128]{1,0:T(8,128)S(1)} %get-tuple-element.62), channel_id=1, source_target_pairs={{0,18},{2,16},{4,22},{6,20},{8,26},{10,24},{12,30},{14,28},{16,2},... | collective-permute-start | bytes 159752 | tf_op jit(solution)/shard_map/ppermute | solution.py:520
  84.7 3.9 %collective-permute-start.25 = (f32[104,128]{1,0:T(8,128)S(1)}, f32[104,128]{1,0:T(8,128)S(1)}, u32[]{:S(2)}, u32[]{:S(2)}) collective-permute-start(f32[104,128]{1,0:T(8,128)S(1)} %get-tuple-element.64), channel_id=1, source_target_pairs={{0,22},{2,20},{4,18},{6,16},{8,30},{10,28},{12,26},{14,24},{16,6},... | collective-permute-start | bytes 159752 | tf_op jit(solution)/shard_map/ppermute | solution.py:520
  88.6 1.1 collective-permute-start.26
  89.7 3.6 %collective-permute-start.27 = (f32[104,128]{1,0:T(8,128)S(1)}, f32[104,128]{1,0:T(8,128)S(1)}, u32[]{:S(2)}, u32[]{:S(2)}) collective-permute-start(f32[104,128]{1,0:T(8,128)S(1)} %get-tuple-element.66), channel_id=1, source_target_pairs={{0,26},{2,24},{4,30},{6,28},{8,18},{10,16},{12,22},{14,20},{16,10}... | collective-permute-start | bytes 159752 | tf_op jit(solution)/shard_map/ppermute | solution.py:520
  93.3 4.7 %collective-permute-start.29 = (f32[104,128]{1,0:T(8,128)S(1)}, f32[104,128]{1,0:T(8,128)S(1)}, u32[]{:S(2)}, u32[]{:S(2)}) collective-permute-start(f32[104,128]{1,0:T(8,128)S(1)} %get-tuple-element.68), channel_id=1, source_target_pairs={{0,30},{2,28},{4,26},{6,24},{8,22},{10,20},{12,18},{14,16},{16,14}... | collective-permute-start | bytes 159752 | tf_op jit(solution)/shard_map/ppermute | solution.py:520
  98.1 2.0 %collective-permute-done.28.refs_14_ = f32[104,128]{1,0:T(8,128)S(1)} collective-permute-done((f32[104,128]{1,0:T(8,128)S(1)}, f32[104,128]{1,0:T(8,128)S(1)}, u32[]{:S(2)}, u32[]{:S(2)}) %collective-permute-start.28) | collective-permute-done | bytes 53280 | tf_op jit(solution)/shard_map/ppermute | solution.py:520
  100.1 1.0 collective-permute-done.29.refs_15_
  101.1 18.3 %analyze.1 = f32[6,32,512]{2,1,0:T(8,128)} custom-call(f32[104,128]{1,0:T(8,128)S(1)} %get-tuple-element.53.refs_0_, f32[104,128]{1,0:T(8,128)S(1)} %collective-permute-done.15.refs_1_, f32[104,128]{1,0:T(8,128)S(1)} %collective-permute-done.16.refs_2_, f32[104,128]{1,0:T(8,128)S(1)} %collective-permute-done.17.refs_3_, ...), custom_call_target="tpu_custom_call" | custom-call | flops 24000000000 | bytes 1048576 | tf_op jit(solution)/shard_map/analyze/pallas_call | solution.py:494
  (58 shorter events, 3.8 us)
Async XLA Ops:
  3.4 1.0 copy-start.1
  5.3 51.7 %copy-start = (f32[1,64,2048]{2,1,0:T(8,128)S(1)}, f32[1,64,2048]{2,1,0:T(8,128)}, u32[]{:S(2)}) copy-start(f32[1,64,2048]{2,1,0:T(8,128)} %param.7) | copy-start | bytes 1572868
  20.2 9.2 %collective-permute-start = (f32[96,128]{1,0:T(8,128)S(1)}, f32[96,128]{1,0:T(8,128)S(1)}, u32[]{:S(2)}, u32[]{:S(2)}) collective-permute-start(f32[96,128]{1,0:T(8,128)S(1)} %get-tuple-element.38), channel_id=1, source_target_pairs={{0,2},{2,0},{4,6},{6,4},{8,10},{10,8},{12,14},{14,12},{16,18},{18,... | collective-permute-start | bytes 147464 | tf_op jit(solution)/shard_map/ppermute | solution.py:520
  24.1 8.4 %collective-permute-start.1 = (f32[96,128]{1,0:T(8,128)S(1)}, f32[96,128]{1,0:T(8,128)S(1)}, u32[]{:S(2)}, u32[]{:S(2)}) collective-permute-start(f32[96,128]{1,0:T(8,128)S(1)} %get-tuple-element.39), channel_id=1, source_target_pairs={{0,4},{2,6},{4,0},{6,2},{8,12},{10,14},{12,8},{14,10},{16,20},{18,... | collective-permute-start | bytes 147464 | tf_op jit(solution)/shard_map/ppermute | solution.py:520
  26.5 6.0 %collective-permute-start.2 = (f32[96,128]{1,0:T(8,128)S(1)}, f32[96,128]{1,0:T(8,128)S(1)}, u32[]{:S(2)}, u32[]{:S(2)}) collective-permute-start(f32[96,128]{1,0:T(8,128)S(1)} %get-tuple-element.40), channel_id=1, source_target_pairs={{0,6},{2,4},{4,2},{6,0},{8,14},{10,12},{12,10},{14,8},{16,22},{18,... | collective-permute-start | bytes 147464 | tf_op jit(solution)/shard_map/ppermute | solution.py:520
  26.5 8.6 %collective-permute-start.3 = (f32[96,128]{1,0:T(8,128)S(1)}, f32[96,128]{1,0:T(8,128)S(1)}, u32[]{:S(2)}, u32[]{:S(2)}) collective-permute-start(f32[96,128]{1,0:T(8,128)S(1)} %get-tuple-element.41), channel_id=1, source_target_pairs={{0,8},{2,10},{4,12},{6,14},{8,0},{10,2},{12,4},{14,6},{16,24},{18,... | collective-permute-start | bytes 147464 | tf_op jit(solution)/shard_map/ppermute | solution.py:520
  28.1 8.3 %collective-permute-start.4 = (f32[96,128]{1,0:T(8,128)S(1)}, f32[96,128]{1,0:T(8,128)S(1)}, u32[]{:S(2)}, u32[]{:S(2)}) collective-permute-start(f32[96,128]{1,0:T(8,128)S(1)} %get-tuple-element.42), channel_id=1, source_target_pairs={{0,10},{2,8},{4,14},{6,12},{8,2},{10,0},{12,6},{14,4},{16,26},{18,... | collective-permute-start | bytes 147464 | tf_op jit(solution)/shard_map/ppermute | solution.py:520
  29.4 10.9 %collective-permute-start.5 = (f32[96,128]{1,0:T(8,128)S(1)}, f32[96,128]{1,0:T(8,128)S(1)}, u32[]{:S(2)}, u32[]{:S(2)}) collective-permute-start(f32[96,128]{1,0:T(8,128)S(1)} %get-tuple-element.43), channel_id=1, source_target_pairs={{0,12},{2,14},{4,8},{6,10},{8,4},{10,6},{12,0},{14,2},{16,28},{18,... | collective-permute-start | bytes 147464 | tf_op jit(solution)/shard_map/ppermute | solution.py:520
  32.5 8.0 %collective-permute-start.6 = (f32[96,128]{1,0:T(8,128)S(1)}, f32[96,128]{1,0:T(8,128)S(1)}, u32[]{:S(2)}, u32[]{:S(2)}) collective-permute-start(f32[96,128]{1,0:T(8,128)S(1)} %get-tuple-element.44), channel_id=1, source_target_pairs={{0,14},{2,12},{4,10},{6,8},{8,6},{10,4},{12,2},{14,0},{16,30},{18,... | collective-permute-start | bytes 147464 | tf_op jit(solution)/shard_map/ppermute | solution.py:520
  32.5 11.3 %collective-permute-start.7 = (f32[96,128]{1,0:T(8,128)S(1)}, f32[96,128]{1,0:T(8,128)S(1)}, u32[]{:S(2)}, u32[]{:S(2)}) collective-permute-start(f32[96,128]{1,0:T(8,128)S(1)} %get-tuple-element.45), channel_id=1, source_target_pairs={{0,16},{2,18},{4,20},{6,22},{8,24},{10,26},{12,28},{14,30},{16,0},... | collective-permute-start | bytes 147464 | tf_op jit(solution)/shard_map/ppermute | solution.py:520
  35.1 10.1 %collective-permute-start.8 = (f32[96,128]{1,0:T(8,128)S(1)}, f32[96,128]{1,0:T(8,128)S(1)}, u32[]{:S(2)}, u32[]{:S(2)}) collective-permute-start(f32[96,128]{1,0:T(8,128)S(1)} %get-tuple-element.46), channel_id=1, source_target_pairs={{0,18},{2,16},{4,22},{6,20},{8,26},{10,24},{12,30},{14,28},{16,2},... | collective-permute-start | bytes 147464 | tf_op jit(solution)/shard_map/ppermute | solution.py:520
  36.4 12.8 %collective-permute-start.9 = (f32[96,128]{1,0:T(8,128)S(1)}, f32[96,128]{1,0:T(8,128)S(1)}, u32[]{:S(2)}, u32[]{:S(2)}) collective-permute-start(f32[96,128]{1,0:T(8,128)S(1)} %get-tuple-element.47), channel_id=1, source_target_pairs={{0,20},{2,22},{4,16},{6,18},{8,28},{10,30},{12,24},{14,26},{16,4},... | collective-permute-start | bytes 147464 | tf_op jit(solution)/shard_map/ppermute | solution.py:520
  40.4 9.9 %collective-permute-start.10 = (f32[96,128]{1,0:T(8,128)S(1)}, f32[96,128]{1,0:T(8,128)S(1)}, u32[]{:S(2)}, u32[]{:S(2)}) collective-permute-start(f32[96,128]{1,0:T(8,128)S(1)} %get-tuple-element.48), channel_id=1, source_target_pairs={{0,22},{2,20},{4,18},{6,16},{8,30},{10,28},{12,26},{14,24},{16,6},... | collective-permute-start | bytes 147464 | tf_op jit(solution)/shard_map/ppermute | solution.py:520
  40.5 9.8 %collective-permute-start.11 = (f32[96,128]{1,0:T(8,128)S(1)}, f32[96,128]{1,0:T(8,128)S(1)}, u32[]{:S(2)}, u32[]{:S(2)}) collective-permute-start(f32[96,128]{1,0:T(8,128)S(1)} %get-tuple-element.49), channel_id=1, source_target_pairs={{0,24},{2,26},{4,28},{6,30},{8,16},{10,18},{12,20},{14,22},{16,8},... | collective-permute-start | bytes 147464 | tf_op jit(solution)/shard_map/ppermute | solution.py:520
  43.8 7.4 %collective-permute-start.12 = (f32[96,128]{1,0:T(8,128)S(1)}, f32[96,128]{1,0:T(8,128)S(1)}, u32[]{:S(2)}, u32[]{:S(2)}) collective-permute-start(f32[96,128]{1,0:T(8,128)S(1)} %get-tuple-element.50), channel_id=1, source_target_pairs={{0,26},{2,24},{4,30},{6,28},{8,18},{10,16},{12,22},{14,20},{16,10}... | collective-permute-start | bytes 147464 | tf_op jit(solution)/shard_map/ppermute | solution.py:520
  45.2 7.2 %collective-permute-start.13 = (f32[96,128]{1,0:T(8,128)S(1)}, f32[96,128]{1,0:T(8,128)S(1)}, u32[]{:S(2)}, u32[]{:S(2)}) collective-permute-start(f32[96,128]{1,0:T(8,128)S(1)} %get-tuple-element.51), channel_id=1, source_target_pairs={{0,28},{2,30},{4,24},{6,26},{8,20},{10,22},{12,16},{14,18},{16,12}... | collective-permute-start | bytes 147464 | tf_op jit(solution)/shard_map/ppermute | solution.py:520
  49.2 7.7 %collective-permute-start.14 = (f32[96,128]{1,0:T(8,128)S(1)}, f32[96,128]{1,0:T(8,128)S(1)}, u32[]{:S(2)}, u32[]{:S(2)}) collective-permute-start(f32[96,128]{1,0:T(8,128)S(1)} %get-tuple-element.52), channel_id=1, source_target_pairs={{0,30},{2,28},{4,26},{6,24},{8,22},{10,20},{12,18},{14,16},{16,14}... | collective-permute-start | bytes 147464 | tf_op jit(solution)/shard_map/ppermute | solution.py:520
  71.5 6.4 %collective-permute-start.15 = (f32[104,128]{1,0:T(8,128)S(1)}, f32[104,128]{1,0:T(8,128)S(1)}, u32[]{:S(2)}, u32[]{:S(2)}) collective-permute-start(f32[104,128]{1,0:T(8,128)S(1)} %get-tuple-element.54), channel_id=1, source_target_pairs={{0,2},{2,0},{4,6},{6,4},{8,10},{10,8},{12,14},{14,12},{16,18},{18,... | collective-permute-start | bytes 159752 | tf_op jit(solution)/shard_map/ppermute | solution.py:520
  73.0 5.3 %collective-permute-start.16 = (f32[104,128]{1,0:T(8,128)S(1)}, f32[104,128]{1,0:T(8,128)S(1)}, u32[]{:S(2)}, u32[]{:S(2)}) collective-permute-start(f32[104,128]{1,0:T(8,128)S(1)} %get-tuple-element.55), channel_id=1, source_target_pairs={{0,4},{2,6},{4,0},{6,2},{8,12},{10,14},{12,8},{14,10},{16,20},{18,... | collective-permute-start | bytes 159752 | tf_op jit(solution)/shard_map/ppermute | solution.py:520
  73.0 7.9 %collective-permute-start.17 = (f32[104,128]{1,0:T(8,128)S(1)}, f32[104,128]{1,0:T(8,128)S(1)}, u32[]{:S(2)}, u32[]{:S(2)}) collective-permute-start(f32[104,128]{1,0:T(8,128)S(1)} %get-tuple-element.56), channel_id=1, source_target_pairs={{0,6},{2,4},{4,2},{6,0},{8,14},{10,12},{12,10},{14,8},{16,22},{18,... | collective-permute-start | bytes 159752 | tf_op jit(solution)/shard_map/ppermute | solution.py:520
  75.1 5.9 %collective-permute-start.18 = (f32[104,128]{1,0:T(8,128)S(1)}, f32[104,128]{1,0:T(8,128)S(1)}, u32[]{:S(2)}, u32[]{:S(2)}) collective-permute-start(f32[104,128]{1,0:T(8,128)S(1)} %get-tuple-element.57), channel_id=1, source_target_pairs={{0,8},{2,10},{4,12},{6,14},{8,0},{10,2},{12,4},{14,6},{16,24},{18,... | collective-permute-start | bytes 159752 | tf_op jit(solution)/shard_map/ppermute | solution.py:520
  75.1 9.6 %collective-permute-start.19 = (f32[104,128]{1,0:T(8,128)S(1)}, f32[104,128]{1,0:T(8,128)S(1)}, u32[]{:S(2)}, u32[]{:S(2)}) collective-permute-start(f32[104,128]{1,0:T(8,128)S(1)} %get-tuple-element.58), channel_id=1, source_target_pairs={{0,10},{2,8},{4,14},{6,12},{8,2},{10,0},{12,6},{14,4},{16,26},{18,... | collective-permute-start | bytes 159752 | tf_op jit(solution)/shard_map/ppermute | solution.py:520
  78.0 6.8 %collective-permute-start.20 = (f32[104,128]{1,0:T(8,128)S(1)}, f32[104,128]{1,0:T(8,128)S(1)}, u32[]{:S(2)}, u32[]{:S(2)}) collective-permute-start(f32[104,128]{1,0:T(8,128)S(1)} %get-tuple-element.59), channel_id=1, source_target_pairs={{0,12},{2,14},{4,8},{6,10},{8,4},{10,6},{12,0},{14,2},{16,28},{18,... | collective-permute-start | bytes 159752 | tf_op jit(solution)/shard_map/ppermute | solution.py:520
  78.3 10.3 %collective-permute-start.21 = (f32[104,128]{1,0:T(8,128)S(1)}, f32[104,128]{1,0:T(8,128)S(1)}, u32[]{:S(2)}, u32[]{:S(2)}) collective-permute-start(f32[104,128]{1,0:T(8,128)S(1)} %get-tuple-element.60), channel_id=1, source_target_pairs={{0,14},{2,12},{4,10},{6,8},{8,6},{10,4},{12,2},{14,0},{16,30},{18,... | collective-permute-start | bytes 159752 | tf_op jit(solution)/shard_map/ppermute | solution.py:520
  81.0 8.7 %collective-permute-start.22 = (f32[104,128]{1,0:T(8,128)S(1)}, f32[104,128]{1,0:T(8,128)S(1)}, u32[]{:S(2)}, u32[]{:S(2)}) collective-permute-start(f32[104,128]{1,0:T(8,128)S(1)} %get-tuple-element.61), channel_id=1, source_target_pairs={{0,16},{2,18},{4,20},{6,22},{8,24},{10,26},{12,28},{14,30},{16,0},... | collective-permute-start | bytes 159752 | tf_op jit(solution)/shard_map/ppermute | solution.py:520
  81.0 12.3 %collective-permute-start.23 = (f32[104,128]{1,0:T(8,128)S(1)}, f32[104,128]{1,0:T(8,128)S(1)}, u32[]{:S(2)}, u32[]{:S(2)}) collective-permute-start(f32[104,128]{1,0:T(8,128)S(1)} %get-tuple-element.62), channel_id=1, source_target_pairs={{0,18},{2,16},{4,22},{6,20},{8,26},{10,24},{12,30},{14,28},{16,2},... | collective-permute-start | bytes 159752 | tf_op jit(solution)/shard_map/ppermute | solution.py:520
  84.7 8.6 %collective-permute-start.24 = (f32[104,128]{1,0:T(8,128)S(1)}, f32[104,128]{1,0:T(8,128)S(1)}, u32[]{:S(2)}, u32[]{:S(2)}) collective-permute-start(f32[104,128]{1,0:T(8,128)S(1)} %get-tuple-element.63), channel_id=1, source_target_pairs={{0,20},{2,22},{4,16},{6,18},{8,28},{10,30},{12,24},{14,26},{16,4},... | collective-permute-start | bytes 159752 | tf_op jit(solution)/shard_map/ppermute | solution.py:520
  84.7 13.3 %collective-permute-start.25 = (f32[104,128]{1,0:T(8,128)S(1)}, f32[104,128]{1,0:T(8,128)S(1)}, u32[]{:S(2)}, u32[]{:S(2)}) collective-permute-start(f32[104,128]{1,0:T(8,128)S(1)} %get-tuple-element.64), channel_id=1, source_target_pairs={{0,22},{2,20},{4,18},{6,16},{8,30},{10,28},{12,26},{14,24},{16,6},... | collective-permute-start | bytes 159752 | tf_op jit(solution)/shard_map/ppermute | solution.py:520
  88.6 9.5 %collective-permute-start.26 = (f32[104,128]{1,0:T(8,128)S(1)}, f32[104,128]{1,0:T(8,128)S(1)}, u32[]{:S(2)}, u32[]{:S(2)}) collective-permute-start(f32[104,128]{1,0:T(8,128)S(1)} %get-tuple-element.65), channel_id=1, source_target_pairs={{0,24},{2,26},{4,28},{6,30},{8,16},{10,18},{12,20},{14,22},{16,8},... | collective-permute-start | bytes 159752 | tf_op jit(solution)/shard_map/ppermute | solution.py:520
  89.7 8.4 %collective-permute-start.27 = (f32[104,128]{1,0:T(8,128)S(1)}, f32[104,128]{1,0:T(8,128)S(1)}, u32[]{:S(2)}, u32[]{:S(2)}) collective-permute-start(f32[104,128]{1,0:T(8,128)S(1)} %get-tuple-element.66), channel_id=1, source_target_pairs={{0,26},{2,24},{4,30},{6,28},{8,18},{10,16},{12,22},{14,20},{16,10}... | collective-permute-start | bytes 159752 | tf_op jit(solution)/shard_map/ppermute | solution.py:520
  93.3 6.8 %collective-permute-start.28 = (f32[104,128]{1,0:T(8,128)S(1)}, f32[104,128]{1,0:T(8,128)S(1)}, u32[]{:S(2)}, u32[]{:S(2)}) collective-permute-start(f32[104,128]{1,0:T(8,128)S(1)} %get-tuple-element.67), channel_id=1, source_target_pairs={{0,28},{2,30},{4,24},{6,26},{8,20},{10,22},{12,16},{14,18},{16,12}... | collective-permute-start | bytes 159752 | tf_op jit(solution)/shard_map/ppermute | solution.py:520
  93.3 7.8 %collective-permute-start.29 = (f32[104,128]{1,0:T(8,128)S(1)}, f32[104,128]{1,0:T(8,128)S(1)}, u32[]{:S(2)}, u32[]{:S(2)}) collective-permute-start(f32[104,128]{1,0:T(8,128)S(1)} %get-tuple-element.68), channel_id=1, source_target_pairs={{0,30},{2,28},{4,26},{6,24},{8,22},{10,20},{12,18},{14,16},{16,14}... | collective-permute-start | bytes 159752 | tf_op jit(solution)/shard_map/ppermute | solution.py:520
  (4 other events, 3.0 us)

commit v2 on v1

v2 whole, which is shorter than its diff:
```python
import functools
import math

import jax
import jax.numpy as jnp
import numpy as np
from jax import lax
from jax.experimental import pallas as pl
from jax.experimental.pallas import tpu as pltpu
from jax.sharding import PartitionSpec as P

DEG = 512
NLAT = 1024
NLON = 2048
FIELDS = 3
HALF = NLAT // 2
CHAN = 2 * FIELDS
BLK = 8
ROWS = CHAN * BLK
CHUNK = 64
LANES = 128
KTILE = 256
BF = jnp.bfloat16
F32 = jnp.float32


def split_two(value):
    high = value.astype(BF)
    low = (value - high.astype(F32)).astype(BF)
    return high, low


def dot(lhs, rhs, contract_rhs=0):
    return lax.dot_general(
        lhs, rhs, (((1,), (contract_rhs,)), ((), ())), preferred_element_type=F32
    )


def latitude_rows():
    theta = np.pi * (np.arange(HALF) + 0.5) / NLAT
    index = np.arange(DEG, dtype=np.float64)
    log_terms = np.zeros(DEG)
    log_terms[1:] = 0.5 * np.log2((2.0 * index[1:] + 1.0) / (2.0 * index[1:]))
    rows = np.zeros((8, DEG))
    rows[0], rows[1], rows[2] = np.cos(theta), np.log2(np.sin(theta)), log_terms
    return rows.astype(np.float32)


def spread_matrix():
    spread = np.zeros((LANES, 2, 2, CHUNK // 2, BLK), np.float32)
    for half in range(2):
        for parity in range(2):
            for step in range(CHUNK // 2):
                spread[half * CHUNK + 2 * step + parity, half, parity, step, :] = 1.0
    return spread.reshape(LANES, 2 * 2 * (CHUNK // 2) * BLK).astype(BF)


def block_orders(slots_ref, first):
    sublane = lax.broadcasted_iota(jnp.int32, (BLK, LANES), 0)
    orders = jnp.zeros((BLK, LANES), jnp.int32)
    lowest = jnp.int32(DEG)
    for i in range(BLK):
        order = slots_ref[first + i]
        orders = jnp.where(sublane == i, order, orders)
        lowest = jnp.minimum(lowest, order)
    return orders[:, :1], lowest


def recursion_tables(order, rows_ref, alpha_ref, beta_ref):
    degree = lax.broadcasted_iota(jnp.int32, (BLK, DEG), 1).astype(F32)
    order_sq = order * order
    denominator = degree * degree - order_sq
    safe = jnp.where(denominator > 0, denominator, 1.0)
    alpha = jnp.sqrt((4.0 * degree * degree - 1.0) / safe)
    back = jnp.maximum((degree - 1.0) * (degree - 1.0) - order_sq, 0.0)
    beta = jnp.sqrt(back * (2.0 * degree + 1.0) / (safe * jnp.maximum(2.0 * degree - 3.0, 1.0)))
    alpha_ref[...] = jnp.where(degree > order, alpha, 0.0)
    beta_ref[...] = jnp.where(degree > order, beta, -1.0)
    terms = jnp.where(degree <= order, rows_ref[2:3, :], 0.0)
    norm = jnp.where(order > 0, 0.5 + jnp.sum(terms, axis=1, keepdims=True), 0.0)
    return norm + order * rows_ref[1:2, :]


def run_chunk(step, carry, cosine, alpha_ref, beta_ref, emit, beside):
    current, previous, log_scale = carry
    tile = pl.ds(pl.multiple_of(step // 2 * LANES, LANES), LANES)
    shift = (step % 2) * CHUNK
    alpha = pltpu.roll(alpha_ref[:, tile], shift, 1)
    beta = pltpu.roll(beta_ref[:, tile], shift, 1)
    scale = None
    for i in range(CHUNK):
        if i % 16 == 0:
            large = jnp.abs(current) > 2.0**60
            factor = jnp.where(large, 2.0**-60, 1.0)
            current = current * factor
            previous = previous * factor
            log_scale = jnp.where(large, log_scale + 60.0, log_scale)
            scale = jnp.exp2(jnp.maximum(log_scale, -200.0))
        newest = (alpha[:, i : i + 1] * cosine) * current - beta[:, i : i + 1] * previous
        current, previous = newest, current
        emit(i, newest * scale)
        if beside and i % (CHUNK // len(beside)) == 1:
            beside[i // (CHUNK // len(beside))]()
    return current, previous, log_scale


def start_state(log_start):
    ones = jnp.ones((BLK, HALF), F32)
    return ones, ones, log_start


def fold_matrix(latitude_ref, fold_ref):
    latitude = latitude_ref[...]
    north = jnp.where(latitude < HALF, latitude, NLAT - 1 - latitude)
    sublane = lax.broadcasted_iota(jnp.int32, (HALF, NLAT), 0)
    fold_ref[...] = jnp.where(sublane == north, 1.0, 0.0).astype(BF)


def synth_kernel(
    dims, slots_ref, place_ref, spec_ref, rows_ref, spread_ref, latitude_ref, out_ref,
    alpha_ref, beta_ref, lhs_ref, high_a, low_a, high_b, low_b, acc_ref, fold_ref, coeff_ref,
):
    bands, row_count, modes, blocks, tiles = dims
    fold_matrix(latitude_ref, fold_ref)
    base = lax.axis_index("band") * modes
    south = latitude_ref[...] >= HALF
    spread_width = 4 * (CHUNK // 2) * BLK
    lane = lax.broadcasted_iota(jnp.int32, (2 * ROWS, spread_width), 1)
    sub = lax.broadcasted_iota(jnp.int32, (2 * ROWS, spread_width), 0)
    diagonal = (lane % BLK) == (sub % BLK)
    width = (CHUNK // 2) * BLK

    def one_block(block, unused):
        orders, lowest = block_orders(slots_ref, base + block * BLK)
        order = orders.astype(F32)
        log_start = recursion_tables(order, rows_ref, alpha_ref, beta_ref)
        for i in range(BLK):
            source = pl.ds(place_ref[base + block * BLK + i], 1)
            coeff_ref[:, i : i + 1, :] = spec_ref[:, source, :]
        degree = lax.broadcasted_iota(jnp.int32, (BLK, DEG), 1)
        coeffs = jnp.where((degree >= orders)[None], coeff_ref[...], 0.0)
        coeff_high, coeff_low = split_two(coeffs.reshape(ROWS, DEG))
        stacked = jnp.concatenate([coeff_high, coeff_low], 0)
        for t in range(DEG // LANES):
            wide = dot(stacked[:, t * LANES : (t + 1) * LANES], spread_ref[...])
            wide = jnp.where(diagonal, wide, 0.0).astype(BF)
            for half in range(2):
                lhs_ref[2 * t + half] = wide[:, half * 2 * width : (half + 1) * 2 * width]
        acc_ref[...] = jnp.zeros_like(acc_ref)
        cosine = jnp.broadcast_to(rows_ref[0:1, :], (BLK, HALF))

        def recur(step, carry, high_ref, low_ref, beside):
            held = {}

            def emit(i, value):
                if i % 4 < 2:
                    held[i] = value
                else:
                    pair = jnp.concatenate([held.pop(i - 2), value], 0)
                    high, low = split_two(pair)
                    at = (i // 4) * 2 * BLK
                    high_ref[i % 2, at : at + 2 * BLK, :] = high
                    low_ref[i % 2, at : at + 2 * BLK, :] = low

            return run_chunk(step, carry, cosine, alpha_ref, beta_ref, emit, beside)

        def add_products(step, high_ref, low_ref):
            def part(parity, columns):
                lhs = lhs_ref[step, :, parity * width : (parity + 1) * width]
                first = dot(lhs, high_ref[parity, :, columns])
                second = dot(lhs[:ROWS], low_ref[parity, :, columns])
                acc_ref[parity, :, columns] += first[:ROWS] + first[ROWS:] + second

            return [
                functools.partial(part, parity, slice(at, at + KTILE))
                for parity in range(2)
                for at in range(0, HALF, KTILE)
            ]

        def two_chunks(pair, carry):
            step = 2 * pair
            beside = add_products(jnp.maximum(step - 1, 0), high_b, low_b)
            carry = recur(step, carry, high_a, low_a, beside)
            beside = add_products(step, high_a, low_a)
            return recur(step + 1, carry, high_b, low_b, beside)

        high_b[...] = jnp.zeros_like(high_b)
        low_b[...] = jnp.zeros_like(low_b)
        chunks = DEG // CHUNK
        lax.fori_loop(lowest // (2 * CHUNK), chunks // 2, two_chunks, start_state(log_start))
        for part in add_products(chunks - 1, high_b, low_b):
            part()
        both = acc_ref[...].reshape(2 * ROWS, HALF)
        high, low = split_two(both)
        moved = dot(jnp.concatenate([high, low], 0), fold_ref[...])
        moved = moved[: 2 * ROWS] + moved[2 * ROWS :]
        sign = jnp.tile(1.0 - 2.0 * (orders % 2).astype(F32), (CHAN, 1))
        even, odd = moved[:ROWS], moved[ROWS:]
        values = jnp.where(south, sign * (even - odd), even + odd)
        for d in range(bands):
            parts = []
            for kind in range(2):
                for field in range(FIELDS):
                    c = field * 2 + kind
                    parts.append(
                        values[c * BLK : (c + 1) * BLK, d * row_count : (d + 1) * row_count]
                    )
            if CHAN * row_count < tiles * LANES:
                parts.append(jnp.zeros((BLK, tiles * LANES - CHAN * row_count), F32))
            joined = jnp.concatenate(parts, 1)
            for t in range(tiles):
                at = pl.ds(pl.multiple_of(t * blocks * BLK + block * BLK, BLK), BLK)
                out_ref[d, at, :] = joined[:, t * LANES : (t + 1) * LANES]
        return unused

    lax.fori_loop(0, blocks, one_block, 0)


def table_kernel(
    dims, slots_ref, rows_ref, out_ref, alpha_ref, beta_ref, first_ref, second_ref, sems,
):
    modes, blocks = dims
    base = lax.axis_index("band") * modes
    cosine = jnp.broadcast_to(rows_ref[0:1, :], (BLK, HALF))
    buffers = (first_ref, second_ref)

    def copy_out(which, block, step):
        return pltpu.make_async_copy(buffers[which], out_ref.at[block, step], sems.at[which])

    def one_block(block, unused):
        orders, lowest = block_orders(slots_ref, base + block * BLK)
        log_start = recursion_tables(orders.astype(F32), rows_ref, alpha_ref, beta_ref)
        start = lowest // (2 * CHUNK)

        def recur(which, step, carry, pending):
            buffer = buffers[which]

            @pl.when(pending)
            def _():
                copy_out(which, block, step).wait()

            held = {}

            def emit(i, value):
                if i % 2 == 0:
                    held[i] = value
                else:
                    pair = jnp.concatenate([held.pop(i - 1), value], 0)
                    high, low = split_two(pair)
                    at = (i // 2) * 2 * BLK
                    buffer[at : at + 2 * BLK, :] = high
                    buffer[CHUNK * BLK + at : CHUNK * BLK + at + 2 * BLK, :] = low

            carry = run_chunk(step, carry, cosine, alpha_ref, beta_ref, emit, ())
            copy_out(which, block, step).start()
            return carry

        def two_chunks(pair, carry):
            pending = (block > 0) | (pair > start)
            carry = recur(0, 2 * pair, carry, pending)
            return recur(1, 2 * pair + 1, carry, pending)

        lax.fori_loop(start, DEG // CHUNK // 2, two_chunks, start_state(log_start))
        return unused

    lax.fori_loop(0, blocks, one_block, 0)
    copy_out(0, 0, 0).wait()
    copy_out(1, 0, 0).wait()


def analyze_kernel(
    dims, total_row, slots_ref, place_ref, data_ref, latitude_ref, table_ref, out_ref,
    chunk_ref, weight_ref, result_ref, fold_ref, coeff_ref, sems,
):
    bands, row_count, modes, blocks, tiles = dims
    base = lax.axis_index("band") * modes
    chunks = DEG // CHUNK

    def copy_in(block, step):
        return pltpu.make_async_copy(
            table_ref.at[block, step], chunk_ref.at[block, step], sems.at[block, step]
        )

    def start_block(block, unused):
        orders, lowest = block_orders(slots_ref, base + block * BLK)

        def start_chunk(step, inner):
            copy_in(block, step).start()
            return inner

        return lax.fori_loop(lowest // (2 * CHUNK) * 2, chunks, start_chunk, unused)

    lax.fori_loop(0, blocks, start_block, 0)
    fold_matrix(latitude_ref, fold_ref)
    south = latitude_ref[...] >= HALF
    total = data_ref[0, total_row : total_row + 8]
    for d in range(1, bands):
        total = total + data_ref[d, total_row : total_row + 8]
    inverse = (1.0 / total)[:, :1]
    lane = lax.broadcasted_iota(jnp.int32, (CHUNK * BLK, LANES), 1)
    sub = lax.broadcasted_iota(jnp.int32, (CHUNK * BLK, LANES), 0)
    keep = (lane % BLK == sub % BLK) & (lane // ROWS == sub // BLK % 2)

    def one_block(block, unused):
        orders, lowest = block_orders(slots_ref, base + block * BLK)
        sign = 1.0 - 2.0 * (orders % 2).astype(F32)
        evens, odds = [], []
        for c in range(CHAN):
            offset = ((c % 2) * FIELDS + c // 2) * row_count
            t, at = offset // LANES, offset % LANES
            rows = pl.ds(pl.multiple_of(t * blocks * BLK + block * BLK, BLK), BLK)
            values = jnp.concatenate(
                [data_ref[d, rows, :][:, at : at + row_count] for d in range(bands)], 1
            )
            flipped = sign * values
            evens.append(jnp.where(south, flipped, values))
            odds.append(jnp.where(south, -flipped, values))
        high, low = split_two(jnp.concatenate(evens + odds, 0))
        folded = dot(jnp.concatenate([high, low], 0), fold_ref[...], 1)
        folded = folded[: 2 * ROWS] + folded[2 * ROWS :]
        padded = jnp.concatenate([folded, jnp.zeros((LANES - 2 * ROWS, HALF), F32)], 0)
        high, low = split_two(padded.T)
        weight_ref[:, :LANES] = high
        weight_ref[:, LANES:] = low
        result_ref[...] = jnp.zeros_like(result_ref)

        def one_chunk(step, inner):
            copy_in(block, step).wait()
            first = dot(chunk_ref[block, step, : CHUNK * BLK], weight_ref[...])
            second = dot(chunk_ref[block, step, CHUNK * BLK :], weight_ref[:, :LANES])
            full = first[:, :LANES] + first[:, LANES:] + second
            picked = jnp.where(keep, full, 0.0).reshape(CHUNK, BLK, LANES)
            to = pl.ds(pl.multiple_of(step * CHUNK, CHUNK), CHUNK)
            result_ref[to, :] = jnp.sum(picked, axis=1)
            return inner

        lax.fori_loop(lowest // (2 * CHUNK) * 2, chunks, one_chunk, 0)
        turned = result_ref[...].T
        turned = turned[:ROWS] + turned[ROWS : 2 * ROWS]
        degree = lax.broadcasted_iota(jnp.int32, (BLK, DEG), 1)
        for c in range(CHAN):
            part = jnp.where(degree >= orders, turned[c * BLK : (c + 1) * BLK], 0.0)
            if c // 2 == FIELDS - 1:
                part = part * inverse
            coeff_ref[c] = part
        for i in range(BLK):
            target = pl.ds(place_ref[base + block * BLK + i], 1)
            out_ref[:, target, :] = coeff_ref[:, i : i + 1, :]
        return unused

    lax.fori_loop(0, blocks, one_block, 0)


def base_trig(order, first):
    lane = lax.broadcasted_iota(jnp.int32, order.shape, 1) + first
    phase = (order * lane) & (NLON - 1)
    quarter = (phase + NLON // 8) >> 9
    rest = (phase - quarter * (NLON // 4)).astype(F32) * (2.0 * math.pi / NLON)
    square = rest * rest
    sine = 1.0 / 362880.0
    for coef in (-1.0 / 5040.0, 1.0 / 120.0, -1.0 / 6.0, 1.0):
        sine = sine * square + coef
    sine = sine * rest
    cosine = 1.0 / 40320.0
    for coef in (-1.0 / 720.0, 1.0 / 24.0, -0.5, 1.0):
        cosine = cosine * square + coef
    swap = (quarter & 1) == 1
    cos_out = jnp.where(swap, sine, cosine)
    sin_out = jnp.where(swap, cosine, sine)
    cos_out = jnp.where(((quarter + 1) & 2) == 2, -cos_out, cos_out)
    sin_out = jnp.where((quarter & 2) == 2, -sin_out, sin_out)
    return cos_out, sin_out


def trig_kernel(high_ref, low_ref, cos_ref, sin_ref):
    half = cos_ref.shape[0]
    root = math.sqrt(0.5)
    for parity in range(2):

        def strip(step, unused):
            at = pl.multiple_of(step * 64, 64)
            shape = (64, LANES)
            order = 2 * (lax.broadcasted_iota(jnp.int32, shape, 0) + at) + parity
            eighth = order & 7
            odd = (eighth & 1) == 1
            turn_cos = jnp.where(odd, root, jnp.where((eighth & 2) == 0, 1.0, 0.0))
            turn_sin = jnp.where(odd, root, jnp.where((eighth & 2) == 2, 1.0, 0.0))
            turn_cos = jnp.where((eighth >= 3) & (eighth <= 5), -turn_cos, turn_cos)
            turn_sin = jnp.where(eighth > 4, -turn_sin, turn_sin)
            for t in range(KTILE // LANES):
                cosine, sine = base_trig(order, t * LANES)
                for k in range(t * LANES, NLON // 2, KTILE):
                    columns = slice(k, k + LANES)
                    high, low = split_two(cosine)
                    high_ref[parity, pl.ds(at, 64), columns] = high
                    low_ref[parity, pl.ds(at, 64), columns] = low
                    high, low = split_two(sine)
                    high_ref[parity, pl.ds(half + at, 64), columns] = high
                    low_ref[parity, pl.ds(half + at, 64), columns] = low
                    cosine, sine = (
                        cosine * turn_cos - sine * turn_sin,
                        sine * turn_cos + cosine * turn_sin,
                    )
            return unused

        lax.fori_loop(0, half // 64, strip, 0)


def grid_kernel(
    dims, data_ref, orders_ref, rate_ref, sine_ref, trig_high, trig_low, out_ref,
    move_ref, lhs_ref, weight_ref, acc_ref,
):
    bands, row_count, modes, tiles, slots = dims
    half = slots // 2
    group = FIELDS * row_count
    padded = weight_ref.shape[1] // 2

    order = orders_ref[...]
    natural = (order & 1) * half + (order >> 1)
    for t in range(slots // LANES):
        lane = lax.broadcasted_iota(jnp.int32, (slots, LANES), 1) + t * LANES
        one_hot = jnp.where(natural == lane, 1.0, 0.0).astype(BF)
        move_ref[:, t * LANES : (t + 1) * LANES] = one_hot
    columns = []
    for t in range(tiles):
        part = data_ref[:, t * modes : (t + 1) * modes, :]
        columns.append(part.reshape(slots, LANES).T)
    turned = jnp.concatenate(columns, 0)
    for kind in range(2):
        high, low = split_two(turned[kind * group : (kind + 1) * group])
        moved = dot(jnp.concatenate([high, low], 0), move_ref[...]).astype(BF)
        for parity in range(2):
            part = moved[:, parity * half : (parity + 1) * half]
            lhs_ref[parity, :, kind * half : (kind + 1) * half] = part
    weight_ref[...] = jnp.zeros_like(weight_ref)
    flux_scale = math.pi / (2.0 * NLAT * NLON * DEG)
    weight = jnp.tile(sine_ref[...], (1, KTILE // LANES))
    total = jnp.zeros((8, KTILE), F32)

    for k in range(0, NLON // 2, KTILE):
        tile = slice(k, k + KTILE)
        sums = []
        for parity in range(2):
            first = dot(lhs_ref[parity], trig_high[parity, :, tile])
            second = dot(lhs_ref[parity, :group, :], trig_low[parity, :, tile])
            sums.append(first[:group] + first[group:] + second)
        values = []
        for fields, at in ((sums[0] + sums[1], k), (sums[0] - sums[1], k + NLON // 2)):
            weighted_rate = rate_ref[:, at : at + KTILE] * weight
            total = total + jnp.sum(weighted_rate.reshape(row_count // 8, 8, KTILE), axis=0)
            scaled = fields[:row_count] * (weight * flux_scale)
            values.append(
                jnp.concatenate(
                    [
                        fields[row_count : 2 * row_count] * scaled,
                        fields[2 * row_count :] * scaled,
                        weighted_rate * fields[:row_count],
                    ],
                    0,
                )
            )
        for parity in range(2):
            both = values[0] + values[1] if parity == 0 else values[0] - values[1]
            high, low = split_two(both)
            weight_ref[parity, :group, :] = high
            weight_ref[parity, padded : padded + group, :] = low
            first = dot(trig_high[parity, :, tile], weight_ref[parity], 1)
            second = dot(trig_low[parity, :, tile], weight_ref[parity, :padded, :], 1)
            part = first[:, :padded] + first[:, padded:] + second
            if k == 0:
                acc_ref[parity] = part
            else:
                acc_ref[parity] += part

    joined = []
    for kind in range(2):
        rows = slice(kind * half, (kind + 1) * half)
        joined.append(jnp.concatenate([acc_ref[0, rows, :group], acc_ref[1, rows, :group]], 0))
    if 2 * group < tiles * LANES:
        joined.append(jnp.zeros((slots, tiles * LANES - 2 * group), F32))
    high, low = split_two(jnp.concatenate(joined, 1))
    moved = dot(move_ref[...], jnp.concatenate([high, low], 1))
    moved = moved[:, : tiles * LANES] + moved[:, tiles * LANES :]
    for t in range(tiles):
        part = moved[:, t * LANES : (t + 1) * LANES]
        out_ref[:, t * modes : (t + 1) * modes, :] = part.reshape(bands, modes, LANES)
    out_ref[:, tiles * modes :, :] = jnp.broadcast_to(jnp.sum(total), (bands, 8, LANES))


VMEM = pl.BlockSpec(memory_space=pltpu.VMEM)
SMEM = pl.BlockSpec(memory_space=pltpu.SMEM)
ANY = pl.BlockSpec(memory_space=pl.ANY)


def work(microseconds):
    return pl.CostEstimate(
        flops=microseconds * 10**9, bytes_accessed=2**20, transcendentals=0
    )


def per_device(spectrum, capture_rate, row_latitude, slot_wavenumber):
    bands = lax.axis_size("band")
    modes = spectrum.shape[3]
    row_count = capture_rate.shape[1]
    slots = slot_wavenumber.shape[0]
    blocks = modes // BLK
    chunks = DEG // CHUNK
    tiles = -(-CHAN * row_count // LANES)
    band_index = lax.axis_index("band")
    table = slot_wavenumber.reshape(bands, modes)
    rank = jnp.sum((table[:, None, :] < table[:, :, None]).astype(jnp.int32), 2)
    match = rank[:, None, :] == jnp.arange(modes, dtype=jnp.int32)[None, :, None]
    ordered = jnp.sum(jnp.where(match, table[:, None, :], 0), 2).reshape(slots)
    place_row = jnp.arange(modes, dtype=jnp.int32)[None, None, :]
    places = jnp.sum(jnp.where(match, place_row, 0), 2).reshape(slots)
    rows = jnp.asarray(latitude_rows())
    spread = jnp.asarray(spread_matrix())
    latitude = row_latitude.reshape(1, NLAT)
    coeffs = spectrum.reshape(CHAN, modes, DEG)
    params = pltpu.CompilerParams(vmem_limit_bytes=48 * 2**20)
    chunk_rows = tiles * modes
    dims = (bands, row_count, modes, blocks, tiles)
    recursion_scratch = [pltpu.VMEM((BLK, DEG), F32)] * 2

    def exchange(value):
        return lax.all_to_all(value, "band", split_axis=0, concat_axis=0, tiled=True)

    sent = pl.pallas_call(
        lambda *refs: synth_kernel(dims, *refs),
        out_shape=jax.ShapeDtypeStruct((bands, chunk_rows, LANES), F32),
        in_specs=[SMEM, SMEM, VMEM, VMEM, VMEM, VMEM],
        out_specs=VMEM,
        scratch_shapes=recursion_scratch
        + [pltpu.VMEM((chunks, 2 * ROWS, CHUNK * BLK), BF)]
        + [pltpu.VMEM((2, CHUNK // 2 * BLK, HALF), BF)] * 4
        + [
            pltpu.VMEM((2, ROWS, HALF), F32),
            pltpu.VMEM((HALF, NLAT), BF),
            pltpu.VMEM((CHAN, BLK, DEG), F32),
        ],
        compiler_params=params,
        cost_estimate=work(15),
        name="synth",
    )(ordered, places, coeffs, rows, spread, latitude)
    received = exchange(sent)

    trig_shape = jax.ShapeDtypeStruct((2, slots, NLON // 2), BF)
    trig_high, trig_low = pl.pallas_call(
        trig_kernel,
        out_shape=[trig_shape, trig_shape],
        out_specs=[VMEM, VMEM],
        scratch_shapes=[pltpu.VMEM((slots // 2, LANES), F32)] * 2,
        compiler_params=params,
        cost_estimate=work(4),
        name="trig",
    )()

    my_latitudes = lax.dynamic_slice_in_dim(row_latitude, band_index * row_count, row_count)
    row_sine = jnp.sin(jnp.pi * (my_latitudes.astype(F32) + 0.5) / NLAT)
    row_sine = jnp.broadcast_to(row_sine[:, None], (row_count, LANES))
    orders = jnp.broadcast_to(ordered.reshape(slots, 1), (slots, LANES))
    group = FIELDS * row_count
    padded = -(-group // LANES) * LANES
    grid_dims = (bands, row_count, modes, tiles, slots)
    fluxes = pl.pallas_call(
        lambda *refs: grid_kernel(grid_dims, *refs),
        out_shape=jax.ShapeDtypeStruct((bands, chunk_rows + 8, LANES), F32),
        in_specs=[VMEM] * 6,
        out_specs=VMEM,
        scratch_shapes=[
            pltpu.VMEM((slots, slots), BF),
            pltpu.VMEM((2, 2 * group, slots), BF),
            pltpu.VMEM((2, 2 * padded, KTILE), BF),
            pltpu.VMEM((2, slots, padded), F32),
        ],
        compiler_params=params,
        cost_estimate=work(8),
        name="grid",
    )(received, orders, capture_rate.reshape(row_count, NLON), row_sine, trig_high, trig_low)
    returned = exchange(fluxes)

    chunk_shape = (blocks, chunks, 2 * CHUNK * BLK, HALF)
    legendre = pl.pallas_call(
        lambda *refs: table_kernel((modes, blocks), *refs),
        out_shape=jax.ShapeDtypeStruct(chunk_shape, BF),
        in_specs=[SMEM, VMEM],
        out_specs=ANY,
        scratch_shapes=recursion_scratch
        + [pltpu.VMEM((2 * CHUNK * BLK, HALF), BF)] * 2
        + [pltpu.SemaphoreType.DMA((2,))],
        compiler_params=params,
        cost_estimate=work(12),
        name="table",
    )(ordered, rows)
    result = pl.pallas_call(
        lambda *refs: analyze_kernel(dims, chunk_rows, *refs),
        out_shape=jax.ShapeDtypeStruct((CHAN, modes, DEG), F32),
        in_specs=[SMEM, SMEM, VMEM, VMEM, ANY],
        out_specs=VMEM,
        scratch_shapes=[
            pltpu.VMEM(chunk_shape, BF),
            pltpu.VMEM((HALF, 2 * LANES), BF),
            pltpu.VMEM((DEG, LANES), F32),
            pltpu.VMEM((HALF, NLAT), BF),
            pltpu.VMEM((CHAN, BLK, DEG), F32),
            pltpu.SemaphoreType.DMA((blocks, chunks)),
        ],
        compiler_params=params,
        cost_estimate=work(9),
        name="analyze",
    )(ordered, places, returned, latitude, legendre)
    return result.reshape(1, FIELDS, 2, modes, DEG)


def solution(mesh):
    return jax.shard_map(
        per_device,
        mesh=mesh,
        in_specs=(P("shell", None, None, "band", None), P("shell", "band", None), P(), P()),
        out_specs=P("shell", None, None, "band", None),
        check_vma=False,
    )
```

time: 121 us -> 98.7 us (0.82); the launches traced: 119 us -> 98.4 us
  starting transfers between devices: 55.8 us -> 10.6 us
  Pallas kernels: 47.7 us -> 64.7 us
  waiting for transfers between devices: 9.95 us -> 16 us
  local copies, waits for them, and re-layouts: 4.33 us -> 5.81 us
    ppermute x30 -> x0, starting transfers between devices: 55.8 us -> none  [exchange(): received.append(lax.ppermute(chunks[k], 'band', pairs))]
    pallas_call x3 -> x5, Pallas kernels: 47.7 us -> 64.7 us  [the longest x1 20.1 us: per_device(): pl.pallas_call(lambda *refs: table_kernel((modes, blocks), *refs), out_sh...]
    all_to_all x0 -> x2, waiting for transfers between devices: none -> 16 us  [exchange(): lax.all_to_all(value, 'band', split_axis=0, concat_axis=0, tiled=True)]
    all_to_all x0 -> x2, starting transfers between devices: none -> 10.6 us  [exchange(): lax.all_to_all(value, 'band', split_axis=0, concat_axis=0, tiled=True)]
    ppermute x30 -> x0, waiting for transfers between devices: 9.95 us -> none  [exchange(): received.append(lax.ppermute(chunks[k], 'band', pairs))]
    unnamed x12 -> x16, local copies, waits for them, and re-layouts: 3.68 us -> 4.7 us
  transfers between devices with their start and end apart: 30 -> 2, of which waited for: 6 -> 1; matrix products, arithmetic and copies ran while one was open for 0% -> 0% of each run, Pallas kernels for 0% -> 23%
where the time goes in v2:
time: 98.7 us; the launch traced here: 98.4 us
  Pallas kernels  64.7 us (66%)
  waiting for transfers between devices  16 us (16%)
  starting transfers between devices  10.6 us (11%)
  local copies, waits for them, and re-layouts  5.81 us (6%)
  other arithmetic  1.19 us (1%)
    pallas_call x1, Pallas kernels, per_device(): pl.pallas_call(lambda *refs: table_kernel((modes, blocks), *refs), out_sh...  20.1 us
    pallas_call x1, Pallas kernels, per_device(): pl.pallas_call(lambda *refs: synth_kernel(dims, *refs), out_shape=jax.Sha...  17.5 us
    pallas_call x1, Pallas kernels, per_device(): pl.pallas_call(lambda *refs: analyze_kernel(dims, chunk_rows, *refs), out...  17.1 us
    all_to_all x2, waiting for transfers between devices, exchange(): lax.all_to_all(value, 'band', split_axis=0, concat_axis=0, tiled=True)  16 us
    all_to_all x2, starting transfers between devices, exchange(): lax.all_to_all(value, 'band', split_axis=0, concat_axis=0, tiled=True)  10.6 us
    pallas_call x1, Pallas kernels, per_device(): pl.pallas_call(lambda *refs: grid_kernel(grid_dims, *refs), out_shape=jax...  7.66 us
    unnamed x16, local copies, waits for them, and re-layouts  4.7 us
    pallas_call x1, Pallas kernels, per_device(): pl.pallas_call(trig_kernel, out_shape=[trig_shape, trig_shape], out_specs...  2.28 us
  transfers between devices with their start and end apart: 2, of which 1 were waited for; matrix products, arithmetic and copies ran while one was open for 0% of the time, Pallas kernels for 23%

profile of v2, /device:TPU:0, one launch (start us, length us, event | category | flops | bytes accessed | tf_op | source)
XLA Modules:
  0.0 98.4 jit_solution(1510482458404935583)
XLA Ops:
  0.0 0.8 lt.18
  0.8 0.5 convert_reduce_fusion
  1.2 0.6 select_reduce_fusion
  1.8 0.1 reshape.24.refs_1_
  1.9 0.1 reshape.23.refs_0_
  2.0 0.0 copy-start
  2.0 0.7 copy-done
  2.7 0.0 copy-start.3
  2.7 1.0 %copy-done.3 = f32[1,3,2,32,512]{4,3,2,1,0:T(8,128)S(1)} copy-done((f32[1,3,2,32,512]{4,3,2,1,0:T(8,128)S(1)}, f32[1,3,2,32,512]{4,3,2,1,0:T(8,128)}, u32[]{:S(2)}) %copy-start.3) | copy-done | bytes 393240
  3.7 0.0 copy-start.4
  3.7 0.9 copy-done.4
  4.6 0.0 copy-start.5
  4.6 0.7 copy-done.5
  5.4 17.5 %synth.1 = f32[16,96,128]{2,1,0:T(8,128)} custom-call(s32[512]{0:T(512)S(1)} %reshape.23.refs_0_, s32[512]{0:T(512)S(1)} %reshape.24.refs_1_, f32[6,32,512]{2,1,0:T(8,128)S(1)} %bitcast.7, f32[8,512]{1,0:T(8,128)S(1)} %copy-done.5, bf16[128,1024]{1,0:T(8,128)(2,1)S(1)} %copy-done.4, s32[1,1024]{1,0:T(1,128)S(1)} %bitcast.4), custom_call_target="tpu_custom_call" | custom-call | flops 15000000512 | bytes 1048576 | tf_op jit(solution)/shard_map/synth/pallas_call | solution.py:528
  22.9 5.7 %all-to-all-start = ((f32[16,96,128]{2,1,0:T(8,128)}), f32[16,96,128]{2,1,0:T(8,128)S(1)}, u32[]{:S(2)}, u32[]{:S(2)}) async-start(f32[16,96,128]{2,1,0:T(8,128)} %synth.1), calls=%async_computation | async-start | bytes 1572864 | tf_op jit(solution)/shard_map/all_to_all | solution.py:526
  28.6 0.0 copy-done.1
  28.6 0.1 multiply_sine_fusion
  28.7 0.0 copy-start.2
  28.7 2.3 %trig.1 = (bf16[2,512,1024]{2,1,0:T(8,128)(2,1)S(1)}, bf16[2,512,1024]{2,1,0:T(8,128)(2,1)S(1)}) custom-call(), custom_call_target="tpu_custom_call" | custom-call | flops 4000000000 | bytes 1048576 | tf_op jit(solution)/shard_map/trig/pallas_call | solution.py:548
  31.0 0.0 copy-start.7
  31.0 1.3 %copy-done.7 = bf16[2,512,1024]{2,1,0:T(8,128)(2,1)} copy-done((bf16[2,512,1024]{2,1,0:T(8,128)(2,1)}, bf16[2,512,1024]{2,1,0:T(8,128)(2,1)S(1)}, u32[]{:S(2)}) %copy-start.7) | copy-done | bytes 2097176
  32.4 16.0 %all-to-all-done.refs_0_ = f32[16,96,128]{2,1,0:T(8,128)S(1)} async-done(((f32[16,96,128]{2,1,0:T(8,128)}), f32[16,96,128]{2,1,0:T(8,128)S(1)}, u32[]{:S(2)}, u32[]{:S(2)}) %all-to-all-start) | async-done | bytes 786464 | tf_op jit(solution)/shard_map/all_to_all | solution.py:526
  48.3 0.1 broadcast_in_dim.37.refs_3_
  48.4 0.1 broadcast_in_dim.36.refs_1_
  48.5 0.0 copy-done.2
  48.5 0.0 copy-start.6
  48.6 7.7 %grid.1 = f32[16,104,128]{2,1,0:T(8,128)} custom-call(f32[16,96,128]{2,1,0:T(8,128)S(1)} %all-to-all-done.refs_0_, s32[512,128]{1,0:T(8,128)S(1)} %broadcast_in_dim.36.refs_1_, f32[64,2048]{1,0:T(8,128)S(1)} %bitcast.6, f32[64,128]{1,0:T(8,128)S(1)} %broadcast_in_dim.37.refs_3_, bf16[2,512,1024]{2,1,0:T(8,128)(2,1)S(1)} %get-tuple-element.7.refs_4_, ...), custom_call_target="tpu_custom_call" | custom-call | flops 8000000000 | bytes 1048576 | tf_op jit(solution)/shard_map/grid/pallas_call | solution.py:565
  56.2 4.9 %all-to-all-start.1 = ((f32[16,104,128]{2,1,0:T(8,128)}), f32[16,104,128]{2,1,0:T(8,128)S(1)}, u32[]{:S(2)}, u32[]{:S(2)}) async-start(f32[16,104,128]{2,1,0:T(8,128)} %grid.1), calls=%async_computation.1 | async-start | bytes 1703936 | tf_op jit(solution)/shard_map/all_to_all | solution.py:526
  61.1 0.0 copy-done.6
  61.1 20.1 %table.1.refs_4_ = bf16[4,8,1024,512]{3,2,1,0:T(8,128)(2,1)} custom-call(s32[512]{0:T(512)S(1)} %reshape.23.refs_0_, f32[8,512]{1,0:T(8,128)S(1)} %copy-done.6), custom_call_target="tpu_custom_call" | custom-call | flops 12000000000 | bytes 1048576 | tf_op jit(solution)/shard_map/table/pallas_call | solution.py:583
  81.3 0.0 all-to-all-done.1.refs_2_
  81.3 17.1 %analyze.1 = f32[6,32,512]{2,1,0:T(8,128)} custom-call(s32[512]{0:T(512)S(1)} %reshape.23.refs_0_, s32[512]{0:T(512)S(1)} %reshape.24.refs_1_, f32[16,104,128]{2,1,0:T(8,128)S(1)} %all-to-all-done.1.refs_2_, s32[1,1024]{1,0:T(1,128)S(1)} %bitcast.5, bf16[4,8,1024,512]{3,2,1,0:T(8,128)(2,1)} %table.1.refs_4_), custom_call_target="tpu_custom_call" | custom-call | flops 8999999488 | bytes 1048576 | tf_op jit(solution)/shard_map/analyze/pallas_call | solution.py:595
  (1 shorter events, 0.0 us)
Async XLA Ops:
  2.0 0.7 copy-start
  2.7 1.0 %copy-start.3 = (f32[1,3,2,32,512]{4,3,2,1,0:T(8,128)S(1)}, f32[1,3,2,32,512]{4,3,2,1,0:T(8,128)}, u32[]{:S(2)}) copy-start(f32[1,3,2,32,512]{4,3,2,1,0:T(8,128)} %param.6) | copy-start | bytes 1179652
  3.7 0.9 copy-start.4
  4.6 0.7 copy-start.5
  5.4 23.2 %copy-start.1 = (s32[1024]{0:T(1024)S(1)}, s32[1024]{0:T(1024)}, u32[]{:S(2)}) copy-start(s32[1024]{0:T(1024)} %param.8) | copy-start | bytes 12292
  22.9 25.5 %all-to-all-start = ((f32[16,96,128]{2,1,0:T(8,128)}), f32[16,96,128]{2,1,0:T(8,128)S(1)}, u32[]{:S(2)}, u32[]{:S(2)}) async-start(f32[16,96,128]{2,1,0:T(8,128)} %synth.1), calls=%async_computation | async-start | bytes 1572864 | tf_op jit(solution)/shard_map/all_to_all | solution.py:526
  28.7 19.8 %copy-start.2 = (f32[1,64,2048]{2,1,0:T(8,128)S(1)}, f32[1,64,2048]{2,1,0:T(8,128)}, u32[]{:S(2)}) copy-start(f32[1,64,2048]{2,1,0:T(8,128)} %param.7) | copy-start | bytes 1572868
  31.0 1.3 %copy-start.7 = (bf16[2,512,1024]{2,1,0:T(8,128)(2,1)}, bf16[2,512,1024]{2,1,0:T(8,128)(2,1)S(1)}, u32[]{:S(2)}) copy-start(bf16[2,512,1024]{2,1,0:T(8,128)(2,1)S(1)} %get-tuple-element.8.refs_5_) | copy-start | bytes 6291460
  48.5 12.6 %copy-start.6 = (f32[8,512]{1,0:T(8,128)S(1)}, f32[8,512]{1,0:T(8,128)}, u32[]{:S(2)}) copy-start(f32[8,512]{1,0:T(8,128)} %constant.23.clone.refs_3_.refs_1_) | copy-start | bytes 49156
  56.2 25.0 %all-to-all-start.1 = ((f32[16,104,128]{2,1,0:T(8,128)}), f32[16,104,128]{2,1,0:T(8,128)S(1)}, u32[]{:S(2)}, u32[]{:S(2)}) async-start(f32[16,104,128]{2,1,0:T(8,128)} %grid.1), calls=%async_computation.1 | async-start | bytes 1703936 | tf_op jit(solution)/shard_map/all_to_all | solution.py:526

commit v3 on v2

--- a/solution.py
+++ b/solution.py
@@ -18,6 +18,7 @@
 BLK = 8
 ROWS = CHAN * BLK
 CHUNK = 64
+CHECK = 16
 LANES = 128
 KTILE = 256
 BF = jnp.bfloat16
@@ -55,6 +56,12 @@
     return spread.reshape(LANES, 2 * 2 * (CHUNK // 2) * BLK).astype(BF)
 
 
+def degree_scalars():
+    before = np.arange(DEG, dtype=np.float64) - 1.0
+    square = before * before
+    return np.concatenate([square, 4.0 / (4.0 * square - 1.0)]).astype(np.float32)
+
+
 def block_orders(slots_ref, first):
     sublane = lax.broadcasted_iota(jnp.int32, (BLK, LANES), 0)
     orders = jnp.zeros((BLK, LANES), jnp.int32)
@@ -63,40 +70,57 @@
         order = slots_ref[first + i]
         orders = jnp.where(sublane == i, order, orders)
         lowest = jnp.minimum(lowest, order)
-    return orders[:, :1], lowest
-
-
-def recursion_tables(order, rows_ref, alpha_ref, beta_ref):
-    degree = lax.broadcasted_iota(jnp.int32, (BLK, DEG), 1).astype(F32)
-    order_sq = order * order
-    denominator = degree * degree - order_sq
-    safe = jnp.where(denominator > 0, denominator, 1.0)
-    alpha = jnp.sqrt((4.0 * degree * degree - 1.0) / safe)
-    back = jnp.maximum((degree - 1.0) * (degree - 1.0) - order_sq, 0.0)
-    beta = jnp.sqrt(back * (2.0 * degree + 1.0) / (safe * jnp.maximum(2.0 * degree - 3.0, 1.0)))
-    alpha_ref[...] = jnp.where(degree > order, alpha, 0.0)
-    beta_ref[...] = jnp.where(degree > order, beta, -1.0)
+    return orders, lowest
+
+
+def running_sum(terms, length):
+    lane = lax.broadcasted_iota(jnp.int32, terms.shape, 1) & (length - 1)
+    shift = 1
+    while shift < length:
+        moved = pltpu.roll(terms, shift, 1)
+        terms = terms + jnp.where(lane >= shift, moved, 0.0)
+        shift *= 2
+    return terms
+
+
+def recursion_tables(slots_ref, base, modes, rows_ref, start_ref, before_ref, within_ref):
+    orders = [block_orders(slots_ref, base + at)[0][:, :1] for at in range(0, modes, BLK)]
+    order = jnp.concatenate(orders, 0).astype(F32)
+    position = lax.broadcasted_iota(jnp.int32, (modes, DEG), 1)
+    degree = position.astype(F32)
+    square = degree * degree
+    above = degree > order
+    gap = jnp.where(above, square - order * order, 1.0)
+    growth = jnp.where(above, 0.5 * jnp.log2((square - 0.25) / gap), 0.0)
+    before_ref[...] = running_sum(growth, DEG)
+    later = jnp.where(position & (CHECK - 1) == 0, 0.0, growth)
+    within_ref[...] = jnp.exp2(running_sum(later, CHECK))
     terms = jnp.where(degree <= order, rows_ref[2:3, :], 0.0)
     norm = jnp.where(order > 0, 0.5 + jnp.sum(terms, axis=1, keepdims=True), 0.0)
-    return norm + order * rows_ref[1:2, :]
-
-
-def run_chunk(step, carry, cosine, alpha_ref, beta_ref, emit, beside):
+    start_ref[...] = norm + order * rows_ref[1:2, :]
+
+
+def run_chunk(step, carry, double_cosine, orders, before, scalars_ref, emit, beside):
     current, previous, log_scale = carry
-    tile = pl.ds(pl.multiple_of(step // 2 * LANES, LANES), LANES)
-    shift = (step % 2) * CHUNK
-    alpha = pltpu.roll(alpha_ref[:, tile], shift, 1)
-    beta = pltpu.roll(beta_ref[:, tile], shift, 1)
+    order = orders.astype(F32)
+    order_square = order * order
+    before = pltpu.roll(before, (step % 2) * CHUNK, 1)
     scale = None
     for i in range(CHUNK):
-        if i % 16 == 0:
-            large = jnp.abs(current) > 2.0**60
-            factor = jnp.where(large, 2.0**-60, 1.0)
+        if i % CHECK == 0:
+            size = jnp.maximum(jnp.abs(current), jnp.abs(previous))
+            large, small = size > 2.0**40, size < 2.0**-40
+            factor = jnp.where(large, 2.0**-60, jnp.where(small, 2.0**60, 1.0))
+            change = jnp.where(large, 60.0, jnp.where(small, -60.0, 0.0))
             current = current * factor
             previous = previous * factor
-            log_scale = jnp.where(large, log_scale + 60.0, log_scale)
-            scale = jnp.exp2(jnp.maximum(log_scale, -200.0))
-        newest = (alpha[:, i : i + 1] * cosine) * current - beta[:, i : i + 1] * previous
+            log_scale = log_scale + change
+            scale = jnp.exp2(jnp.maximum(log_scale + before[:, i : i + 1], -200.0))
+        degree = step * CHUNK + i
+        factor = (scalars_ref[degree] - order_square) * scalars_ref[DEG + degree]
+        factor = jnp.tile(factor, (1, HALF // LANES))
+        started = jnp.tile(orders, (1, HALF // LANES)) < degree
+        newest = jnp.where(started, double_cosine * current - factor * previous, 1.0)
         current, previous = newest, current
         emit(i, newest * scale)
         if beside and i % (CHUNK // len(beside)) == 1:
@@ -104,9 +128,14 @@
     return current, previous, log_scale
 
 
-def start_state(log_start):
+def before_tile(before_ref, block, step):
+    rows = pl.ds(pl.multiple_of(block * BLK, BLK), BLK)
+    return before_ref[rows, pl.ds(pl.multiple_of(step // 2 * LANES, LANES), LANES)]
+
+
+def start_state(start_ref, block):
     ones = jnp.ones((BLK, HALF), F32)
-    return ones, ones, log_start
+    return ones, ones, start_ref[pl.ds(pl.multiple_of(block * BLK, BLK), BLK), :]
 
 
 def fold_matrix(latitude_ref, fold_ref):
@@ -117,12 +146,13 @@
 
 
 def synth_kernel(
-    dims, slots_ref, place_ref, spec_ref, rows_ref, spread_ref, latitude_ref, out_ref,
-    alpha_ref, beta_ref, lhs_ref, high_a, low_a, high_b, low_b, acc_ref, fold_ref, coeff_ref,
+    dims, slots_ref, place_ref, scalars_ref, spec_ref, rows_ref, spread_ref, latitude_ref,
+    out_ref, start_ref, before_ref, within_ref, lhs_ref, high_a, low_a, high_b, low_b, acc_ref, fold_ref, coeff_ref,
 ):
     bands, row_count, modes, blocks, tiles = dims
     fold_matrix(latitude_ref, fold_ref)
     base = lax.axis_index("band") * modes
+    recursion_tables(slots_ref, base, modes, rows_ref, start_ref, before_ref, within_ref)
     south = latitude_ref[...] >= HALF
     spread_width = 4 * (CHUNK // 2) * BLK
     lane = lax.broadcasted_iota(jnp.int32, (2 * ROWS, spread_width), 1)
@@ -132,13 +162,14 @@
 
     def one_block(block, unused):
         orders, lowest = block_orders(slots_ref, base + block * BLK)
-        order = orders.astype(F32)
-        log_start = recursion_tables(order, rows_ref, alpha_ref, beta_ref)
+        column = orders[:, :1]
+        here = pl.ds(pl.multiple_of(block * BLK, BLK), BLK)
         for i in range(BLK):
             source = pl.ds(place_ref[base + block * BLK + i], 1)
             coeff_ref[:, i : i + 1, :] = spec_ref[:, source, :]
         degree = lax.broadcasted_iota(jnp.int32, (BLK, DEG), 1)
-        coeffs = jnp.where((degree >= orders)[None], coeff_ref[...], 0.0)
+        within = jnp.where(degree >= column, within_ref[here, :], 0.0)
+        coeffs = coeff_ref[...] * within[None]
         coeff_high, coeff_low = split_two(coeffs.reshape(ROWS, DEG))
         stacked = jnp.concatenate([coeff_high, coeff_low], 0)
         for t in range(DEG // LANES):
@@ -147,7 +178,7 @@
             for half in range(2):
                 lhs_ref[2 * t + half] = wide[:, half * 2 * width : (half + 1) * 2 * width]
         acc_ref[...] = jnp.zeros_like(acc_ref)
-        cosine = jnp.broadcast_to(rows_ref[0:1, :], (BLK, HALF))
+        cosine = jnp.broadcast_to(2.0 * rows_ref[0:1, :], (BLK, HALF))
 
         def recur(step, carry, high_ref, low_ref, beside):
             held = {}
@@ -162,7 +193,8 @@
                     high_ref[i % 2, at : at + 2 * BLK, :] = high
                     low_ref[i % 2, at : at + 2 * BLK, :] = low
 
-            return run_chunk(step, carry, cosine, alpha_ref, beta_ref, emit, beside)
+            before = before_tile(before_ref, block, step)
+            return run_chunk(step, carry, cosine, orders, before, scalars_ref, emit, beside)
 
         def add_products(step, high_ref, low_ref):
             def part(parity, columns):
@@ -187,14 +219,14 @@
         high_b[...] = jnp.zeros_like(high_b)
         low_b[...] = jnp.zeros_like(low_b)
         chunks = DEG // CHUNK
-        lax.fori_loop(lowest // (2 * CHUNK), chunks // 2, two_chunks, start_state(log_start))
+        lax.fori_loop(lowest // (2 * CHUNK), chunks // 2, two_chunks, start_state(start_ref, block))
         for part in add_products(chunks - 1, high_b, low_b):
             part()
         both = acc_ref[...].reshape(2 * ROWS, HALF)
         high, low = split_two(both)
         moved = dot(jnp.concatenate([high, low], 0), fold_ref[...])
         moved = moved[: 2 * ROWS] + moved[2 * ROWS :]
-        sign = jnp.tile(1.0 - 2.0 * (orders % 2).astype(F32), (CHAN, 1))
+        sign = jnp.tile(1.0 - 2.0 * (column % 2).astype(F32), (CHAN, 1))
         even, odd = moved[:ROWS], moved[ROWS:]
         values = jnp.where(south, sign * (even - odd), even + odd)
         for d in range(bands):
@@ -217,11 +249,13 @@
 
 
 def table_kernel(
-    dims, slots_ref, rows_ref, out_ref, alpha_ref, beta_ref, first_ref, second_ref, sems,
+    dims, slots_ref, scalars_ref, rows_ref, out_ref, within_out, start_ref, before_ref,
+    first_ref, second_ref, sems,
 ):
     modes, blocks = dims
     base = lax.axis_index("band") * modes
-    cosine = jnp.broadcast_to(rows_ref[0:1, :], (BLK, HALF))
+    cosine = jnp.broadcast_to(2.0 * rows_ref[0:1, :], (BLK, HALF))
+    recursion_tables(slots_ref, base, modes, rows_ref, start_ref, before_ref, within_out)
     buffers = (first_ref, second_ref)
 
     def copy_out(which, block, step):
@@ -229,7 +263,6 @@
 
     def one_block(block, unused):
         orders, lowest = block_orders(slots_ref, base + block * BLK)
-        log_start = recursion_tables(orders.astype(F32), rows_ref, alpha_ref, beta_ref)
         start = lowest // (2 * CHUNK)
 
         def recur(which, step, carry, pending):
@@ -251,7 +284,8 @@
                     buffer[at : at + 2 * BLK, :] = high
                     buffer[CHUNK * BLK + at : CHUNK * BLK + at + 2 * BLK, :] = low
 
-            carry = run_chunk(step, carry, cosine, alpha_ref, beta_ref, emit, ())
+            before = before_tile(before_ref, block, step)
+            carry = run_chunk(step, carry, cosine, orders, before, scalars_ref, emit, ())
             copy_out(which, block, step).start()
             return carry
 
@@ -260,7 +294,7 @@
             carry = recur(0, 2 * pair, carry, pending)
             return recur(1, 2 * pair + 1, carry, pending)
 
-        lax.fori_loop(start, DEG // CHUNK // 2, two_chunks, start_state(log_start))
+        lax.fori_loop(start, DEG // CHUNK // 2, two_chunks, start_state(start_ref, block))
         return unused
 
     lax.fori_loop(0, blocks, one_block, 0)
@@ -269,7 +303,7 @@
 
 
 def analyze_kernel(
-    dims, total_row, slots_ref, place_ref, data_ref, latitude_ref, table_ref, out_ref,
+    dims, total_row, slots_ref, place_ref, data_ref, latitude_ref, within_ref, table_ref, out_ref,
     chunk_ref, weight_ref, result_ref, fold_ref, coeff_ref, sems,
 ):
     bands, row_count, modes, blocks, tiles = dims
@@ -303,6 +337,8 @@
 
     def one_block(block, unused):
         orders, lowest = block_orders(slots_ref, base + block * BLK)
+        orders = orders[:, :1]
+        here = pl.ds(pl.multiple_of(block * BLK, BLK), BLK)
         sign = 1.0 - 2.0 * (orders % 2).astype(F32)
         evens, odds = [], []
         for c in range(CHAN):
@@ -338,8 +374,9 @@
         turned = result_ref[...].T
         turned = turned[:ROWS] + turned[ROWS : 2 * ROWS]
         degree = lax.broadcasted_iota(jnp.int32, (BLK, DEG), 1)
+        within = jnp.where(degree >= orders, within_ref[here, :], 0.0)
         for c in range(CHAN):
-            part = jnp.where(degree >= orders, turned[c * BLK : (c + 1) * BLK], 0.0)
+            part = turned[c * BLK : (c + 1) * BLK] * within
             if c // 2 == FIELDS - 1:
                 part = part * inverse
             coeff_ref[c] = part
@@ -520,7 +557,8 @@
     params = pltpu.CompilerParams(vmem_limit_bytes=48 * 2**20)
     chunk_rows = tiles * modes
     dims = (bands, row_count, modes, blocks, tiles)
-    recursion_scratch = [pltpu.VMEM((BLK, DEG), F32)] * 2
+    scalars = jnp.asarray(degree_scalars())
+    per_order = pltpu.VMEM((modes, DEG), F32)
 
     def exchange(value):
         return lax.all_to_all(value, "band", split_axis=0, concat_axis=0, tiled=True)
@@ -528,9 +566,9 @@
     sent = pl.pallas_call(
         lambda *refs: synth_kernel(dims, *refs),
         out_shape=jax.ShapeDtypeStruct((bands, chunk_rows, LANES), F32),
-        in_specs=[SMEM, SMEM, VMEM, VMEM, VMEM, VMEM],
+        in_specs=[SMEM, SMEM, SMEM, VMEM, VMEM, VMEM, VMEM],
         out_specs=VMEM,
-        scratch_shapes=recursion_scratch
+        scratch_shapes=[per_order] * 3
         + [pltpu.VMEM((chunks, 2 * ROWS, CHUNK * BLK), BF)]
         + [pltpu.VMEM((2, CHUNK // 2 * BLK, HALF), BF)] * 4
         + [
@@ -541,7 +579,7 @@
         compiler_params=params,
         cost_estimate=work(15),
         name="synth",
-    )(ordered, places, coeffs, rows, spread, latitude)
+    )(ordered, places, scalars, coeffs, rows, spread, latitude)
     received = exchange(sent)
 
     trig_shape = jax.ShapeDtypeStruct((2, slots, NLON // 2), BF)
@@ -580,22 +618,25 @@
     returned = exchange(fluxes)
 
     chunk_shape = (blocks, chunks, 2 * CHUNK * BLK, HALF)
-    legendre = pl.pallas_call(
+    legendre, within = pl.pallas_call(
         lambda *refs: table_kernel((modes, blocks), *refs),
-        out_shape=jax.ShapeDtypeStruct(chunk_shape, BF),
-        in_specs=[SMEM, VMEM],
-        out_specs=ANY,
-        scratch_shapes=recursion_scratch
+        out_shape=[
+            jax.ShapeDtypeStruct(chunk_shape, BF),
+            jax.ShapeDtypeStruct((modes, DEG), F32),
+        ],
+        in_specs=[SMEM, SMEM, VMEM],
+        out_specs=[ANY, VMEM],
+        scratch_shapes=[per_order] * 2
         + [pltpu.VMEM((2 * CHUNK * BLK, HALF), BF)] * 2
         + [pltpu.SemaphoreType.DMA((2,))],
         compiler_params=params,
         cost_estimate=work(12),
         name="table",
-    )(ordered, rows)
+    )(ordered, scalars, rows)
     result = pl.pallas_call(
         lambda *refs: analyze_kernel(dims, chunk_rows, *refs),
         out_shape=jax.ShapeDtypeStruct((CHAN, modes, DEG), F32),
-        in_specs=[SMEM, SMEM, VMEM, VMEM, ANY],
+        in_specs=[SMEM, SMEM, VMEM, VMEM, VMEM, ANY],
         out_specs=VMEM,
         scratch_shapes=[
             pltpu.VMEM(chunk_shape, BF),
@@ -608,7 +649,7 @@
         compiler_params=params,
         cost_estimate=work(9),
         name="analyze",
-    )(ordered, places, returned, latitude, legendre)
+    )(ordered, places, returned, latitude, within, legendre)
     return result.reshape(1, FIELDS, 2, modes, DEG)
 
 

time: 98.7 us -> 101 us (1.023)
  local copies, waits for them, and re-layouts: 5.81 us -> 9.4 us
  Pallas kernels: 64.7 us -> 62.1 us
  starting transfers between devices: 10.6 us -> 12.3 us
    unnamed x16 -> x24, local copies, waits for them, and re-layouts: 4.7 us -> 8.29 us
    all_to_all x2, starting transfers between devices: 10.6 us -> 12.3 us  [exchange(): lax.all_to_all(value, 'band', split_axis=0, concat_axis=0, tiled=True)]
    pallas_call x1, Pallas kernels: 20.1 us -> 18.5 us  [per_device(): pl.pallas_call(lambda *refs: table_kernel((modes, blocks), *refs), out_sh...]
  transfers between devices with their start and end apart: 2 -> 2, of which waited for: 1 -> 2; matrix products, arithmetic and copies ran while one was open for 0% -> 0% of each run, Pallas kernels for 23% -> 21%
where the time goes in v3:
time: 101 us
  Pallas kernels  62.1 us (61%)
  waiting for transfers between devices  15.9 us (16%)
  starting transfers between devices  12.3 us (12%)
  local copies, waits for them, and re-layouts  9.4 us (9%)
  other arithmetic  1.19 us (1%)
    pallas_call x1, Pallas kernels, per_device(): pl.pallas_call(lambda *refs: table_kernel((modes, blocks), *refs), out_sh...  18.5 us
    pallas_call x1, Pallas kernels, per_device(): pl.pallas_call(lambda *refs: synth_kernel(dims, *refs), out_shape=jax.Sha...  17.4 us
    pallas_call x1, Pallas kernels, per_device(): pl.pallas_call(lambda *refs: analyze_kernel(dims, chunk_rows, *refs), out...  16.2 us
    all_to_all x2, waiting for transfers between devices, exchange(): lax.all_to_all(value, 'band', split_axis=0, concat_axis=0, tiled=True)  15.9 us
    all_to_all x2, starting transfers between devices, exchange(): lax.all_to_all(value, 'band', split_axis=0, concat_axis=0, tiled=True)  12.3 us
    unnamed x24, local copies, waits for them, and re-layouts  8.29 us
    pallas_call x1, Pallas kernels, per_device(): pl.pallas_call(lambda *refs: grid_kernel(grid_dims, *refs), out_shape=jax...  7.66 us
    pallas_call x1, Pallas kernels, per_device(): pl.pallas_call(trig_kernel, out_shape=[trig_shape, trig_shape], out_specs...  2.28 us
  transfers between devices with their start and end apart: 2, of which 2 were waited for; matrix products, arithmetic and copies ran while one was open for 0% of the time, Pallas kernels for 21%

profile of v3, /device:TPU:0, one launch (start us, length us, event | category | flops | bytes accessed | tf_op | source)
XLA Modules:
  0.0 101.0 jit_solution(12019117197041936264)
XLA Ops:
  0.0 0.8 lt.18
  0.8 0.5 convert_reduce_fusion
  1.2 0.6 select_reduce_fusion
  1.8 0.1 reshape.24.refs_1_
  1.9 0.1 reshape.23.refs_0_
  2.0 0.7 copy-done
  2.7 1.0 copy-done.3
  3.7 0.9 copy-done.4
  4.6 0.7 copy-done.5
  5.4 0.7 copy-done.7
  6.0 17.4 %synth.1 = f32[16,96,128]{2,1,0:T(8,128)} custom-call(s32[512]{0:T(512)S(1)} %reshape.23.refs_0_, s32[512]{0:T(512)S(1)} %reshape.24.refs_1_, f32[1024]{0:T(1024)S(1)} %copy-done.7, f32[6,32,512]{2,1,0:T(8,128)S(1)} %bitcast.7, f32[8,512]{1,0:T(8,128)S(1)} %copy-done.5, bf16[128,1024]{1,0:T(8,128)(2,1)S(1)} %copy-done.4, s32[1,1024]{1,0:T(1,128)S(1)} %bitcast.4), custom_call_target="tpu_custom_call" | custom-call | flops 15000000512 | bytes 1048576 | tf_op jit(solution)/shard_map/synth/pallas_call | solution.py:566
  23.4 7.4 %all-to-all-start = ((f32[16,96,128]{2,1,0:T(8,128)}), f32[16,96,128]{2,1,0:T(8,128)S(1)}, u32[]{:S(2)}, u32[]{:S(2)}) async-start(f32[16,96,128]{2,1,0:T(8,128)} %synth.1), calls=%async_computation | async-start | bytes 1572864 | tf_op jit(solution)/shard_map/all_to_all | solution.py:564
  30.8 0.0 copy-done.1
  30.8 0.1 multiply_sine_fusion
  30.9 0.0 copy-start.2
  30.9 2.3 %trig.1 = (bf16[2,512,1024]{2,1,0:T(8,128)(2,1)S(1)}, bf16[2,512,1024]{2,1,0:T(8,128)(2,1)S(1)}) custom-call(), custom_call_target="tpu_custom_call" | custom-call | flops 4000000000 | bytes 1048576 | tf_op jit(solution)/shard_map/trig/pallas_call | solution.py:586
  33.2 0.0 copy-start.9
  33.2 1.3 %copy-done.9 = bf16[2,512,1024]{2,1,0:T(8,128)(2,1)} copy-done((bf16[2,512,1024]{2,1,0:T(8,128)(2,1)}, bf16[2,512,1024]{2,1,0:T(8,128)(2,1)S(1)}, u32[]{:S(2)}) %copy-start.9) | copy-done | bytes 2097176
  34.6 1.3 %copy-done.11 = bf16[2,512,1024]{2,1,0:T(8,128)(2,1)} copy-done((bf16[2,512,1024]{2,1,0:T(8,128)(2,1)}, bf16[2,512,1024]{2,1,0:T(8,128)(2,1)S(1)}, u32[]{:S(2)}) %copy-start.11) | copy-done | bytes 2097176
  35.9 14.7 %all-to-all-done.refs_0_ = f32[16,96,128]{2,1,0:T(8,128)S(1)} async-done(((f32[16,96,128]{2,1,0:T(8,128)}), f32[16,96,128]{2,1,0:T(8,128)S(1)}, u32[]{:S(2)}, u32[]{:S(2)}) %all-to-all-start) | async-done | bytes 786464 | tf_op jit(solution)/shard_map/all_to_all | solution.py:564
  50.5 0.1 broadcast_in_dim.37.refs_3_
  50.6 0.1 broadcast_in_dim.36.refs_1_
  50.8 0.0 copy-done.2
  50.8 0.0 copy-start.10
  50.8 1.6 %copy-done.10 = bf16[2,512,1024]{2,1,0:T(8,128)(2,1)S(1)} copy-done((bf16[2,512,1024]{2,1,0:T(8,128)(2,1)S(1)}, bf16[2,512,1024]{2,1,0:T(8,128)(2,1)}, u32[]{:S(2)}) %copy-start.10) | copy-done | bytes 2097176
  52.4 7.7 %grid.1 = f32[16,104,128]{2,1,0:T(8,128)} custom-call(f32[16,96,128]{2,1,0:T(8,128)S(1)} %all-to-all-done.refs_0_, s32[512,128]{1,0:T(8,128)S(1)} %broadcast_in_dim.36.refs_1_, f32[64,2048]{1,0:T(8,128)S(1)} %bitcast.6, f32[64,128]{1,0:T(8,128)S(1)} %broadcast_in_dim.37.refs_3_, bf16[2,512,1024]{2,1,0:T(8,128)(2,1)S(1)} %copy-done.10, ...), custom_call_target="tpu_custom_call" | custom-call | flops 8000000000 | bytes 1048576 | tf_op jit(solution)/shard_map/grid/pallas_call | solution.py:603
  60.0 4.9 %all-to-all-start.1 = ((f32[16,104,128]{2,1,0:T(8,128)}), f32[16,104,128]{2,1,0:T(8,128)S(1)}, u32[]{:S(2)}, u32[]{:S(2)}) async-start(f32[16,104,128]{2,1,0:T(8,128)} %grid.1), calls=%async_computation.1 | async-start | bytes 1703936 | tf_op jit(solution)/shard_map/all_to_all | solution.py:564
  64.9 0.0 copy-done.6
  64.9 0.0 copy-done.8
  64.9 18.5 %table.1 = (bf16[4,8,1024,512]{3,2,1,0:T(8,128)(2,1)}, f32[32,512]{1,0:T(8,128)S(1)}) custom-call(s32[512]{0:T(512)S(1)} %reshape.23.refs_0_, f32[1024]{0:T(1024)S(1)} %copy-done.8, f32[8,512]{1,0:T(8,128)S(1)} %copy-done.6), custom_call_target="tpu_custom_call" | custom-call | flops 12000000000 | bytes 1048576 | tf_op jit(solution)/shard_map/table/pallas_call | solution.py:621
  83.5 1.2 %all-to-all-done.1.refs_2_ = f32[16,104,128]{2,1,0:T(8,128)S(1)} async-done(((f32[16,104,128]{2,1,0:T(8,128)}), f32[16,104,128]{2,1,0:T(8,128)S(1)}, u32[]{:S(2)}, u32[]{:S(2)}) %all-to-all-start.1) | async-done | bytes 852000 | tf_op jit(solution)/shard_map/all_to_all | solution.py:564
  84.7 16.2 %analyze.1 = f32[6,32,512]{2,1,0:T(8,128)} custom-call(s32[512]{0:T(512)S(1)} %reshape.23.refs_0_, s32[512]{0:T(512)S(1)} %reshape.24.refs_1_, f32[16,104,128]{2,1,0:T(8,128)S(1)} %all-to-all-done.1.refs_2_, s32[1,1024]{1,0:T(1,128)S(1)} %bitcast.5, f32[32,512]{1,0:T(8,128)S(1)} %get-tuple-element.11.refs_4_, bf16[4,8,1024,512]{3,2,1,0:T(8,128)(2,1)} %get-tuple-element.12.refs_5_), custom_call_target="tpu_custom_call" | custom-call | flops 8999999488 | bytes 1048576 | tf_op jit(solution)/shard_map/analyze/pallas_call | solution.py:636
  (9 shorter events, 0.0 us)
Async XLA Ops:
  2.0 0.7 copy-start
  2.7 1.0 copy-start.3
  3.7 0.9 copy-start.4
  4.6 0.7 copy-start.5
  5.4 0.7 copy-start.7
  6.0 24.8 %copy-start.1 = (s32[1024]{0:T(1024)S(1)}, s32[1024]{0:T(1024)}, u32[]{:S(2)}) copy-start(s32[1024]{0:T(1024)} %param.9) | copy-start | bytes 12292
  23.4 27.1 %all-to-all-start = ((f32[16,96,128]{2,1,0:T(8,128)}), f32[16,96,128]{2,1,0:T(8,128)S(1)}, u32[]{:S(2)}, u32[]{:S(2)}) async-start(f32[16,96,128]{2,1,0:T(8,128)} %synth.1), calls=%async_computation | async-start | bytes 1572864 | tf_op jit(solution)/shard_map/all_to_all | solution.py:564
  30.9 19.8 %copy-start.2 = (f32[1,64,2048]{2,1,0:T(8,128)S(1)}, f32[1,64,2048]{2,1,0:T(8,128)}, u32[]{:S(2)}) copy-start(f32[1,64,2048]{2,1,0:T(8,128)} %param.8) | copy-start | bytes 1572868
  33.2 1.3 %copy-start.9 = (bf16[2,512,1024]{2,1,0:T(8,128)(2,1)}, bf16[2,512,1024]{2,1,0:T(8,128)(2,1)S(1)}, u32[]{:S(2)}) copy-start(bf16[2,512,1024]{2,1,0:T(8,128)(2,1)S(1)} %get-tuple-element.9.refs_4_) | copy-start | bytes 6291460
  34.6 1.3 %copy-start.11 = (bf16[2,512,1024]{2,1,0:T(8,128)(2,1)}, bf16[2,512,1024]{2,1,0:T(8,128)(2,1)S(1)}, u32[]{:S(2)}) copy-start(bf16[2,512,1024]{2,1,0:T(8,128)(2,1)S(1)} %get-tuple-element.10.refs_5_) | copy-start | bytes 6291460
  50.8 1.6 %copy-start.10 = (bf16[2,512,1024]{2,1,0:T(8,128)(2,1)S(1)}, bf16[2,512,1024]{2,1,0:T(8,128)(2,1)}, u32[]{:S(2)}) copy-start(bf16[2,512,1024]{2,1,0:T(8,128)(2,1)} %copy-done.9) | copy-start | bytes 6291460
  52.4 12.6 %copy-start.6 = (f32[8,512]{1,0:T(8,128)S(1)}, f32[8,512]{1,0:T(8,128)}, u32[]{:S(2)}) copy-start(f32[8,512]{1,0:T(8,128)} %constant.25.clone.refs_4_.refs_2_) | copy-start | bytes 49156
  52.4 12.6 %copy-start.8 = (f32[1024]{0:T(1024)S(1)}, f32[1024]{0:T(1024)}, u32[]{:S(2)}) copy-start(f32[1024]{0:T(1024)} %constant.27.clone.refs_2_.refs_1_) | copy-start | bytes 12292
  60.0 24.7 %all-to-all-start.1 = ((f32[16,104,128]{2,1,0:T(8,128)}), f32[16,104,128]{2,1,0:T(8,128)S(1)}, u32[]{:S(2)}, u32[]{:S(2)}) async-start(f32[16,104,128]{2,1,0:T(8,128)} %grid.1), calls=%async_computation.1 | async-start | bytes 1703936 | tf_op jit(solution)/shard_map/all_to_all | solution.py:564

commit v4 on v3

--- a/solution.py
+++ b/solution.py
@@ -83,8 +83,8 @@
     return terms
 
 
-def recursion_tables(slots_ref, base, modes, rows_ref, start_ref, before_ref, within_ref):
-    orders = [block_orders(slots_ref, base + at)[0][:, :1] for at in range(0, modes, BLK)]
+def recursion_tables(slots_ref, modes, rows_ref, start_ref, before_ref, within_ref):
+    orders = [block_orders(slots_ref, at)[0][:, :1] for at in range(0, modes, BLK)]
     order = jnp.concatenate(orders, 0).astype(F32)
     position = lax.broadcasted_iota(jnp.int32, (modes, DEG), 1)
     degree = position.astype(F32)
@@ -146,13 +146,12 @@
 
 
 def synth_kernel(
-    dims, slots_ref, place_ref, scalars_ref, spec_ref, rows_ref, spread_ref, latitude_ref,
+    dims, slots_ref, scalars_ref, spec_ref, rows_ref, spread_ref, latitude_ref,
     out_ref, start_ref, before_ref, within_ref, lhs_ref, high_a, low_a, high_b, low_b, acc_ref, fold_ref, coeff_ref,
 ):
     bands, row_count, modes, blocks, tiles = dims
     fold_matrix(latitude_ref, fold_ref)
-    base = lax.axis_index("band") * modes
-    recursion_tables(slots_ref, base, modes, rows_ref, start_ref, before_ref, within_ref)
+    recursion_tables(slots_ref, modes, rows_ref, start_ref, before_ref, within_ref)
     south = latitude_ref[...] >= HALF
     spread_width = 4 * (CHUNK // 2) * BLK
     lane = lax.broadcasted_iota(jnp.int32, (2 * ROWS, spread_width), 1)
@@ -161,11 +160,11 @@
     width = (CHUNK // 2) * BLK
 
     def one_block(block, unused):
-        orders, lowest = block_orders(slots_ref, base + block * BLK)
+        orders, lowest = block_orders(slots_ref, block * BLK)
         column = orders[:, :1]
         here = pl.ds(pl.multiple_of(block * BLK, BLK), BLK)
         for i in range(BLK):
-            source = pl.ds(place_ref[base + block * BLK + i], 1)
+            source = pl.ds(slots_ref[modes + block * BLK + i], 1)
             coeff_ref[:, i : i + 1, :] = spec_ref[:, source, :]
         degree = lax.broadcasted_iota(jnp.int32, (BLK, DEG), 1)
         within = jnp.where(degree >= column, within_ref[here, :], 0.0)
@@ -177,7 +176,7 @@
             wide = jnp.where(diagonal, wide, 0.0).astype(BF)
             for half in range(2):
                 lhs_ref[2 * t + half] = wide[:, half * 2 * width : (half + 1) * 2 * width]
-        acc_ref[...] = jnp.zeros_like(acc_ref)
+        acc_ref[block] = jnp.zeros((2, ROWS, HALF), F32)
         cosine = jnp.broadcast_to(2.0 * rows_ref[0:1, :], (BLK, HALF))
 
         def recur(step, carry, high_ref, low_ref, beside):
@@ -201,7 +200,7 @@
                 lhs = lhs_ref[step, :, parity * width : (parity + 1) * width]
                 first = dot(lhs, high_ref[parity, :, columns])
                 second = dot(lhs[:ROWS], low_ref[parity, :, columns])
-                acc_ref[parity, :, columns] += first[:ROWS] + first[ROWS:] + second
+                acc_ref[block, parity, :, columns] += first[:ROWS] + first[ROWS:] + second
 
             return [
                 functools.partial(part, parity, slice(at, at + KTILE))
@@ -222,12 +221,17 @@
         lax.fori_loop(lowest // (2 * CHUNK), chunks // 2, two_chunks, start_state(start_ref, block))
         for part in add_products(chunks - 1, high_b, low_b):
             part()
-        both = acc_ref[...].reshape(2 * ROWS, HALF)
-        high, low = split_two(both)
-        moved = dot(jnp.concatenate([high, low], 0), fold_ref[...])
-        moved = moved[: 2 * ROWS] + moved[2 * ROWS :]
-        sign = jnp.tile(1.0 - 2.0 * (column % 2).astype(F32), (CHAN, 1))
-        even, odd = moved[:ROWS], moved[ROWS:]
+        return unused
+
+    lax.fori_loop(0, blocks, one_block, 0)
+    high, low = split_two(acc_ref[...].reshape(blocks * 2 * ROWS, HALF))
+    moved = dot(jnp.concatenate([high, low], 0), fold_ref[...])
+    moved = moved[: blocks * 2 * ROWS] + moved[blocks * 2 * ROWS :]
+    for block in range(blocks):
+        orders = block_orders(slots_ref, block * BLK)[0][:, :1]
+        sign = jnp.tile(1.0 - 2.0 * (orders % 2).astype(F32), (CHAN, 1))
+        even = moved[block * 2 * ROWS : block * 2 * ROWS + ROWS]
+        odd = moved[block * 2 * ROWS + ROWS : (block + 1) * 2 * ROWS]
         values = jnp.where(south, sign * (even - odd), even + odd)
         for d in range(bands):
             parts = []
@@ -241,37 +245,27 @@
                 parts.append(jnp.zeros((BLK, tiles * LANES - CHAN * row_count), F32))
             joined = jnp.concatenate(parts, 1)
             for t in range(tiles):
-                at = pl.ds(pl.multiple_of(t * blocks * BLK + block * BLK, BLK), BLK)
+                at = slice((t * blocks + block) * BLK, (t * blocks + block + 1) * BLK)
                 out_ref[d, at, :] = joined[:, t * LANES : (t + 1) * LANES]
-        return unused
-
-    lax.fori_loop(0, blocks, one_block, 0)
 
 
 def table_kernel(
-    dims, slots_ref, scalars_ref, rows_ref, out_ref, within_out, start_ref, before_ref,
-    first_ref, second_ref, sems,
+    blocks, slots_ref, scalars_ref, rows_ref, out_ref, within_out, start_ref, before_ref,
+    chunk_ref, sems,
 ):
-    modes, blocks = dims
-    base = lax.axis_index("band") * modes
+    modes = blocks * BLK
     cosine = jnp.broadcast_to(2.0 * rows_ref[0:1, :], (BLK, HALF))
-    recursion_tables(slots_ref, base, modes, rows_ref, start_ref, before_ref, within_out)
-    buffers = (first_ref, second_ref)
-
-    def copy_out(which, block, step):
-        return pltpu.make_async_copy(buffers[which], out_ref.at[block, step], sems.at[which])
+    recursion_tables(slots_ref, modes, rows_ref, start_ref, before_ref, within_out)
+
+    def copy_out(block, step):
+        return pltpu.make_async_copy(
+            chunk_ref.at[block, step], out_ref.at[block, step], sems.at[block, step]
+        )
 
     def one_block(block, unused):
-        orders, lowest = block_orders(slots_ref, base + block * BLK)
-        start = lowest // (2 * CHUNK)
-
-        def recur(which, step, carry, pending):
-            buffer = buffers[which]
-
-            @pl.when(pending)
-            def _():
-                copy_out(which, block, step).wait()
-
+        orders, lowest = block_orders(slots_ref, block * BLK)
+
+        def one_chunk(step, carry):
             held = {}
 
             def emit(i, value):
@@ -281,33 +275,36 @@
                     pair = jnp.concatenate([held.pop(i - 1), value], 0)
                     high, low = split_two(pair)
                     at = (i // 2) * 2 * BLK
-                    buffer[at : at + 2 * BLK, :] = high
-                    buffer[CHUNK * BLK + at : CHUNK * BLK + at + 2 * BLK, :] = low
+                    chunk_ref[block, step, at : at + 2 * BLK, :HALF] = high
+                    chunk_ref[block, step, at : at + 2 * BLK, HALF:] = low
 
             before = before_tile(before_ref, block, step)
             carry = run_chunk(step, carry, cosine, orders, before, scalars_ref, emit, ())
-            copy_out(which, block, step).start()
+            copy_out(block, step).start()
             return carry
 
-        def two_chunks(pair, carry):
-            pending = (block > 0) | (pair > start)
-            carry = recur(0, 2 * pair, carry, pending)
-            return recur(1, 2 * pair + 1, carry, pending)
-
-        lax.fori_loop(start, DEG // CHUNK // 2, two_chunks, start_state(start_ref, block))
+        first = lowest // (2 * CHUNK) * 2
+        lax.fori_loop(first, DEG // CHUNK, one_chunk, start_state(start_ref, block))
         return unused
 
+    def finish_block(block, unused):
+        orders, lowest = block_orders(slots_ref, block * BLK)
+
+        def finish_chunk(step, inner):
+            copy_out(block, step).wait()
+            return inner
+
+        return lax.fori_loop(lowest // (2 * CHUNK) * 2, DEG // CHUNK, finish_chunk, unused)
+
     lax.fori_loop(0, blocks, one_block, 0)
-    copy_out(0, 0, 0).wait()
-    copy_out(1, 0, 0).wait()
+    lax.fori_loop(0, blocks, finish_block, 0)
 
 
 def analyze_kernel(
-    dims, total_row, slots_ref, place_ref, data_ref, latitude_ref, within_ref, table_ref, out_ref,
-    chunk_ref, weight_ref, result_ref, fold_ref, coeff_ref, sems,
+    dims, total_row, slots_ref, data_ref, column_ref, latitude_ref, within_ref, table_ref,
+    out_ref, chunk_ref, weight_ref, stack_ref, result_ref, fold_ref, coeff_ref, sems,
 ):
     bands, row_count, modes, blocks, tiles = dims
-    base = lax.axis_index("band") * modes
     chunks = DEG // CHUNK
 
     def copy_in(block, step):
@@ -316,7 +313,7 @@
         )
 
     def start_block(block, unused):
-        orders, lowest = block_orders(slots_ref, base + block * BLK)
+        orders, lowest = block_orders(slots_ref, block * BLK)
 
         def start_chunk(step, inner):
             copy_in(block, step).start()
@@ -325,8 +322,41 @@
         return lax.fori_loop(lowest // (2 * CHUNK) * 2, chunks, start_chunk, unused)
 
     lax.fori_loop(0, blocks, start_block, 0)
-    fold_matrix(latitude_ref, fold_ref)
+    latitude = column_ref[...]
+    north = jnp.where(latitude < HALF, latitude, NLAT - 1 - latitude)
+    lane = lax.broadcasted_iota(jnp.int32, (NLAT, LANES), 1)
+    for t in range(HALF // LANES):
+        one_hot = jnp.where(north == lane + t * LANES, 1.0, 0.0).astype(BF)
+        fold_ref[:, t * LANES : (t + 1) * LANES] = one_hot
     south = latitude_ref[...] >= HALF
+    for block in range(blocks):
+        orders = block_orders(slots_ref, block * BLK)[0][:, :1]
+        sign = 1.0 - 2.0 * (orders % 2).astype(F32)
+        evens, odds = [], []
+        for c in range(CHAN):
+            offset = ((c % 2) * FIELDS + c // 2) * row_count
+            t, at = offset // LANES, offset % LANES
+            rows = slice((t * blocks + block) * BLK, (t * blocks + block + 1) * BLK)
+            values = jnp.concatenate(
+                [data_ref[d, rows, :][:, at : at + row_count] for d in range(bands)], 1
+            )
+            flipped = sign * values
+            evens.append(jnp.where(south, flipped, values))
+            odds.append(jnp.where(south, -flipped, values))
+        high, low = split_two(jnp.concatenate(evens + odds, 0))
+        stack_ref[block * 4 * ROWS : block * 4 * ROWS + 2 * ROWS, :] = high
+        stack_ref[block * 4 * ROWS + 2 * ROWS : (block + 1) * 4 * ROWS, :] = low
+    folded = dot(stack_ref[...], fold_ref[...])
+    for block in range(blocks):
+        at = block * 4 * ROWS
+        part = folded[at : at + 2 * ROWS] + folded[at + 2 * ROWS : at + 4 * ROWS]
+        part = jnp.concatenate([part, jnp.zeros((LANES - 2 * ROWS, HALF), F32)], 0)
+        high, low = split_two(part.T)
+        weight_ref[block, :HALF, :LANES] = high
+        weight_ref[block, :HALF, LANES:] = low
+        weight_ref[block, HALF:, :LANES] = high
+        weight_ref[block, HALF:, LANES:] = jnp.zeros_like(low)
+
     total = data_ref[0, total_row : total_row + 8]
     for d in range(1, bands):
         total = total + data_ref[d, total_row : total_row + 8]
@@ -336,41 +366,23 @@
     keep = (lane % BLK == sub % BLK) & (lane // ROWS == sub // BLK % 2)
 
     def one_block(block, unused):
-        orders, lowest = block_orders(slots_ref, base + block * BLK)
+        orders, lowest = block_orders(slots_ref, block * BLK)
         orders = orders[:, :1]
         here = pl.ds(pl.multiple_of(block * BLK, BLK), BLK)
-        sign = 1.0 - 2.0 * (orders % 2).astype(F32)
-        evens, odds = [], []
-        for c in range(CHAN):
-            offset = ((c % 2) * FIELDS + c // 2) * row_count
-            t, at = offset // LANES, offset % LANES
-            rows = pl.ds(pl.multiple_of(t * blocks * BLK + block * BLK, BLK), BLK)
-            values = jnp.concatenate(
-                [data_ref[d, rows, :][:, at : at + row_count] for d in range(bands)], 1
-            )
-            flipped = sign * values
-            evens.append(jnp.where(south, flipped, values))
-            odds.append(jnp.where(south, -flipped, values))
-        high, low = split_two(jnp.concatenate(evens + odds, 0))
-        folded = dot(jnp.concatenate([high, low], 0), fold_ref[...], 1)
-        folded = folded[: 2 * ROWS] + folded[2 * ROWS :]
-        padded = jnp.concatenate([folded, jnp.zeros((LANES - 2 * ROWS, HALF), F32)], 0)
-        high, low = split_two(padded.T)
-        weight_ref[:, :LANES] = high
-        weight_ref[:, LANES:] = low
         result_ref[...] = jnp.zeros_like(result_ref)
 
-        def one_chunk(step, inner):
-            copy_in(block, step).wait()
-            first = dot(chunk_ref[block, step, : CHUNK * BLK], weight_ref[...])
-            second = dot(chunk_ref[block, step, CHUNK * BLK :], weight_ref[:, :LANES])
-            full = first[:, :LANES] + first[:, LANES:] + second
-            picked = jnp.where(keep, full, 0.0).reshape(CHUNK, BLK, LANES)
-            to = pl.ds(pl.multiple_of(step * CHUNK, CHUNK), CHUNK)
-            result_ref[to, :] = jnp.sum(picked, axis=1)
+        def two_chunks(pair, inner):
+            for step in (2 * pair, 2 * pair + 1):
+                copy_in(block, step).wait()
+            for step in (2 * pair, 2 * pair + 1):
+                full = dot(chunk_ref[block, step], weight_ref[block])
+                full = full[:, :LANES] + full[:, LANES:]
+                picked = jnp.where(keep, full, 0.0).reshape(CHUNK, BLK, LANES)
+                to = pl.ds(pl.multiple_of(step * CHUNK, CHUNK), CHUNK)
+                result_ref[to, :] = jnp.sum(picked, axis=1)
             return inner
 
-        lax.fori_loop(lowest // (2 * CHUNK) * 2, chunks, one_chunk, 0)
+        lax.fori_loop(lowest // (2 * CHUNK), chunks // 2, two_chunks, 0)
         turned = result_ref[...].T
         turned = turned[:ROWS] + turned[ROWS : 2 * ROWS]
         degree = lax.broadcasted_iota(jnp.int32, (BLK, DEG), 1)
@@ -381,7 +393,7 @@
                 part = part * inverse
             coeff_ref[c] = part
         for i in range(BLK):
-            target = pl.ds(place_ref[base + block * BLK + i], 1)
+            target = pl.ds(slots_ref[modes + block * BLK + i], 1)
             out_ref[:, target, :] = coeff_ref[:, i : i + 1, :]
         return unused
 
@@ -409,8 +421,9 @@
     return cos_out, sin_out
 
 
-def trig_kernel(high_ref, low_ref, cos_ref, sin_ref):
-    half = cos_ref.shape[0]
+def trig_kernel(out_ref, trig_ref, sem):
+    half = trig_ref.shape[2] // 2
+    high_ref, low_ref = trig_ref.at[0], trig_ref.at[1]
     root = math.sqrt(0.5)
     for parity in range(2):
 
@@ -441,17 +454,23 @@
             return unused
 
         lax.fori_loop(0, half // 64, strip, 0)
+    copy = pltpu.make_async_copy(trig_ref, out_ref, sem)
+    copy.start()
+    copy.wait()
 
 
 def grid_kernel(
-    dims, data_ref, orders_ref, rate_ref, sine_ref, trig_high, trig_low, out_ref,
-    move_ref, lhs_ref, weight_ref, acc_ref,
+    dims, data_ref, orders_ref, rate_ref, sine_ref, trig_in, out_ref,
+    move_ref, lhs_ref, weight_ref, acc_ref, trig_ref, sem,
 ):
     bands, row_count, modes, tiles, slots = dims
     half = slots // 2
     group = FIELDS * row_count
     padded = weight_ref.shape[1] // 2
 
+    copy = pltpu.make_async_copy(trig_in, trig_ref, sem)
+    copy.start()
+    trig_high, trig_low = trig_ref.at[0], trig_ref.at[1]
     order = orders_ref[...]
     natural = (order & 1) * half + (order >> 1)
     for t in range(slots // LANES):
@@ -473,6 +492,7 @@
     flux_scale = math.pi / (2.0 * NLAT * NLON * DEG)
     weight = jnp.tile(sine_ref[...], (1, KTILE // LANES))
     total = jnp.zeros((8, KTILE), F32)
+    copy.wait()
 
     for k in range(0, NLON // 2, KTILE):
         tile = slice(k, k + KTILE)
@@ -544,12 +564,19 @@
     chunks = DEG // CHUNK
     tiles = -(-CHAN * row_count // LANES)
     band_index = lax.axis_index("band")
-    table = slot_wavenumber.reshape(bands, modes)
-    rank = jnp.sum((table[:, None, :] < table[:, :, None]).astype(jnp.int32), 2)
-    match = rank[:, None, :] == jnp.arange(modes, dtype=jnp.int32)[None, :, None]
-    ordered = jnp.sum(jnp.where(match, table[:, None, :], 0), 2).reshape(slots)
-    place_row = jnp.arange(modes, dtype=jnp.int32)[None, None, :]
-    places = jnp.sum(jnp.where(match, place_row, 0), 2).reshape(slots)
+
+    def sort_rows(table):
+        rank = jnp.sum((table[:, None, :] < table[:, :, None]).astype(jnp.int32), 2)
+        match = rank[:, None, :] == jnp.arange(modes, dtype=jnp.int32)[None, :, None]
+        places = jnp.arange(modes, dtype=jnp.int32)[None, None, :]
+        return [
+            jnp.sum(jnp.where(match, values, 0), 2).reshape(-1)
+            for values in (table[:, None, :], places)
+        ]
+
+    own = lax.dynamic_slice_in_dim(slot_wavenumber, band_index * modes, modes)
+    local = jnp.concatenate(sort_rows(own.reshape(1, modes)))
+    ordered = sort_rows(slot_wavenumber.reshape(bands, modes))[0]
     rows = jnp.asarray(latitude_rows())
     spread = jnp.asarray(spread_matrix())
     latitude = row_latitude.reshape(1, NLAT)
@@ -566,28 +593,29 @@
     sent = pl.pallas_call(
         lambda *refs: synth_kernel(dims, *refs),
         out_shape=jax.ShapeDtypeStruct((bands, chunk_rows, LANES), F32),
-        in_specs=[SMEM, SMEM, SMEM, VMEM, VMEM, VMEM, VMEM],
+        in_specs=[SMEM, SMEM, VMEM, VMEM, VMEM, VMEM],
         out_specs=VMEM,
         scratch_shapes=[per_order] * 3
         + [pltpu.VMEM((chunks, 2 * ROWS, CHUNK * BLK), BF)]
         + [pltpu.VMEM((2, CHUNK // 2 * BLK, HALF), BF)] * 4
         + [
-            pltpu.VMEM((2, ROWS, HALF), F32),
+            pltpu.VMEM((blocks, 2, ROWS, HALF), F32),
             pltpu.VMEM((HALF, NLAT), BF),
             pltpu.VMEM((CHAN, BLK, DEG), F32),
         ],
         compiler_params=params,
         cost_estimate=work(15),
         name="synth",
-    )(ordered, places, scalars, coeffs, rows, spread, latitude)
+    )(local, scalars, coeffs, rows, spread, latitude)
     received = exchange(sent)
 
-    trig_shape = jax.ShapeDtypeStruct((2, slots, NLON // 2), BF)
-    trig_high, trig_low = pl.pallas_call(
+    trig_shape = (2, 2, slots, NLON // 2)
+    trig_scratch = [pltpu.VMEM(trig_shape, BF), pltpu.SemaphoreType.DMA(())]
+    trig = pl.pallas_call(
         trig_kernel,
-        out_shape=[trig_shape, trig_shape],
-        out_specs=[VMEM, VMEM],
-        scratch_shapes=[pltpu.VMEM((slots // 2, LANES), F32)] * 2,
+        out_shape=jax.ShapeDtypeStruct(trig_shape, BF),
+        out_specs=ANY,
+        scratch_shapes=trig_scratch,
         compiler_params=params,
         cost_estimate=work(4),
         name="trig",
@@ -603,23 +631,24 @@
     fluxes = pl.pallas_call(
         lambda *refs: grid_kernel(grid_dims, *refs),
         out_shape=jax.ShapeDtypeStruct((bands, chunk_rows + 8, LANES), F32),
-        in_specs=[VMEM] * 6,
+        in_specs=[VMEM] * 4 + [ANY],
         out_specs=VMEM,
         scratch_shapes=[
             pltpu.VMEM((slots, slots), BF),
             pltpu.VMEM((2, 2 * group, slots), BF),
             pltpu.VMEM((2, 2 * padded, KTILE), BF),
             pltpu.VMEM((2, slots, padded), F32),
-        ],
+        ]
+        + trig_scratch,
         compiler_params=params,
         cost_estimate=work(8),
         name="grid",
-    )(received, orders, capture_rate.reshape(row_count, NLON), row_sine, trig_high, trig_low)
+    )(received, orders, capture_rate.reshape(row_count, NLON), row_sine, trig)
     returned = exchange(fluxes)
 
-    chunk_shape = (blocks, chunks, 2 * CHUNK * BLK, HALF)
+    chunk_shape = (blocks, chunks, CHUNK * BLK, 2 * HALF)
     legendre, within = pl.pallas_call(
-        lambda *refs: table_kernel((modes, blocks), *refs),
+        lambda *refs: table_kernel(blocks, *refs),
         out_shape=[
             jax.ShapeDtypeStruct(chunk_shape, BF),
             jax.ShapeDtypeStruct((modes, DEG), F32),
@@ -627,29 +656,30 @@
         in_specs=[SMEM, SMEM, VMEM],
         out_specs=[ANY, VMEM],
         scratch_shapes=[per_order] * 2
-        + [pltpu.VMEM((2 * CHUNK * BLK, HALF), BF)] * 2
-        + [pltpu.SemaphoreType.DMA((2,))],
+        + [pltpu.VMEM(chunk_shape, BF), pltpu.SemaphoreType.DMA((blocks, chunks))],
         compiler_params=params,
         cost_estimate=work(12),
         name="table",
-    )(ordered, scalars, rows)
+    )(local, scalars, rows)
+    column = jnp.broadcast_to(row_latitude[:, None], (NLAT, LANES))
     result = pl.pallas_call(
         lambda *refs: analyze_kernel(dims, chunk_rows, *refs),
         out_shape=jax.ShapeDtypeStruct((CHAN, modes, DEG), F32),
-        in_specs=[SMEM, SMEM, VMEM, VMEM, VMEM, ANY],
+        in_specs=[SMEM, VMEM, VMEM, VMEM, VMEM, ANY],
         out_specs=VMEM,
         scratch_shapes=[
             pltpu.VMEM(chunk_shape, BF),
-            pltpu.VMEM((HALF, 2 * LANES), BF),
+            pltpu.VMEM((blocks, 2 * HALF, 2 * LANES), BF),
+            pltpu.VMEM((blocks * 4 * ROWS, NLAT), BF),
             pltpu.VMEM((DEG, LANES), F32),
-            pltpu.VMEM((HALF, NLAT), BF),
+            pltpu.VMEM((NLAT, HALF), BF),
             pltpu.VMEM((CHAN, BLK, DEG), F32),
             pltpu.SemaphoreType.DMA((blocks, chunks)),
         ],
         compiler_params=params,
         cost_estimate=work(9),
         name="analyze",
-    )(ordered, places, returned, latitude, within, legendre)
+    )(local, returned, column, latitude, within, legendre)
     return result.reshape(1, FIELDS, 2, modes, DEG)
 
 

time: 101 us -> 96.9 us (0.959)
  Pallas kernels: 62.1 us -> 48.3 us
  waiting for transfers between devices: 15.9 us -> 22.9 us
  starting transfers between devices: 12.3 us -> 15.9 us
  local copies, waits for them, and re-layouts: 9.4 us -> 7.35 us
    pallas_call x2, Pallas kernels: 20.8 us -> 13.5 us  [the longest x1 10.7 us: per_device(): pl.pallas_call(lambda *refs: table_kernel(blocks, *refs), out_shape=[jax....]
    all_to_all x2, waiting for transfers between devices: 15.9 us -> 22.9 us  [exchange(): lax.all_to_all(value, 'band', split_axis=0, concat_axis=0, tiled=True)]
    pallas_call x1, Pallas kernels: 16.2 us -> 11.6 us  [per_device(): pl.pallas_call(lambda *refs: analyze_kernel(dims, chunk_rows, *refs), out...]
    all_to_all x2, starting transfers between devices: 12.3 us -> 15.9 us  [exchange(): lax.all_to_all(value, 'band', split_axis=0, concat_axis=0, tiled=True)]
    pallas_call x1, Pallas kernels: 17.4 us -> 15.1 us  [per_device(): pl.pallas_call(lambda *refs: synth_kernel(dims, *refs), out_shape=jax.Sha...]
    unnamed x24 -> x22, local copies, waits for them, and re-layouts: 8.29 us -> 5.99 us
  transfers between devices with their start and end apart: 2 -> 2, of which waited for: 2 -> 2; matrix products, arithmetic and copies ran while one was open for 0% -> 1% of each run, Pallas kernels for 21% -> 14%
where the time goes in v4:
time: 96.9 us; the launch traced here: 95.9 us
  Pallas kernels  48.3 us (50%)
  waiting for transfers between devices  22.9 us (24%)
  starting transfers between devices  15.9 us (16%)
  local copies, waits for them, and re-layouts  7.35 us (8%)
  other arithmetic  1.3 us (1%)
    all_to_all x2, waiting for transfers between devices, exchange(): lax.all_to_all(value, 'band', split_axis=0, concat_axis=0, tiled=True)  22.9 us
    all_to_all x2, starting transfers between devices, exchange(): lax.all_to_all(value, 'band', split_axis=0, concat_axis=0, tiled=True)  15.9 us
    pallas_call x1, Pallas kernels, per_device(): pl.pallas_call(lambda *refs: synth_kernel(dims, *refs), out_shape=jax.Sha...  15.1 us
    pallas_call x1, Pallas kernels, per_device(): pl.pallas_call(lambda *refs: analyze_kernel(dims, chunk_rows, *refs), out...  11.6 us
    pallas_call x1, Pallas kernels, per_device(): pl.pallas_call(lambda *refs: table_kernel(blocks, *refs), out_shape=[jax....  10.7 us
    pallas_call x1, Pallas kernels, per_device(): pl.pallas_call(lambda *refs: grid_kernel(grid_dims, *refs), out_shape=jax...  8.13 us
    unnamed x22, local copies, waits for them, and re-layouts  5.99 us
    pallas_call x1, Pallas kernels, per_device(): pl.pallas_call(trig_kernel, out_shape=jax.ShapeDtypeStruct(trig_shape, BF...  2.88 us
  transfers between devices with their start and end apart: 2, of which 2 were waited for; matrix products, arithmetic and copies ran while one was open for 1% of the time, Pallas kernels for 14%

profile of v4, /device:TPU:0, one launch (start us, length us, event | category | flops | bytes accessed | tf_op | source)
XLA Modules:
  0.0 95.9 jit_solution(6232866974181280371)
XLA Ops:
  0.0 0.8 dynamic_slice.6
  0.8 0.2 convert_reduce_fusion.1
  1.0 0.1 select_reduce_fusion.2
  1.1 0.1 pad_add_fusion.refs_0_
  1.2 0.7 copy-done
  1.9 1.0 %copy-done.3 = f32[1,3,2,32,512]{4,3,2,1,0:T(8,128)S(1)} copy-done((f32[1,3,2,32,512]{4,3,2,1,0:T(8,128)S(1)}, f32[1,3,2,32,512]{4,3,2,1,0:T(8,128)}, u32[]{:S(2)}) %copy-start.3) | copy-done | bytes 393240
  2.9 0.9 copy-done.4
  3.9 0.7 copy-done.5
  4.6 0.7 copy-done.7
  5.3 15.1 %synth.1 = f32[16,96,128]{2,1,0:T(8,128)} custom-call(s32[64]{0:T(128)S(1)} %pad_add_fusion.refs_0_, f32[1024]{0:T(1024)S(1)} %copy-done.7, f32[6,32,512]{2,1,0:T(8,128)S(1)} %bitcast.7, f32[8,512]{1,0:T(8,128)S(1)} %copy-done.5, bf16[128,1024]{1,0:T(8,128)(2,1)S(1)} %copy-done.4, s32[1,1024]{1,0:T(1,128)S(1)} %bitcast.4), custom_call_target="tpu_custom_call" | custom-call | flops 15000000512 | bytes 1048576 | tf_op jit(solution)/shard_map/synth/pallas_call | solution.py:593
  20.3 11.0 %all-to-all-start = ((f32[16,96,128]{2,1,0:T(8,128)}), f32[16,96,128]{2,1,0:T(8,128)S(1)}, u32[]{:S(2)}, u32[]{:S(2)}) async-start(f32[16,96,128]{2,1,0:T(8,128)} %synth.1), calls=%async_computation | async-start | bytes 1572864 | tf_op jit(solution)/shard_map/all_to_all | solution.py:591
  31.3 0.0 copy-done.10
  31.3 0.1 lt.46
  31.4 0.5 convert_reduce_fusion
  31.9 0.3 select_reduce_fusion
  32.2 0.1 broadcast_in_dim.53
  32.3 0.0 copy-done.1
  32.3 0.1 multiply_sine_fusion
  32.4 2.9 %trig.1.refs_4_ = bf16[2,2,512,1024]{3,2,1,0:T(8,128)(2,1)S(1)} custom-call(), custom_call_target="tpu_custom_call" | custom-call | flops 4000000000 | bytes 1048576 | tf_op jit(solution)/shard_map/trig/pallas_call | solution.py:614
  35.3 0.0 copy-start.9
  35.3 1.9 %copy-done.9 = bf16[2,2,512,1024]{3,2,1,0:T(8,128)(2,1)} copy-done((bf16[2,2,512,1024]{3,2,1,0:T(8,128)(2,1)}, bf16[2,2,512,1024]{3,2,1,0:T(8,128)(2,1)S(1)}, u32[]{:S(2)}) %copy-start.9) | copy-done | bytes 4194328
  37.2 13.8 %all-to-all-done.refs_0_ = f32[16,96,128]{2,1,0:T(8,128)S(1)} async-done(((f32[16,96,128]{2,1,0:T(8,128)}), f32[16,96,128]{2,1,0:T(8,128)S(1)}, u32[]{:S(2)}, u32[]{:S(2)}) %all-to-all-start) | async-done | bytes 786464 | tf_op jit(solution)/shard_map/all_to_all | solution.py:591
  51.1 0.1 broadcast_in_dim.55.refs_3_
  51.1 0.1 broadcast_in_dim.54.refs_1_
  51.3 0.0 copy-done.2
  51.3 8.1 %grid.1 = f32[16,104,128]{2,1,0:T(8,128)} custom-call(f32[16,96,128]{2,1,0:T(8,128)S(1)} %all-to-all-done.refs_0_, s32[512,128]{1,0:T(8,128)S(1)} %broadcast_in_dim.54.refs_1_, f32[64,2048]{1,0:T(8,128)S(1)} %bitcast.6, f32[64,128]{1,0:T(8,128)S(1)} %broadcast_in_dim.55.refs_3_, bf16[2,2,512,1024]{3,2,1,0:T(8,128)(2,1)} %copy-done.9), custom_call_target="tpu_custom_call" | custom-call | flops 8000000000 | bytes 1048576 | tf_op jit(solution)/shard_map/grid/pallas_call | solution.py:631
  59.4 4.9 %all-to-all-start.1 = ((f32[16,104,128]{2,1,0:T(8,128)}), f32[16,104,128]{2,1,0:T(8,128)S(1)}, u32[]{:S(2)}, u32[]{:S(2)}) async-start(f32[16,104,128]{2,1,0:T(8,128)} %grid.1), calls=%async_computation.1 | async-start | bytes 1703936 | tf_op jit(solution)/shard_map/all_to_all | solution.py:591
  64.3 0.0 copy-done.6
  64.3 10.7 %table.1 = (bf16[4,8,512,1024]{3,2,1,0:T(8,128)(2,1)}, f32[32,512]{1,0:T(8,128)S(1)}) custom-call(s32[64]{0:T(128)S(1)} %pad_add_fusion.refs_0_, f32[1024]{0:T(1024)S(1)} %copy-done.8, f32[8,512]{1,0:T(8,128)S(1)} %copy-done.6), custom_call_target="tpu_custom_call" | custom-call | flops 12000000000 | bytes 1048576 | tf_op jit(solution)/shard_map/table/pallas_call | solution.py:650
  75.0 9.1 %all-to-all-done.1.refs_1_ = f32[16,104,128]{2,1,0:T(8,128)S(1)} async-done(((f32[16,104,128]{2,1,0:T(8,128)}), f32[16,104,128]{2,1,0:T(8,128)S(1)}, u32[]{:S(2)}, u32[]{:S(2)}) %all-to-all-start.1) | async-done | bytes 852000 | tf_op jit(solution)/shard_map/all_to_all | solution.py:591
  84.1 0.2 broadcast_in_dim.56.refs_2_
  84.3 11.6 %analyze.1 = f32[6,32,512]{2,1,0:T(8,128)} custom-call(s32[64]{0:T(128)S(1)} %pad_add_fusion.refs_0_, f32[16,104,128]{2,1,0:T(8,128)S(1)} %all-to-all-done.1.refs_1_, s32[1024,128]{1,0:T(8,128)S(1)} %broadcast_in_dim.56.refs_2_, s32[1,1024]{1,0:T(1,128)S(1)} %bitcast.5, f32[32,512]{1,0:T(8,128)S(1)} %get-tuple-element.7.refs_4_, ...), custom_call_target="tpu_custom_call" | custom-call | flops 8999999488 | bytes 1048576 | tf_op jit(solution)/shard_map/analyze/pallas_call | solution.py:665
  (11 shorter events, 0.0 us)
Async XLA Ops:
  0.0 31.3 %copy-start.10 = (s32[512]{0:T(512)S(1)}, s32[512]{0:T(512)}, u32[]{:S(2)}) copy-start(s32[512]{0:T(512)} %param.10) | copy-start | bytes 6148
  0.0 32.3 %copy-start.1 = (s32[1024]{0:T(1024)S(1)}, s32[1024]{0:T(1024)}, u32[]{:S(2)}) copy-start(s32[1024]{0:T(1024)} %param.9) | copy-start | bytes 12292
  1.2 0.7 copy-start
  1.9 1.0 %copy-start.3 = (f32[1,3,2,32,512]{4,3,2,1,0:T(8,128)S(1)}, f32[1,3,2,32,512]{4,3,2,1,0:T(8,128)}, u32[]{:S(2)}) copy-start(f32[1,3,2,32,512]{4,3,2,1,0:T(8,128)} %param.7) | copy-start | bytes 1179652
  2.9 0.9 copy-start.4
  3.8 0.7 copy-start.5
  4.6 0.7 copy-start.7
  5.3 46.0 %copy-start.2 = (f32[1,64,2048]{2,1,0:T(8,128)S(1)}, f32[1,64,2048]{2,1,0:T(8,128)}, u32[]{:S(2)}) copy-start(f32[1,64,2048]{2,1,0:T(8,128)} %param.8) | copy-start | bytes 1572868
  20.3 44.0 %copy-start.6 = (f32[8,512]{1,0:T(8,128)S(1)}, f32[8,512]{1,0:T(8,128)}, u32[]{:S(2)}) copy-start(f32[8,512]{1,0:T(8,128)} %constant.29.clone.refs_3_.refs_2_) | copy-start | bytes 49156
  20.3 44.0 %copy-start.8 = (f32[1024]{0:T(1024)S(1)}, f32[1024]{0:T(1024)}, u32[]{:S(2)}) copy-start(f32[1024]{0:T(1024)} %constant.31.clone.refs_1_) | copy-start | bytes 12292
  20.3 30.7 %all-to-all-start = ((f32[16,96,128]{2,1,0:T(8,128)}), f32[16,96,128]{2,1,0:T(8,128)S(1)}, u32[]{:S(2)}, u32[]{:S(2)}) async-start(f32[16,96,128]{2,1,0:T(8,128)} %synth.1), calls=%async_computation | async-start | bytes 1572864 | tf_op jit(solution)/shard_map/all_to_all | solution.py:591
  35.3 1.9 %copy-start.9 = (bf16[2,2,512,1024]{3,2,1,0:T(8,128)(2,1)}, bf16[2,2,512,1024]{3,2,1,0:T(8,128)(2,1)S(1)}, u32[]{:S(2)}) copy-start(bf16[2,2,512,1024]{3,2,1,0:T(8,128)(2,1)S(1)} %trig.1.refs_4_) | copy-start | bytes 12582916
  59.4 24.7 %all-to-all-start.1 = ((f32[16,104,128]{2,1,0:T(8,128)}), f32[16,104,128]{2,1,0:T(8,128)S(1)}, u32[]{:S(2)}, u32[]{:S(2)}) async-start(f32[16,104,128]{2,1,0:T(8,128)} %grid.1), calls=%async_computation.1 | async-start | bytes 1703936 | tf_op jit(solution)/shard_map/all_to_all | solution.py:591

commit v5 on v4

--- a/solution.py
+++ b/solution.py
@@ -65,12 +65,12 @@
 def block_orders(slots_ref, first):
     sublane = lax.broadcasted_iota(jnp.int32, (BLK, LANES), 0)
     orders = jnp.zeros((BLK, LANES), jnp.int32)
-    lowest = jnp.int32(DEG)
+    lowest, highest = jnp.int32(DEG), jnp.int32(0)
     for i in range(BLK):
         order = slots_ref[first + i]
         orders = jnp.where(sublane == i, order, orders)
-        lowest = jnp.minimum(lowest, order)
-    return orders, lowest
+        lowest, highest = jnp.minimum(lowest, order), jnp.maximum(highest, order)
+    return orders, lowest // CHUNK, highest // CHUNK + 1
 
 
 def running_sum(terms, length):
@@ -100,7 +100,7 @@
     start_ref[...] = norm + order * rows_ref[1:2, :]
 
 
-def run_chunk(step, carry, double_cosine, orders, before, scalars_ref, emit, beside):
+def run_chunk(step, carry, double_cosine, orders, before, scalars_ref, emit, beside, guard):
     current, previous, log_scale = carry
     order = orders.astype(F32)
     order_square = order * order
@@ -119,8 +119,10 @@
         degree = step * CHUNK + i
         factor = (scalars_ref[degree] - order_square) * scalars_ref[DEG + degree]
         factor = jnp.tile(factor, (1, HALF // LANES))
-        started = jnp.tile(orders, (1, HALF // LANES)) < degree
-        newest = jnp.where(started, double_cosine * current - factor * previous, 1.0)
+        newest = double_cosine * current - factor * previous
+        if guard:
+            started = jnp.tile(orders, (1, HALF // LANES)) < degree
+            newest = jnp.where(started, newest, 1.0)
         current, previous = newest, current
         emit(i, newest * scale)
         if beside and i % (CHUNK // len(beside)) == 1:
@@ -146,10 +148,21 @@
 
 
 def synth_kernel(
-    dims, slots_ref, scalars_ref, spec_ref, rows_ref, spread_ref, latitude_ref,
-    out_ref, start_ref, before_ref, within_ref, lhs_ref, high_a, low_a, high_b, low_b, acc_ref, fold_ref, coeff_ref,
+    dims, slots_ref, scalars_in, spec_in, rows_in, spread_in, latitude_in,
+    out_ref, scalars_ref, spec_ref, rows_ref, spread_ref, latitude_ref, sems,
+    start_ref, before_ref, within_ref, lhs_ref, high_a, low_a, high_b, low_b, acc_ref, fold_ref, coeff_ref,
 ):
     bands, row_count, modes, blocks, tiles = dims
+    pairs = (
+        (rows_in, rows_ref), (scalars_in, scalars_ref), (latitude_in, latitude_ref),
+        (spread_in, spread_ref), (spec_in, spec_ref),
+    )
+    copies = []
+    for index, (source, target) in enumerate(pairs):
+        copies.append(pltpu.make_async_copy(source, target, sems.at[index]))
+        copies[-1].start()
+    for copy in copies:
+        copy.wait()
     fold_matrix(latitude_ref, fold_ref)
     recursion_tables(slots_ref, modes, rows_ref, start_ref, before_ref, within_ref)
     south = latitude_ref[...] >= HALF
@@ -160,7 +173,7 @@
     width = (CHUNK // 2) * BLK
 
     def one_block(block, unused):
-        orders, lowest = block_orders(slots_ref, block * BLK)
+        orders, first, last = block_orders(slots_ref, block * BLK)
         column = orders[:, :1]
         here = pl.ds(pl.multiple_of(block * BLK, BLK), BLK)
         for i in range(BLK):
@@ -179,7 +192,7 @@
         acc_ref[block] = jnp.zeros((2, ROWS, HALF), F32)
         cosine = jnp.broadcast_to(2.0 * rows_ref[0:1, :], (BLK, HALF))
 
-        def recur(step, carry, high_ref, low_ref, beside):
+        def recur(step, carry, high_ref, low_ref, beside, guard):
             held = {}
 
             def emit(i, value):
@@ -193,7 +206,9 @@
                     low_ref[i % 2, at : at + 2 * BLK, :] = low
 
             before = before_tile(before_ref, block, step)
-            return run_chunk(step, carry, cosine, orders, before, scalars_ref, emit, beside)
+            return run_chunk(
+                step, carry, cosine, orders, before, scalars_ref, emit, beside, guard
+            )
 
         def add_products(step, high_ref, low_ref):
             def part(parity, columns):
@@ -208,17 +223,27 @@
                 for at in range(0, HALF, KTILE)
             ]
 
-        def two_chunks(pair, carry):
+        def two_chunks(guard, pair, carry):
             step = 2 * pair
             beside = add_products(jnp.maximum(step - 1, 0), high_b, low_b)
-            carry = recur(step, carry, high_a, low_a, beside)
+            carry = recur(step, carry, high_a, low_a, beside, guard)
             beside = add_products(step, high_a, low_a)
-            return recur(step + 1, carry, high_b, low_b, beside)
+            return recur(step + 1, carry, high_b, low_b, beside, guard)
 
         high_b[...] = jnp.zeros_like(high_b)
         low_b[...] = jnp.zeros_like(low_b)
         chunks = DEG // CHUNK
-        lax.fori_loop(lowest // (2 * CHUNK), chunks // 2, two_chunks, start_state(start_ref, block))
+        state = lax.fori_loop(
+            0,
+            first & 1,
+            lambda unused, carry: recur(first, carry, high_b, low_b, (), True),
+            start_state(start_ref, block),
+        )
+        middle = (last + 1) // 2
+        state = lax.fori_loop(
+            (first + 1) // 2, middle, functools.partial(two_chunks, True), state
+        )
+        lax.fori_loop(middle, chunks // 2, functools.partial(two_chunks, False), state)
         for part in add_products(chunks - 1, high_b, low_b):
             part()
         return unused
@@ -263,9 +288,9 @@
         )
 
     def one_block(block, unused):
-        orders, lowest = block_orders(slots_ref, block * BLK)
-
-        def one_chunk(step, carry):
+        orders, first, last = block_orders(slots_ref, block * BLK)
+
+        def one_chunk(guard, step, carry):
             held = {}
 
             def emit(i, value):
@@ -279,22 +304,25 @@
                     chunk_ref[block, step, at : at + 2 * BLK, HALF:] = low
 
             before = before_tile(before_ref, block, step)
-            carry = run_chunk(step, carry, cosine, orders, before, scalars_ref, emit, ())
+            carry = run_chunk(
+                step, carry, cosine, orders, before, scalars_ref, emit, (), guard
+            )
             copy_out(block, step).start()
             return carry
 
-        first = lowest // (2 * CHUNK) * 2
-        lax.fori_loop(first, DEG // CHUNK, one_chunk, start_state(start_ref, block))
+        state = start_state(start_ref, block)
+        state = lax.fori_loop(first, last, functools.partial(one_chunk, True), state)
+        lax.fori_loop(last, DEG // CHUNK, functools.partial(one_chunk, False), state)
         return unused
 
     def finish_block(block, unused):
-        orders, lowest = block_orders(slots_ref, block * BLK)
+        orders, first, last = block_orders(slots_ref, block * BLK)
 
         def finish_chunk(step, inner):
             copy_out(block, step).wait()
             return inner
 
-        return lax.fori_loop(lowest // (2 * CHUNK) * 2, DEG // CHUNK, finish_chunk, unused)
+        return lax.fori_loop(first, DEG // CHUNK, finish_chunk, unused)
 
     lax.fori_loop(0, blocks, one_block, 0)
     lax.fori_loop(0, blocks, finish_block, 0)
@@ -313,13 +341,13 @@
         )
 
     def start_block(block, unused):
-        orders, lowest = block_orders(slots_ref, block * BLK)
+        orders, first, last = block_orders(slots_ref, block * BLK)
 
         def start_chunk(step, inner):
             copy_in(block, step).start()
             return inner
 
-        return lax.fori_loop(lowest // (2 * CHUNK) * 2, chunks, start_chunk, unused)
+        return lax.fori_loop(first, chunks, start_chunk, unused)
 
     lax.fori_loop(0, blocks, start_block, 0)
     latitude = column_ref[...]
@@ -366,15 +394,15 @@
     keep = (lane % BLK == sub % BLK) & (lane // ROWS == sub // BLK % 2)
 
     def one_block(block, unused):
-        orders, lowest = block_orders(slots_ref, block * BLK)
+        orders, first, last = block_orders(slots_ref, block * BLK)
         orders = orders[:, :1]
         here = pl.ds(pl.multiple_of(block * BLK, BLK), BLK)
         result_ref[...] = jnp.zeros_like(result_ref)
 
-        def two_chunks(pair, inner):
-            for step in (2 * pair, 2 * pair + 1):
+        def some_chunks(steps, inner):
+            for step in steps:
                 copy_in(block, step).wait()
-            for step in (2 * pair, 2 * pair + 1):
+            for step in steps:
                 full = dot(chunk_ref[block, step], weight_ref[block])
                 full = full[:, :LANES] + full[:, LANES:]
                 picked = jnp.where(keep, full, 0.0).reshape(CHUNK, BLK, LANES)
@@ -382,7 +410,13 @@
                 result_ref[to, :] = jnp.sum(picked, axis=1)
             return inner
 
-        lax.fori_loop(lowest // (2 * CHUNK), chunks // 2, two_chunks, 0)
+        lax.fori_loop(0, first & 1, lambda unused, inner: some_chunks((first,), inner), 0)
+        lax.fori_loop(
+            (first + 1) // 2,
+            chunks // 2,
+            lambda pair, inner: some_chunks((2 * pair, 2 * pair + 1), inner),
+            0,
+        )
         turned = result_ref[...].T
         turned = turned[:ROWS] + turned[ROWS : 2 * ROWS]
         degree = lax.broadcasted_iota(jnp.int32, (BLK, DEG), 1)
@@ -422,8 +456,7 @@
 
 
 def trig_kernel(out_ref, trig_ref, sem):
-    half = trig_ref.shape[2] // 2
-    high_ref, low_ref = trig_ref.at[0], trig_ref.at[1]
+    half = trig_ref.shape[3] // 2
     root = math.sqrt(0.5)
     for parity in range(2):
 
@@ -440,13 +473,11 @@
             for t in range(KTILE // LANES):
                 cosine, sine = base_trig(order, t * LANES)
                 for k in range(t * LANES, NLON // 2, KTILE):
-                    columns = slice(k, k + LANES)
-                    high, low = split_two(cosine)
-                    high_ref[parity, pl.ds(at, 64), columns] = high
-                    low_ref[parity, pl.ds(at, 64), columns] = low
-                    high, low = split_two(sine)
-                    high_ref[parity, pl.ds(half + at, 64), columns] = high
-                    low_ref[parity, pl.ds(half + at, 64), columns] = low
+                    columns = slice(t * LANES, (t + 1) * LANES)
+                    for values, start in ((cosine, at), (sine, half + at)):
+                        high, low = split_two(values)
+                        trig_ref[k // KTILE, 0, parity, pl.ds(start, 64), columns] = high
+                        trig_ref[k // KTILE, 1, parity, pl.ds(start, 64), columns] = low
                     cosine, sine = (
                         cosine * turn_cos - sine * turn_sin,
                         sine * turn_cos + cosine * turn_sin,
@@ -461,16 +492,18 @@
 
 def grid_kernel(
     dims, data_ref, orders_ref, rate_ref, sine_ref, trig_in, out_ref,
-    move_ref, lhs_ref, weight_ref, acc_ref, trig_ref, sem,
+    move_ref, lhs_ref, weight_ref, acc_ref, trig_ref, sems,
 ):
     bands, row_count, modes, tiles, slots = dims
     half = slots // 2
     group = FIELDS * row_count
     padded = weight_ref.shape[1] // 2
 
-    copy = pltpu.make_async_copy(trig_in, trig_ref, sem)
-    copy.start()
-    trig_high, trig_low = trig_ref.at[0], trig_ref.at[1]
+    copies = []
+    for tile in range(NLON // 2 // KTILE):
+        copy = pltpu.make_async_copy(trig_in.at[tile], trig_ref.at[tile], sems.at[tile])
+        copy.start()
+        copies.append(copy)
     order = orders_ref[...]
     natural = (order & 1) * half + (order >> 1)
     for t in range(slots // LANES):
@@ -492,14 +525,14 @@
     flux_scale = math.pi / (2.0 * NLAT * NLON * DEG)
     weight = jnp.tile(sine_ref[...], (1, KTILE // LANES))
     total = jnp.zeros((8, KTILE), F32)
-    copy.wait()
 
     for k in range(0, NLON // 2, KTILE):
-        tile = slice(k, k + KTILE)
+        copies[k // KTILE].wait()
+        trig_high, trig_low = trig_ref.at[k // KTILE, 0], trig_ref.at[k // KTILE, 1]
         sums = []
         for parity in range(2):
-            first = dot(lhs_ref[parity], trig_high[parity, :, tile])
-            second = dot(lhs_ref[parity, :group, :], trig_low[parity, :, tile])
+            first = dot(lhs_ref[parity], trig_high[parity])
+            second = dot(lhs_ref[parity, :group, :], trig_low[parity])
             sums.append(first[:group] + first[group:] + second)
         values = []
         for fields, at in ((sums[0] + sums[1], k), (sums[0] - sums[1], k + NLON // 2)):
@@ -521,8 +554,8 @@
             high, low = split_two(both)
             weight_ref[parity, :group, :] = high
             weight_ref[parity, padded : padded + group, :] = low
-            first = dot(trig_high[parity, :, tile], weight_ref[parity], 1)
-            second = dot(trig_low[parity, :, tile], weight_ref[parity, :padded, :], 1)
+            first = dot(trig_high[parity], weight_ref[parity], 1)
+            second = dot(trig_low[parity], weight_ref[parity, :padded, :], 1)
             part = first[:, :padded] + first[:, padded:] + second
             if k == 0:
                 acc_ref[parity] = part
@@ -546,7 +579,7 @@
 
 VMEM = pl.BlockSpec(memory_space=pltpu.VMEM)
 SMEM = pl.BlockSpec(memory_space=pltpu.SMEM)
-ANY = pl.BlockSpec(memory_space=pl.ANY)
+HBM = pl.BlockSpec(memory_space=pltpu.HBM)
 
 
 def work(microseconds):
@@ -593,9 +626,17 @@
     sent = pl.pallas_call(
         lambda *refs: synth_kernel(dims, *refs),
         out_shape=jax.ShapeDtypeStruct((bands, chunk_rows, LANES), F32),
-        in_specs=[SMEM, SMEM, VMEM, VMEM, VMEM, VMEM],
+        in_specs=[SMEM] + [HBM] * 5,
         out_specs=VMEM,
-        scratch_shapes=[per_order] * 3
+        scratch_shapes=[
+            pltpu.SMEM(scalars.shape, F32),
+            pltpu.VMEM(coeffs.shape, F32),
+            pltpu.VMEM(rows.shape, F32),
+            pltpu.VMEM(spread.shape, BF),
+            pltpu.VMEM(latitude.shape, jnp.int32),
+            pltpu.SemaphoreType.DMA((5,)),
+        ]
+        + [per_order] * 3
         + [pltpu.VMEM((chunks, 2 * ROWS, CHUNK * BLK), BF)]
         + [pltpu.VMEM((2, CHUNK // 2 * BLK, HALF), BF)] * 4
         + [
@@ -603,19 +644,20 @@
             pltpu.VMEM((HALF, NLAT), BF),
             pltpu.VMEM((CHAN, BLK, DEG), F32),
         ],
-        compiler_params=params,
+        compiler_params=pltpu.CompilerParams(vmem_limit_bytes=62 * 2**20),
         cost_estimate=work(15),
         name="synth",
     )(local, scalars, coeffs, rows, spread, latitude)
     received = exchange(sent)
 
-    trig_shape = (2, 2, slots, NLON // 2)
-    trig_scratch = [pltpu.VMEM(trig_shape, BF), pltpu.SemaphoreType.DMA(())]
+    trig_tiles = NLON // 2 // KTILE
+    trig_shape = (trig_tiles, 2, 2, slots, KTILE)
+    trig_scratch = pltpu.VMEM(trig_shape, BF)
     trig = pl.pallas_call(
         trig_kernel,
         out_shape=jax.ShapeDtypeStruct(trig_shape, BF),
-        out_specs=ANY,
-        scratch_shapes=trig_scratch,
+        out_specs=HBM,
+        scratch_shapes=[trig_scratch, pltpu.SemaphoreType.DMA(())],
         compiler_params=params,
         cost_estimate=work(4),
         name="trig",
@@ -631,15 +673,16 @@
     fluxes = pl.pallas_call(
         lambda *refs: grid_kernel(grid_dims, *refs),
         out_shape=jax.ShapeDtypeStruct((bands, chunk_rows + 8, LANES), F32),
-        in_specs=[VMEM] * 4 + [ANY],
+        in_specs=[VMEM] * 4 + [HBM],
         out_specs=VMEM,
         scratch_shapes=[
             pltpu.VMEM((slots, slots), BF),
             pltpu.VMEM((2, 2 * group, slots), BF),
             pltpu.VMEM((2, 2 * padded, KTILE), BF),
             pltpu.VMEM((2, slots, padded), F32),
-        ]
-        + trig_scratch,
+            trig_scratch,
+            pltpu.SemaphoreType.DMA((trig_tiles,)),
+        ],
         compiler_params=params,
         cost_estimate=work(8),
         name="grid",
@@ -654,7 +697,7 @@
             jax.ShapeDtypeStruct((modes, DEG), F32),
         ],
         in_specs=[SMEM, SMEM, VMEM],
-        out_specs=[ANY, VMEM],
+        out_specs=[HBM, VMEM],
         scratch_shapes=[per_order] * 2
         + [pltpu.VMEM(chunk_shape, BF), pltpu.SemaphoreType.DMA((blocks, chunks))],
         compiler_params=params,
@@ -665,7 +708,7 @@
     result = pl.pallas_call(
         lambda *refs: analyze_kernel(dims, chunk_rows, *refs),
         out_shape=jax.ShapeDtypeStruct((CHAN, modes, DEG), F32),
-        in_specs=[SMEM, VMEM, VMEM, VMEM, VMEM, ANY],
+        in_specs=[SMEM, VMEM, VMEM, VMEM, VMEM, HBM],
         out_specs=VMEM,
         scratch_shapes=[
             pltpu.VMEM(chunk_shape, BF),

time: 96.9 us -> 91.9 us (0.948)
  the two profiles are of different devices: /device:TPU:0 before, /device:TPU:8 now
where the time goes in v5:
time: 91.9 us; the launch traced here: 91.1 us
  Pallas kernels  51.5 us (56%)
  waiting for transfers between devices  23.1 us (25%)
  starting transfers between devices  11.1 us (12%)
  local copies, waits for them, and re-layouts  3.31 us (4%)
  other arithmetic  1.82 us (2%)
    all_to_all x2, waiting for transfers between devices, exchange(): lax.all_to_all(value, 'band', split_axis=0, concat_axis=0, tiled=True)  23.1 us
    pallas_call x1, Pallas kernels, per_device(): pl.pallas_call(lambda *refs: synth_kernel(dims, *refs), out_shape=jax.Sha...  17.2 us
    pallas_call x1, Pallas kernels, per_device(): pl.pallas_call(lambda *refs: analyze_kernel(dims, chunk_rows, *refs), out...  12.9 us
    pallas_call x1, Pallas kernels, per_device(): pl.pallas_call(lambda *refs: table_kernel(blocks, *refs), out_shape=[jax....  11.5 us
    all_to_all x2, starting transfers between devices, exchange(): lax.all_to_all(value, 'band', split_axis=0, concat_axis=0, tiled=True)  11.1 us
    pallas_call x1, Pallas kernels, per_device(): pl.pallas_call(lambda *refs: grid_kernel(grid_dims, *refs), out_shape=jax...  7.33 us
    pallas_call x1, Pallas kernels, per_device(): pl.pallas_call(trig_kernel, out_shape=jax.ShapeDtypeStruct(trig_shape, BF...  2.47 us
    unnamed x14, local copies, waits for them, and re-layouts  1.95 us
  transfers between devices with their start and end apart: 2, of which 2 were waited for; matrix products, arithmetic and copies ran while one was open for 1% of the time, Pallas kernels for 15%

profile of v5, /device:TPU:8, one launch (start us, length us, event | category | flops | bytes accessed | tf_op | source)
XLA Modules:
  0.0 91.1 jit_solution(5185162486577411829)
XLA Ops:
  0.0 0.8 dynamic_slice.6
  0.8 0.2 convert_reduce_fusion.1
  1.0 0.1 select_reduce_fusion.2
  1.1 0.6 pad_add_fusion.refs_0_
  1.7 17.2 %synth.1 = f32[16,96,128]{2,1,0:T(8,128)} custom-call(s32[64]{0:T(128)} %pad_add_fusion.refs_0_, f32[1024]{0:T(1024)} %constant.31.clone.refs_1_, f32[6,32,512]{2,1,0:T(8,128)} %bitcast.7, f32[8,512]{1,0:T(8,128)} %constant.29.clone.refs_3_.refs_2_, bf16[128,1024]{1,0:T(8,128)(2,1)} %constant.30.clone.refs_4_, s32[1,1024]{1,0:T(1,128)} %bitcast.4), custom_call_target="tpu_custom_call" | custom-call | flops 15000000512 | bytes 1048576 | tf_op jit(solution)/shard_map/synth/pallas_call | solution.py:626
  18.9 0.0 copy-start.1
  18.9 0.0 copy-start.3
  19.0 0.0 copy-start.4
  19.0 6.4 %all-to-all-start = ((f32[16,96,128]{2,1,0:T(8,128)}), f32[16,96,128]{2,1,0:T(8,128)S(1)}, u32[]{:S(2)}, u32[]{:S(2)}) async-start(f32[16,96,128]{2,1,0:T(8,128)} %synth.1), calls=%async_computation | async-start | bytes 1572864 | tf_op jit(solution)/shard_map/all_to_all | solution.py:624
  25.4 0.0 copy-done.6
  25.4 0.1 lt.46
  25.5 0.5 convert_reduce_fusion
  25.9 0.3 select_reduce_fusion
  26.3 0.1 broadcast_in_dim.53
  26.4 0.0 copy-done
  26.4 0.1 multiply_sine_fusion
  26.5 2.5 %trig.1.refs_4_ = bf16[4,2,2,512,256]{4,3,2,1,0:T(8,128)(2,1)S(1)} custom-call(), custom_call_target="tpu_custom_call" | custom-call | flops 4000000000 | bytes 1048576 | tf_op jit(solution)/shard_map/trig/pallas_call | solution.py:656
  29.0 0.0 copy-start.5
  29.0 1.9 %copy-done.5 = bf16[4,2,2,512,256]{4,3,2,1,0:T(8,128)(2,1)} copy-done((bf16[4,2,2,512,256]{4,3,2,1,0:T(8,128)(2,1)}, bf16[4,2,2,512,256]{4,3,2,1,0:T(8,128)(2,1)S(1)}, u32[]{:S(2)}) %copy-start.5) | copy-done | bytes 4194328
  30.9 14.5 %all-to-all-done.refs_0_ = f32[16,96,128]{2,1,0:T(8,128)S(1)} async-done(((f32[16,96,128]{2,1,0:T(8,128)}), f32[16,96,128]{2,1,0:T(8,128)S(1)}, u32[]{:S(2)}, u32[]{:S(2)}) %all-to-all-start) | async-done | bytes 786464 | tf_op jit(solution)/shard_map/all_to_all | solution.py:624
  45.3 0.1 broadcast_in_dim.55.refs_3_
  45.4 0.1 broadcast_in_dim.54.refs_1_
  45.6 0.0 copy-done.2
  45.6 7.3 %grid.1 = f32[16,104,128]{2,1,0:T(8,128)} custom-call(f32[16,96,128]{2,1,0:T(8,128)S(1)} %all-to-all-done.refs_0_, s32[512,128]{1,0:T(8,128)S(1)} %broadcast_in_dim.54.refs_1_, f32[64,2048]{1,0:T(8,128)S(1)} %bitcast.6, f32[64,128]{1,0:T(8,128)S(1)} %broadcast_in_dim.55.refs_3_, bf16[4,2,2,512,256]{4,3,2,1,0:T(8,128)(2,1)} %copy-done.5), custom_call_target="tpu_custom_call" | custom-call | flops 8000000000 | bytes 1048576 | tf_op jit(solution)/shard_map/grid/pallas_call | solution.py:673
  52.9 4.7 %all-to-all-start.1 = ((f32[16,104,128]{2,1,0:T(8,128)}), f32[16,104,128]{2,1,0:T(8,128)S(1)}, u32[]{:S(2)}, u32[]{:S(2)}) async-start(f32[16,104,128]{2,1,0:T(8,128)} %grid.1), calls=%async_computation.1 | async-start | bytes 1703936 | tf_op jit(solution)/shard_map/all_to_all | solution.py:624
  57.6 0.0 copy-done.1
  57.6 0.0 copy-done.3
  57.6 0.0 copy-done.4
  57.6 11.5 %table.1 = (bf16[4,8,512,1024]{3,2,1,0:T(8,128)(2,1)}, f32[32,512]{1,0:T(8,128)S(1)}) custom-call(s32[64]{0:T(128)S(1)} %copy-done.1, f32[1024]{0:T(1024)S(1)} %copy-done.4, f32[8,512]{1,0:T(8,128)S(1)} %copy-done.3), custom_call_target="tpu_custom_call" | custom-call | flops 12000000000 | bytes 1048576 | tf_op jit(solution)/shard_map/table/pallas_call | solution.py:693
  69.2 8.6 %all-to-all-done.1.refs_1_ = f32[16,104,128]{2,1,0:T(8,128)S(1)} async-done(((f32[16,104,128]{2,1,0:T(8,128)}), f32[16,104,128]{2,1,0:T(8,128)S(1)}, u32[]{:S(2)}, u32[]{:S(2)}) %all-to-all-start.1) | async-done | bytes 852000 | tf_op jit(solution)/shard_map/all_to_all | solution.py:624
  77.8 0.2 broadcast_in_dim.56.refs_2_
  78.0 12.9 %analyze.1 = f32[6,32,512]{2,1,0:T(8,128)} custom-call(s32[64]{0:T(128)S(1)} %copy-done.1, f32[16,104,128]{2,1,0:T(8,128)S(1)} %all-to-all-done.1.refs_1_, s32[1024,128]{1,0:T(8,128)S(1)} %broadcast_in_dim.56.refs_2_, s32[1,1024]{1,0:T(1,128)S(1)} %bitcast.5, f32[32,512]{1,0:T(8,128)S(1)} %get-tuple-element.7.refs_4_, ...), custom_call_target="tpu_custom_call" | custom-call | flops 8999999488 | bytes 1048576 | tf_op jit(solution)/shard_map/analyze/pallas_call | solution.py:708
  (3 shorter events, 0.0 us)
Async XLA Ops:
  0.0 25.4 %copy-start.6 = (s32[512]{0:T(512)S(1)}, s32[512]{0:T(512)}, u32[]{:S(2)}) copy-start(s32[512]{0:T(512)} %param.10) | copy-start | bytes 6148
  0.0 26.4 %copy-start = (s32[1024]{0:T(1024)S(1)}, s32[1024]{0:T(1024)}, u32[]{:S(2)}) copy-start(s32[1024]{0:T(1024)} %param.9) | copy-start | bytes 12292
  1.7 43.8 %copy-start.2 = (f32[1,64,2048]{2,1,0:T(8,128)S(1)}, f32[1,64,2048]{2,1,0:T(8,128)}, u32[]{:S(2)}) copy-start(f32[1,64,2048]{2,1,0:T(8,128)} %param.8) | copy-start | bytes 1572868
  18.9 38.7 %copy-start.1 = (s32[64]{0:T(128)S(1)}, s32[64]{0:T(128)}, u32[]{:S(2)}) copy-start(s32[64]{0:T(128)} %pad_add_fusion.refs_0_) | copy-start | bytes 772
  18.9 38.7 %copy-start.3 = (f32[8,512]{1,0:T(8,128)S(1)}, f32[8,512]{1,0:T(8,128)}, u32[]{:S(2)}) copy-start(f32[8,512]{1,0:T(8,128)} %constant.29.clone.refs_3_.refs_2_) | copy-start | bytes 49156
  19.0 38.7 %copy-start.4 = (f32[1024]{0:T(1024)S(1)}, f32[1024]{0:T(1024)}, u32[]{:S(2)}) copy-start(f32[1024]{0:T(1024)} %constant.31.clone.refs_1_) | copy-start | bytes 12292
  19.0 26.4 %all-to-all-start = ((f32[16,96,128]{2,1,0:T(8,128)}), f32[16,96,128]{2,1,0:T(8,128)S(1)}, u32[]{:S(2)}, u32[]{:S(2)}) async-start(f32[16,96,128]{2,1,0:T(8,128)} %synth.1), calls=%async_computation | async-start | bytes 1572864 | tf_op jit(solution)/shard_map/all_to_all | solution.py:624
  29.0 1.9 %copy-start.5 = (bf16[4,2,2,512,256]{4,3,2,1,0:T(8,128)(2,1)}, bf16[4,2,2,512,256]{4,3,2,1,0:T(8,128)(2,1)S(1)}, u32[]{:S(2)}) copy-start(bf16[4,2,2,512,256]{4,3,2,1,0:T(8,128)(2,1)S(1)} %trig.1.refs_4_) | copy-start | bytes 12582916
  52.9 24.9 %all-to-all-start.1 = ((f32[16,104,128]{2,1,0:T(8,128)}), f32[16,104,128]{2,1,0:T(8,128)S(1)}, u32[]{:S(2)}, u32[]{:S(2)}) async-start(f32[16,104,128]{2,1,0:T(8,128)} %grid.1), calls=%async_computation.1 | async-start | bytes 1703936 | tf_op jit(solution)/shard_map/all_to_all | solution.py:624

commit v6 on v5

--- a/solution.py
+++ b/solution.py
@@ -19,6 +19,7 @@
 ROWS = CHAN * BLK
 CHUNK = 64
 CHECK = 16
+PLACES = 1024
 LANES = 128
 KTILE = 256
 BF = jnp.bfloat16
@@ -67,7 +68,7 @@
     orders = jnp.zeros((BLK, LANES), jnp.int32)
     lowest, highest = jnp.int32(DEG), jnp.int32(0)
     for i in range(BLK):
-        order = slots_ref[first + i]
+        order = slots_ref[first + i] // PLACES
         orders = jnp.where(sublane == i, order, orders)
         lowest, highest = jnp.minimum(lowest, order), jnp.maximum(highest, order)
     return orders, lowest // CHUNK, highest // CHUNK + 1
@@ -177,7 +178,7 @@
         column = orders[:, :1]
         here = pl.ds(pl.multiple_of(block * BLK, BLK), BLK)
         for i in range(BLK):
-            source = pl.ds(slots_ref[modes + block * BLK + i], 1)
+            source = pl.ds(slots_ref[block * BLK + i] % PLACES, 1)
             coeff_ref[:, i : i + 1, :] = spec_ref[:, source, :]
         degree = lax.broadcasted_iota(jnp.int32, (BLK, DEG), 1)
         within = jnp.where(degree >= column, within_ref[here, :], 0.0)
@@ -211,16 +212,20 @@
             )
 
         def add_products(step, high_ref, low_ref):
-            def part(parity, columns):
+            def high_part(parity, columns):
                 lhs = lhs_ref[step, :, parity * width : (parity + 1) * width]
                 first = dot(lhs, high_ref[parity, :, columns])
-                second = dot(lhs[:ROWS], low_ref[parity, :, columns])
-                acc_ref[block, parity, :, columns] += first[:ROWS] + first[ROWS:] + second
+                acc_ref[block, parity, :, columns] += first[:ROWS] + first[ROWS:]
+
+            def low_part(parity, columns):
+                lhs = lhs_ref[step, :ROWS, parity * width : (parity + 1) * width]
+                acc_ref[block, parity, :, columns] += dot(lhs, low_ref[parity, :, columns])
 
             return [
                 functools.partial(part, parity, slice(at, at + KTILE))
                 for parity in range(2)
                 for at in range(0, HALF, KTILE)
+                for part in (high_part, low_part)
             ]
 
         def two_chunks(guard, pair, carry):
@@ -397,7 +402,7 @@
         orders, first, last = block_orders(slots_ref, block * BLK)
         orders = orders[:, :1]
         here = pl.ds(pl.multiple_of(block * BLK, BLK), BLK)
-        result_ref[...] = jnp.zeros_like(result_ref)
+        result_ref[block] = jnp.zeros((DEG, LANES), F32)
 
         def some_chunks(steps, inner):
             for step in steps:
@@ -407,7 +412,7 @@
                 full = full[:, :LANES] + full[:, LANES:]
                 picked = jnp.where(keep, full, 0.0).reshape(CHUNK, BLK, LANES)
                 to = pl.ds(pl.multiple_of(step * CHUNK, CHUNK), CHUNK)
-                result_ref[to, :] = jnp.sum(picked, axis=1)
+                result_ref[block, to, :] = jnp.sum(picked, axis=1)
             return inner
 
         lax.fori_loop(0, first & 1, lambda unused, inner: some_chunks((first,), inner), 0)
@@ -417,21 +422,23 @@
             lambda pair, inner: some_chunks((2 * pair, 2 * pair + 1), inner),
             0,
         )
-        turned = result_ref[...].T
+        return unused
+
+    lax.fori_loop(0, blocks, one_block, 0)
+    for block in range(blocks):
+        orders = block_orders(slots_ref, block * BLK)[0][:, :1]
+        turned = result_ref[block].T
         turned = turned[:ROWS] + turned[ROWS : 2 * ROWS]
         degree = lax.broadcasted_iota(jnp.int32, (BLK, DEG), 1)
-        within = jnp.where(degree >= orders, within_ref[here, :], 0.0)
+        within = jnp.where(degree >= orders, within_ref[block * BLK : (block + 1) * BLK, :], 0.0)
         for c in range(CHAN):
             part = turned[c * BLK : (c + 1) * BLK] * within
             if c // 2 == FIELDS - 1:
                 part = part * inverse
-            coeff_ref[c] = part
+            coeff_ref[block, c] = part
         for i in range(BLK):
-            target = pl.ds(slots_ref[modes + block * BLK + i], 1)
-            out_ref[:, target, :] = coeff_ref[:, i : i + 1, :]
-        return unused
-
-    lax.fori_loop(0, blocks, one_block, 0)
+            target = pl.ds(slots_ref[block * BLK + i] % PLACES, 1)
+            out_ref[:, target, :] = coeff_ref[block, :, i : i + 1, :]
 
 
 def base_trig(order, first):
@@ -601,15 +608,12 @@
     def sort_rows(table):
         rank = jnp.sum((table[:, None, :] < table[:, :, None]).astype(jnp.int32), 2)
         match = rank[:, None, :] == jnp.arange(modes, dtype=jnp.int32)[None, :, None]
-        places = jnp.arange(modes, dtype=jnp.int32)[None, None, :]
-        return [
-            jnp.sum(jnp.where(match, values, 0), 2).reshape(-1)
-            for values in (table[:, None, :], places)
-        ]
+        keys = table * PLACES + jnp.arange(modes, dtype=jnp.int32)[None, :]
+        return jnp.sum(jnp.where(match, keys[:, None, :], 0), 2).reshape(-1)
 
     own = lax.dynamic_slice_in_dim(slot_wavenumber, band_index * modes, modes)
-    local = jnp.concatenate(sort_rows(own.reshape(1, modes)))
-    ordered = sort_rows(slot_wavenumber.reshape(bands, modes))[0]
+    local = sort_rows(own.reshape(1, modes))
+    ordered = sort_rows(slot_wavenumber.reshape(bands, modes)) // PLACES
     rows = jnp.asarray(latitude_rows())
     spread = jnp.asarray(spread_matrix())
     latitude = row_latitude.reshape(1, NLAT)
@@ -714,9 +718,9 @@
             pltpu.VMEM(chunk_shape, BF),
             pltpu.VMEM((blocks, 2 * HALF, 2 * LANES), BF),
             pltpu.VMEM((blocks * 4 * ROWS, NLAT), BF),
-            pltpu.VMEM((DEG, LANES), F32),
+            pltpu.VMEM((blocks, DEG, LANES), F32),
             pltpu.VMEM((NLAT, HALF), BF),
-            pltpu.VMEM((CHAN, BLK, DEG), F32),
+            pltpu.VMEM((blocks, CHAN, BLK, DEG), F32),
             pltpu.SemaphoreType.DMA((blocks, chunks)),
         ],
         compiler_params=params,

time: 91.9 us -> 92.6 us (level)
  the two profiles are of different devices: /device:TPU:8 before, /device:TPU:0 now
where the time goes in v6:
time: 92.6 us; the launch traced here: 92.5 us
  Pallas kernels  51.9 us (56%)
  waiting for transfers between devices  22.1 us (24%)
  starting transfers between devices  13 us (14%)
  other arithmetic  2.57 us (3%)
  local copies, waits for them, and re-layouts  2.5 us (3%)
    all_to_all x2, waiting for transfers between devices, exchange(): lax.all_to_all(value, 'band', split_axis=0, concat_axis=0, tiled=True)  22.1 us
    pallas_call x1, Pallas kernels, per_device(): pl.pallas_call(lambda *refs: synth_kernel(dims, *refs), out_shape=jax.Sha...  17.4 us
    all_to_all x2, starting transfers between devices, exchange(): lax.all_to_all(value, 'band', split_axis=0, concat_axis=0, tiled=True)  13 us
    pallas_call x1, Pallas kernels, per_device(): pl.pallas_call(lambda *refs: analyze_kernel(dims, chunk_rows, *refs), out...  12.9 us
    pallas_call x1, Pallas kernels, per_device(): pl.pallas_call(lambda *refs: table_kernel(blocks, *refs), out_shape=[jax....  11.8 us
    pallas_call x1, Pallas kernels, per_device(): pl.pallas_call(lambda *refs: grid_kernel(grid_dims, *refs), out_shape=jax...  7.34 us
    pallas_call x1, Pallas kernels, per_device(): pl.pallas_call(trig_kernel, out_shape=jax.ShapeDtypeStruct(trig_shape, BF...  2.47 us
    unnamed x14, local copies, waits for them, and re-layouts  1.96 us
  transfers between devices with their start and end apart: 2, of which 2 were waited for; matrix products, arithmetic and copies ran while one was open for 1% of the time, Pallas kernels for 15%

profile of v6, /device:TPU:0, one launch (start us, length us, event | category | flops | bytes accessed | tf_op | source)
XLA Modules:
  0.0 92.5 jit_solution(3370792843624850185)
XLA Ops:
  0.0 0.0 copy-start.6
  0.0 0.8 iota_add_fusion.1
  0.8 0.2 convert_reduce_fusion.1
  1.0 0.6 select_reduce_fusion.1.refs_0_
  1.6 17.4 %synth.1 = f32[16,96,128]{2,1,0:T(8,128)} custom-call(s32[32]{0:T(128)} %select_reduce_fusion.1.refs_0_, f32[1024]{0:T(1024)} %constant.47.clone.refs_1_, f32[6,32,512]{2,1,0:T(8,128)} %bitcast.7, f32[8,512]{1,0:T(8,128)} %constant.45.clone.refs_3_.refs_2_, bf16[128,1024]{1,0:T(8,128)(2,1)} %constant.46.clone.refs_4_, s32[1,1024]{1,0:T(1,128)} %bitcast.4), custom_call_target="tpu_custom_call" | custom-call | flops 15000000512 | bytes 1048576 | tf_op jit(solution)/shard_map/synth/pallas_call | solution.py:630
  19.1 0.0 copy-start.1
  19.1 0.0 copy-start.3
  19.1 0.0 copy-start.4
  19.1 8.1 %all-to-all-start = ((f32[16,96,128]{2,1,0:T(8,128)}), f32[16,96,128]{2,1,0:T(8,128)S(1)}, u32[]{:S(2)}, u32[]{:S(2)}) async-start(f32[16,96,128]{2,1,0:T(8,128)} %synth.1), calls=%async_computation | async-start | bytes 1572864 | tf_op jit(solution)/shard_map/all_to_all | solution.py:628
  27.2 0.0 copy-done.6
  27.2 0.1 lt.46
  27.3 0.5 convert_reduce_fusion
  27.8 0.3 select_reduce_fusion
  28.1 0.1 reshape.188
  28.2 0.0 copy-done
  28.2 0.1 multiply_sine_fusion
  28.3 2.5 %trig.1.refs_4_ = bf16[4,2,2,512,256]{4,3,2,1,0:T(8,128)(2,1)S(1)} custom-call(), custom_call_target="tpu_custom_call" | custom-call | flops 4000000000 | bytes 1048576 | tf_op jit(solution)/shard_map/trig/pallas_call | solution.py:660
  30.8 0.0 copy-start.5
  30.8 1.9 %copy-done.5 = bf16[4,2,2,512,256]{4,3,2,1,0:T(8,128)(2,1)} copy-done((bf16[4,2,2,512,256]{4,3,2,1,0:T(8,128)(2,1)}, bf16[4,2,2,512,256]{4,3,2,1,0:T(8,128)(2,1)S(1)}, u32[]{:S(2)}) %copy-start.5) | copy-done | bytes 4194328
  32.7 14.2 %all-to-all-done.refs_0_ = f32[16,96,128]{2,1,0:T(8,128)S(1)} async-done(((f32[16,96,128]{2,1,0:T(8,128)}), f32[16,96,128]{2,1,0:T(8,128)S(1)}, u32[]{:S(2)}, u32[]{:S(2)}) %all-to-all-start) | async-done | bytes 786464 | tf_op jit(solution)/shard_map/all_to_all | solution.py:628
  46.9 0.1 broadcast_in_dim.54.refs_3_
  47.0 0.1 broadcast_in_dim.34.refs_1_
  47.1 0.0 copy-done.2
  47.2 7.3 %grid.1 = f32[16,104,128]{2,1,0:T(8,128)} custom-call(f32[16,96,128]{2,1,0:T(8,128)S(1)} %all-to-all-done.refs_0_, s32[512,128]{1,0:T(8,128)S(1)} %broadcast_in_dim.34.refs_1_, f32[64,2048]{1,0:T(8,128)S(1)} %bitcast.6, f32[64,128]{1,0:T(8,128)S(1)} %broadcast_in_dim.54.refs_3_, bf16[4,2,2,512,256]{4,3,2,1,0:T(8,128)(2,1)} %copy-done.5), custom_call_target="tpu_custom_call" | custom-call | flops 8000000000 | bytes 1048576 | tf_op jit(solution)/shard_map/grid/pallas_call | solution.py:677
  54.5 4.9 %all-to-all-start.1 = ((f32[16,104,128]{2,1,0:T(8,128)}), f32[16,104,128]{2,1,0:T(8,128)S(1)}, u32[]{:S(2)}, u32[]{:S(2)}) async-start(f32[16,104,128]{2,1,0:T(8,128)} %grid.1), calls=%async_computation.1 | async-start | bytes 1703936 | tf_op jit(solution)/shard_map/all_to_all | solution.py:628
  59.4 0.0 copy-done.1
  59.4 0.0 copy-done.3
  59.4 0.0 copy-done.4
  59.5 11.8 %table.1 = (bf16[4,8,512,1024]{3,2,1,0:T(8,128)(2,1)}, f32[32,512]{1,0:T(8,128)S(1)}) custom-call(s32[32]{0:T(128)S(1)} %copy-done.1, f32[1024]{0:T(1024)S(1)} %copy-done.4, f32[8,512]{1,0:T(8,128)S(1)} %copy-done.3), custom_call_target="tpu_custom_call" | custom-call | flops 12000000000 | bytes 1048576 | tf_op jit(solution)/shard_map/table/pallas_call | solution.py:697
  71.3 7.9 %all-to-all-done.1.refs_1_ = f32[16,104,128]{2,1,0:T(8,128)S(1)} async-done(((f32[16,104,128]{2,1,0:T(8,128)}), f32[16,104,128]{2,1,0:T(8,128)S(1)}, u32[]{:S(2)}, u32[]{:S(2)}) %all-to-all-start.1) | async-done | bytes 852000 | tf_op jit(solution)/shard_map/all_to_all | solution.py:628
  79.2 0.2 broadcast_in_dim.55.refs_2_
  79.4 12.9 %analyze.1 = f32[6,32,512]{2,1,0:T(8,128)} custom-call(s32[32]{0:T(128)S(1)} %copy-done.1, f32[16,104,128]{2,1,0:T(8,128)S(1)} %all-to-all-done.1.refs_1_, s32[1024,128]{1,0:T(8,128)S(1)} %broadcast_in_dim.55.refs_2_, s32[1,1024]{1,0:T(1,128)S(1)} %bitcast.5, f32[32,512]{1,0:T(8,128)S(1)} %get-tuple-element.7.refs_4_, ...), custom_call_target="tpu_custom_call" | custom-call | flops 8999999488 | bytes 1048576 | tf_op jit(solution)/shard_map/analyze/pallas_call | solution.py:712
  (4 shorter events, 0.0 us)
Async XLA Ops:
  0.0 27.2 %copy-start.6 = (s32[512]{0:T(512)S(1)}, s32[512]{0:T(512)}, u32[]{:S(2)}) copy-start(s32[512]{0:T(512)} %param.10) | copy-start | bytes 6148
  0.0 28.2 %copy-start = (s32[1024]{0:T(1024)S(1)}, s32[1024]{0:T(1024)}, u32[]{:S(2)}) copy-start(s32[1024]{0:T(1024)} %param.9) | copy-start | bytes 12292
  1.6 45.5 %copy-start.2 = (f32[1,64,2048]{2,1,0:T(8,128)S(1)}, f32[1,64,2048]{2,1,0:T(8,128)}, u32[]{:S(2)}) copy-start(f32[1,64,2048]{2,1,0:T(8,128)} %param.8) | copy-start | bytes 1572868
  19.1 40.4 %copy-start.1 = (s32[32]{0:T(128)S(1)}, s32[32]{0:T(128)}, u32[]{:S(2)}) copy-start(s32[32]{0:T(128)} %select_reduce_fusion.1.refs_0_) | copy-start | bytes 388
  19.1 40.3 %copy-start.3 = (f32[8,512]{1,0:T(8,128)S(1)}, f32[8,512]{1,0:T(8,128)}, u32[]{:S(2)}) copy-start(f32[8,512]{1,0:T(8,128)} %constant.45.clone.refs_3_.refs_2_) | copy-start | bytes 49156
  19.1 40.3 %copy-start.4 = (f32[1024]{0:T(1024)S(1)}, f32[1024]{0:T(1024)}, u32[]{:S(2)}) copy-start(f32[1024]{0:T(1024)} %constant.47.clone.refs_1_) | copy-start | bytes 12292
  19.1 27.8 %all-to-all-start = ((f32[16,96,128]{2,1,0:T(8,128)}), f32[16,96,128]{2,1,0:T(8,128)S(1)}, u32[]{:S(2)}, u32[]{:S(2)}) async-start(f32[16,96,128]{2,1,0:T(8,128)} %synth.1), calls=%async_computation | async-start | bytes 1572864 | tf_op jit(solution)/shard_map/all_to_all | solution.py:628
  30.8 1.9 %copy-start.5 = (bf16[4,2,2,512,256]{4,3,2,1,0:T(8,128)(2,1)}, bf16[4,2,2,512,256]{4,3,2,1,0:T(8,128)(2,1)S(1)}, u32[]{:S(2)}) copy-start(bf16[4,2,2,512,256]{4,3,2,1,0:T(8,128)(2,1)S(1)} %trig.1.refs_4_) | copy-start | bytes 12582916
  54.5 24.7 %all-to-all-start.1 = ((f32[16,104,128]{2,1,0:T(8,128)}), f32[16,104,128]{2,1,0:T(8,128)S(1)}, u32[]{:S(2)}, u32[]{:S(2)}) async-start(f32[16,104,128]{2,1,0:T(8,128)} %grid.1), calls=%async_computation.1 | async-start | bytes 1703936 | tf_op jit(solution)/shard_map/all_to_all | solution.py:628

commit v7 on v6

--- a/solution.py
+++ b/solution.py
@@ -162,10 +162,11 @@
     for index, (source, target) in enumerate(pairs):
         copies.append(pltpu.make_async_copy(source, target, sems.at[index]))
         copies[-1].start()
-    for copy in copies:
+    copies[0].wait()
+    recursion_tables(slots_ref, modes, rows_ref, start_ref, before_ref, within_ref)
+    for copy in copies[1:]:
         copy.wait()
     fold_matrix(latitude_ref, fold_ref)
-    recursion_tables(slots_ref, modes, rows_ref, start_ref, before_ref, within_ref)
     south = latitude_ref[...] >= HALF
     spread_width = 4 * (CHUNK // 2) * BLK
     lane = lax.broadcasted_iota(jnp.int32, (2 * ROWS, spread_width), 1)
@@ -335,7 +336,7 @@
 
 def analyze_kernel(
     dims, total_row, slots_ref, data_ref, column_ref, latitude_ref, within_ref, table_ref,
-    out_ref, chunk_ref, weight_ref, stack_ref, result_ref, fold_ref, coeff_ref, sems,
+    out_ref, chunk_ref, weight_ref, stack_ref, result_ref, fold_ref, coeff_ref, raw_ref, sems,
 ):
     bands, row_count, modes, blocks, tiles = dims
     chunks = DEG // CHUNK
@@ -404,24 +405,34 @@
         here = pl.ds(pl.multiple_of(block * BLK, BLK), BLK)
         result_ref[block] = jnp.zeros((DEG, LANES), F32)
 
-        def some_chunks(steps, inner):
-            for step in steps:
-                copy_in(block, step).wait()
-            for step in steps:
-                full = dot(chunk_ref[block, step], weight_ref[block])
-                full = full[:, :LANES] + full[:, LANES:]
-                picked = jnp.where(keep, full, 0.0).reshape(CHUNK, BLK, LANES)
-                to = pl.ds(pl.multiple_of(step * CHUNK, CHUNK), CHUNK)
-                result_ref[block, to, :] = jnp.sum(picked, axis=1)
+        def product(step, which):
+            full = dot(chunk_ref[block, step], weight_ref[block])
+            raw_ref[which] = full[:, :LANES] + full[:, LANES:]
+
+        def pick(step, which):
+            picked = jnp.where(keep, raw_ref[which], 0.0).reshape(CHUNK, BLK, LANES)
+            to = pl.ds(pl.multiple_of(step * CHUNK, CHUNK), CHUNK)
+            result_ref[block, to, :] = jnp.sum(picked, axis=1)
+
+        def lone_chunk(unused, inner):
+            copy_in(block, first).wait()
+            product(first, 1)
             return inner
 
-        lax.fori_loop(0, first & 1, lambda unused, inner: some_chunks((first,), inner), 0)
-        lax.fori_loop(
-            (first + 1) // 2,
-            chunks // 2,
-            lambda pair, inner: some_chunks((2 * pair, 2 * pair + 1), inner),
-            0,
-        )
+        def two_chunks(pair, inner):
+            step = 2 * pair
+            copy_in(block, step).wait()
+            copy_in(block, step + 1).wait()
+            product(step, 0)
+            pick(jnp.maximum(step - 1, 0), 1)
+            product(step + 1, 1)
+            pick(step, 0)
+            return inner
+
+        raw_ref[1] = jnp.zeros((CHUNK * BLK, LANES), F32)
+        lax.fori_loop(0, first & 1, lone_chunk, 0)
+        lax.fori_loop((first + 1) // 2, chunks // 2, two_chunks, 0)
+        pick(chunks - 1, 1)
         return unused
 
     lax.fori_loop(0, blocks, one_block, 0)
@@ -559,15 +570,17 @@
         for parity in range(2):
             both = values[0] + values[1] if parity == 0 else values[0] - values[1]
             high, low = split_two(both)
-            weight_ref[parity, :group, :] = high
-            weight_ref[parity, padded : padded + group, :] = low
-            first = dot(trig_high[parity], weight_ref[parity], 1)
-            second = dot(trig_low[parity], weight_ref[parity, :padded, :], 1)
-            part = first[:, :padded] + first[:, padded:] + second
-            if k == 0:
-                acc_ref[parity] = part
-            else:
-                acc_ref[parity] += part
+            columns = slice(k, k + KTILE)
+            weight_ref[parity, :group, columns] = high
+            weight_ref[parity, padded : padded + group, columns] = low
+    for parity in range(2):
+        trig_high, trig_low = [
+            jnp.concatenate([trig_ref[t, part, parity] for t in range(len(copies))], 1)
+            for part in range(2)
+        ]
+        first = dot(trig_high, weight_ref[parity], 1)
+        second = dot(trig_low, weight_ref[parity, :padded, :], 1)
+        acc_ref[parity] = first[:, :padded] + first[:, padded:] + second
 
     joined = []
     for kind in range(2):
@@ -682,7 +695,7 @@
         scratch_shapes=[
             pltpu.VMEM((slots, slots), BF),
             pltpu.VMEM((2, 2 * group, slots), BF),
-            pltpu.VMEM((2, 2 * padded, KTILE), BF),
+            pltpu.VMEM((2, 2 * padded, NLON // 2), BF),
             pltpu.VMEM((2, slots, padded), F32),
             trig_scratch,
             pltpu.SemaphoreType.DMA((trig_tiles,)),
@@ -721,6 +734,7 @@
             pltpu.VMEM((blocks, DEG, LANES), F32),
             pltpu.VMEM((NLAT, HALF), BF),
             pltpu.VMEM((blocks, CHAN, BLK, DEG), F32),
+            pltpu.VMEM((2, CHUNK * BLK, LANES), F32),
             pltpu.SemaphoreType.DMA((blocks, chunks)),
         ],
         compiler_params=params,

time: 92.6 us -> 91.5 us (0.988)
  Pallas kernels: 51.9 us -> 49 us
    pallas_call x1, Pallas kernels: 17.4 us -> 16.2 us  [per_device(): pl.pallas_call(lambda *refs: synth_kernel(dims, *refs), out_shape=jax.Sha...]
where the time goes in v7:
time: 91.5 us; the launch traced here: 90.9 us
  Pallas kernels  49 us (54%)
  waiting for transfers between devices  22.9 us (25%)
  starting transfers between devices  13.6 us (15%)
  other arithmetic  2.57 us (3%)
  local copies, waits for them, and re-layouts  2.5 us (3%)
    all_to_all x2, waiting for transfers between devices, exchange(): lax.all_to_all(value, 'band', split_axis=0, concat_axis=0, tiled=True)  22.9 us
    pallas_call x1, Pallas kernels, per_device(): pl.pallas_call(lambda *refs: synth_kernel(dims, *refs), out_shape=jax.Sha...  16.2 us
    all_to_all x2, starting transfers between devices, exchange(): lax.all_to_all(value, 'band', split_axis=0, concat_axis=0, tiled=True)  13.6 us
    pallas_call x1, Pallas kernels, per_device(): pl.pallas_call(lambda *refs: analyze_kernel(dims, chunk_rows, *refs), out...  12.3 us
    pallas_call x1, Pallas kernels, per_device(): pl.pallas_call(lambda *refs: table_kernel(blocks, *refs), out_shape=[jax....  11.1 us
    pallas_call x1, Pallas kernels, per_device(): pl.pallas_call(lambda *refs: grid_kernel(grid_dims, *refs), out_shape=jax...  6.98 us
    pallas_call x1, Pallas kernels, per_device(): pl.pallas_call(trig_kernel, out_shape=jax.ShapeDtypeStruct(trig_shape, BF...  2.47 us
    unnamed x14, local copies, waits for them, and re-layouts  1.96 us
  transfers between devices with their start and end apart: 2, of which 2 were waited for; matrix products, arithmetic and copies ran while one was open for 1% of the time, Pallas kernels for 15%

profile of v7, /device:TPU:0, one launch (start us, length us, event | category | flops | bytes accessed | tf_op | source)
XLA Modules:
  0.0 90.9 jit_solution(12058092989406329554)
XLA Ops:
  0.0 0.0 copy-start.6
  0.0 0.8 iota_add_fusion.1
  0.8 0.2 convert_reduce_fusion.1
  1.0 0.6 select_reduce_fusion.1.refs_0_
  1.6 16.2 %synth.1 = f32[16,96,128]{2,1,0:T(8,128)} custom-call(s32[32]{0:T(128)} %select_reduce_fusion.1.refs_0_, f32[1024]{0:T(1024)} %constant.47.clone.refs_1_, f32[6,32,512]{2,1,0:T(8,128)} %bitcast.7, f32[8,512]{1,0:T(8,128)} %constant.45.clone.refs_3_.refs_2_, bf16[128,1024]{1,0:T(8,128)(2,1)} %constant.46.clone.refs_4_, s32[1,1024]{1,0:T(1,128)} %bitcast.4), custom_call_target="tpu_custom_call" | custom-call | flops 15000000512 | bytes 1048576 | tf_op jit(solution)/shard_map/synth/pallas_call | solution.py:643
  17.8 0.0 copy-start.1
  17.9 0.0 copy-start.3
  17.9 0.0 copy-start.4
  17.9 8.7 %all-to-all-start = ((f32[16,96,128]{2,1,0:T(8,128)}), f32[16,96,128]{2,1,0:T(8,128)S(1)}, u32[]{:S(2)}, u32[]{:S(2)}) async-start(f32[16,96,128]{2,1,0:T(8,128)} %synth.1), calls=%async_computation | async-start | bytes 1572864 | tf_op jit(solution)/shard_map/all_to_all | solution.py:641
  26.6 0.0 copy-done.6
  26.6 0.1 lt.46
  26.7 0.5 convert_reduce_fusion
  27.2 0.3 select_reduce_fusion
  27.5 0.1 reshape.188
  27.6 0.0 copy-done
  27.6 0.1 multiply_sine_fusion
  27.8 2.5 %trig.1.refs_4_ = bf16[4,2,2,512,256]{4,3,2,1,0:T(8,128)(2,1)S(1)} custom-call(), custom_call_target="tpu_custom_call" | custom-call | flops 4000000000 | bytes 1048576 | tf_op jit(solution)/shard_map/trig/pallas_call | solution.py:673
  30.2 0.0 copy-start.5
  30.2 1.9 %copy-done.5 = bf16[4,2,2,512,256]{4,3,2,1,0:T(8,128)(2,1)} copy-done((bf16[4,2,2,512,256]{4,3,2,1,0:T(8,128)(2,1)}, bf16[4,2,2,512,256]{4,3,2,1,0:T(8,128)(2,1)S(1)}, u32[]{:S(2)}) %copy-start.5) | copy-done | bytes 4194328
  32.2 14.2 %all-to-all-done.refs_0_ = f32[16,96,128]{2,1,0:T(8,128)S(1)} async-done(((f32[16,96,128]{2,1,0:T(8,128)}), f32[16,96,128]{2,1,0:T(8,128)S(1)}, u32[]{:S(2)}, u32[]{:S(2)}) %all-to-all-start) | async-done | bytes 786464 | tf_op jit(solution)/shard_map/all_to_all | solution.py:641
  46.4 0.1 broadcast_in_dim.54.refs_3_
  46.4 0.1 broadcast_in_dim.34.refs_1_
  46.6 0.0 copy-done.2
  46.6 7.0 %grid.1 = f32[16,104,128]{2,1,0:T(8,128)} custom-call(f32[16,96,128]{2,1,0:T(8,128)S(1)} %all-to-all-done.refs_0_, s32[512,128]{1,0:T(8,128)S(1)} %broadcast_in_dim.34.refs_1_, f32[64,2048]{1,0:T(8,128)S(1)} %bitcast.6, f32[64,128]{1,0:T(8,128)S(1)} %broadcast_in_dim.54.refs_3_, bf16[4,2,2,512,256]{4,3,2,1,0:T(8,128)(2,1)} %copy-done.5), custom_call_target="tpu_custom_call" | custom-call | flops 8000000000 | bytes 1048576 | tf_op jit(solution)/shard_map/grid/pallas_call | solution.py:690
  53.6 4.9 %all-to-all-start.1 = ((f32[16,104,128]{2,1,0:T(8,128)}), f32[16,104,128]{2,1,0:T(8,128)S(1)}, u32[]{:S(2)}, u32[]{:S(2)}) async-start(f32[16,104,128]{2,1,0:T(8,128)} %grid.1), calls=%async_computation.1 | async-start | bytes 1703936 | tf_op jit(solution)/shard_map/all_to_all | solution.py:641
  58.5 0.0 copy-done.1
  58.5 0.0 copy-done.3
  58.5 0.0 copy-done.4
  58.5 11.1 %table.1 = (bf16[4,8,512,1024]{3,2,1,0:T(8,128)(2,1)}, f32[32,512]{1,0:T(8,128)S(1)}) custom-call(s32[32]{0:T(128)S(1)} %copy-done.1, f32[1024]{0:T(1024)S(1)} %copy-done.4, f32[8,512]{1,0:T(8,128)S(1)} %copy-done.3), custom_call_target="tpu_custom_call" | custom-call | flops 12000000000 | bytes 1048576 | tf_op jit(solution)/shard_map/table/pallas_call | solution.py:710
  69.6 8.7 %all-to-all-done.1.refs_1_ = f32[16,104,128]{2,1,0:T(8,128)S(1)} async-done(((f32[16,104,128]{2,1,0:T(8,128)}), f32[16,104,128]{2,1,0:T(8,128)S(1)}, u32[]{:S(2)}, u32[]{:S(2)}) %all-to-all-start.1) | async-done | bytes 852000 | tf_op jit(solution)/shard_map/all_to_all | solution.py:641
  78.3 0.2 broadcast_in_dim.55.refs_2_
  78.5 12.3 %analyze.1 = f32[6,32,512]{2,1,0:T(8,128)} custom-call(s32[32]{0:T(128)S(1)} %copy-done.1, f32[16,104,128]{2,1,0:T(8,128)S(1)} %all-to-all-done.1.refs_1_, s32[1024,128]{1,0:T(8,128)S(1)} %broadcast_in_dim.55.refs_2_, s32[1,1024]{1,0:T(1,128)S(1)} %bitcast.5, f32[32,512]{1,0:T(8,128)S(1)} %get-tuple-element.7.refs_4_, ...), custom_call_target="tpu_custom_call" | custom-call | flops 8999999488 | bytes 1048576 | tf_op jit(solution)/shard_map/analyze/pallas_call | solution.py:725
  (4 shorter events, 0.0 us)
Async XLA Ops:
  0.0 26.6 %copy-start.6 = (s32[512]{0:T(512)S(1)}, s32[512]{0:T(512)}, u32[]{:S(2)}) copy-start(s32[512]{0:T(512)} %param.10) | copy-start | bytes 6148
  0.0 27.6 %copy-start = (s32[1024]{0:T(1024)S(1)}, s32[1024]{0:T(1024)}, u32[]{:S(2)}) copy-start(s32[1024]{0:T(1024)} %param.9) | copy-start | bytes 12292
  1.6 44.9 %copy-start.2 = (f32[1,64,2048]{2,1,0:T(8,128)S(1)}, f32[1,64,2048]{2,1,0:T(8,128)}, u32[]{:S(2)}) copy-start(f32[1,64,2048]{2,1,0:T(8,128)} %param.8) | copy-start | bytes 1572868
  17.8 40.7 %copy-start.1 = (s32[32]{0:T(128)S(1)}, s32[32]{0:T(128)}, u32[]{:S(2)}) copy-start(s32[32]{0:T(128)} %select_reduce_fusion.1.refs_0_) | copy-start | bytes 388
  17.9 40.7 %copy-start.3 = (f32[8,512]{1,0:T(8,128)S(1)}, f32[8,512]{1,0:T(8,128)}, u32[]{:S(2)}) copy-start(f32[8,512]{1,0:T(8,128)} %constant.45.clone.refs_3_.refs_2_) | copy-start | bytes 49156
  17.9 40.7 %copy-start.4 = (f32[1024]{0:T(1024)S(1)}, f32[1024]{0:T(1024)}, u32[]{:S(2)}) copy-start(f32[1024]{0:T(1024)} %constant.47.clone.refs_1_) | copy-start | bytes 12292
  17.9 28.5 %all-to-all-start = ((f32[16,96,128]{2,1,0:T(8,128)}), f32[16,96,128]{2,1,0:T(8,128)S(1)}, u32[]{:S(2)}, u32[]{:S(2)}) async-start(f32[16,96,128]{2,1,0:T(8,128)} %synth.1), calls=%async_computation | async-start | bytes 1572864 | tf_op jit(solution)/shard_map/all_to_all | solution.py:641
  30.2 1.9 %copy-start.5 = (bf16[4,2,2,512,256]{4,3,2,1,0:T(8,128)(2,1)}, bf16[4,2,2,512,256]{4,3,2,1,0:T(8,128)(2,1)S(1)}, u32[]{:S(2)}) copy-start(bf16[4,2,2,512,256]{4,3,2,1,0:T(8,128)(2,1)S(1)} %trig.1.refs_4_) | copy-start | bytes 12582916
  53.6 24.7 %all-to-all-start.1 = ((f32[16,104,128]{2,1,0:T(8,128)}), f32[16,104,128]{2,1,0:T(8,128)S(1)}, u32[]{:S(2)}, u32[]{:S(2)}) async-start(f32[16,104,128]{2,1,0:T(8,128)} %grid.1), calls=%async_computation.1 | async-start | bytes 1703936 | tf_op jit(solution)/shard_map/all_to_all | solution.py:641

commit v8 on v7

--- a/solution.py
+++ b/solution.py
@@ -335,7 +335,7 @@
 
 
 def analyze_kernel(
-    dims, total_row, slots_ref, data_ref, column_ref, latitude_ref, within_ref, table_ref,
+    dims, slots_ref, data_ref, total_ref, column_ref, latitude_ref, within_ref, table_ref,
     out_ref, chunk_ref, weight_ref, stack_ref, result_ref, fold_ref, coeff_ref, raw_ref, sems,
 ):
     bands, row_count, modes, blocks, tiles = dims
@@ -391,10 +391,7 @@
         weight_ref[block, HALF:, :LANES] = high
         weight_ref[block, HALF:, LANES:] = jnp.zeros_like(low)
 
-    total = data_ref[0, total_row : total_row + 8]
-    for d in range(1, bands):
-        total = total + data_ref[d, total_row : total_row + 8]
-    inverse = (1.0 / total)[:, :1]
+    inverse = (1.0 / total_ref[...])[:, :1]
     lane = lax.broadcasted_iota(jnp.int32, (CHUNK * BLK, LANES), 1)
     sub = lax.broadcasted_iota(jnp.int32, (CHUNK * BLK, LANES), 0)
     keep = (lane % BLK == sub % BLK) & (lane // ROWS == sub // BLK % 2)
@@ -542,7 +539,6 @@
     weight_ref[...] = jnp.zeros_like(weight_ref)
     flux_scale = math.pi / (2.0 * NLAT * NLON * DEG)
     weight = jnp.tile(sine_ref[...], (1, KTILE // LANES))
-    total = jnp.zeros((8, KTILE), F32)
 
     for k in range(0, NLON // 2, KTILE):
         copies[k // KTILE].wait()
@@ -555,7 +551,6 @@
         values = []
         for fields, at in ((sums[0] + sums[1], k), (sums[0] - sums[1], k + NLON // 2)):
             weighted_rate = rate_ref[:, at : at + KTILE] * weight
-            total = total + jnp.sum(weighted_rate.reshape(row_count // 8, 8, KTILE), axis=0)
             scaled = fields[:row_count] * (weight * flux_scale)
             values.append(
                 jnp.concatenate(
@@ -594,7 +589,6 @@
     for t in range(tiles):
         part = moved[:, t * LANES : (t + 1) * LANES]
         out_ref[:, t * modes : (t + 1) * modes, :] = part.reshape(bands, modes, LANES)
-    out_ref[:, tiles * modes :, :] = jnp.broadcast_to(jnp.sum(total), (bands, 8, LANES))
 
 
 VMEM = pl.BlockSpec(memory_space=pltpu.VMEM)
@@ -665,7 +659,6 @@
         cost_estimate=work(15),
         name="synth",
     )(local, scalars, coeffs, rows, spread, latitude)
-    received = exchange(sent)
 
     trig_tiles = NLON // 2 // KTILE
     trig_shape = (trig_tiles, 2, 2, slots, KTILE)
@@ -682,6 +675,14 @@
 
     my_latitudes = lax.dynamic_slice_in_dim(row_latitude, band_index * row_count, row_count)
     row_sine = jnp.sin(jnp.pi * (my_latitudes.astype(F32) + 0.5) / NLAT)
+    later_sine, sent = lax.optimization_barrier((row_sine, sent))
+    total = jnp.full((8, LANES), jnp.sum(capture_rate * later_sine[None, :, None]))
+    received = exchange(sent)
+    step = 1
+    while step < bands:
+        pairs = [(i, i ^ step) for i in range(bands)]
+        total = total + lax.ppermute(total, "band", pairs)
+        step *= 2
     row_sine = jnp.broadcast_to(row_sine[:, None], (row_count, LANES))
     orders = jnp.broadcast_to(ordered.reshape(slots, 1), (slots, LANES))
     group = FIELDS * row_count
@@ -689,7 +690,7 @@
     grid_dims = (bands, row_count, modes, tiles, slots)
     fluxes = pl.pallas_call(
         lambda *refs: grid_kernel(grid_dims, *refs),
-        out_shape=jax.ShapeDtypeStruct((bands, chunk_rows + 8, LANES), F32),
+        out_shape=jax.ShapeDtypeStruct((bands, chunk_rows, LANES), F32),
         in_specs=[VMEM] * 4 + [HBM],
         out_specs=VMEM,
         scratch_shapes=[
@@ -723,9 +724,9 @@
     )(local, scalars, rows)
     column = jnp.broadcast_to(row_latitude[:, None], (NLAT, LANES))
     result = pl.pallas_call(
-        lambda *refs: analyze_kernel(dims, chunk_rows, *refs),
+        lambda *refs: analyze_kernel(dims, *refs),
         out_shape=jax.ShapeDtypeStruct((CHAN, modes, DEG), F32),
-        in_specs=[SMEM, VMEM, VMEM, VMEM, VMEM, HBM],
+        in_specs=[SMEM, VMEM, VMEM, VMEM, VMEM, VMEM, HBM],
         out_specs=VMEM,
         scratch_shapes=[
             pltpu.VMEM(chunk_shape, BF),
@@ -740,7 +741,7 @@
         compiler_params=params,
         cost_estimate=work(9),
         name="analyze",
-    )(local, returned, column, latitude, within, legendre)
+    )(local, returned, total, column, latitude, within, legendre)
     return result.reshape(1, FIELDS, 2, modes, DEG)
 
 

time: 91.5 us -> 100 us (1.093)
  starting transfers between devices: 13.6 us -> 25.5 us
  waiting for transfers between devices: 22.9 us -> 16.1 us
  other arithmetic: 2.57 us -> 5.19 us
    ppermute x0 -> x4, starting transfers between devices: none -> 12.2 us  [per_device(): total = total + lax.ppermute(total, 'band', pairs)]
    all_to_all x2, waiting for transfers between devices: 22.9 us -> 11 us  [exchange(): lax.all_to_all(value, 'band', split_axis=0, concat_axis=0, tiled=True)]
    ppermute x0 -> x4, waiting for transfers between devices: none -> 5.08 us  [per_device(): total = total + lax.ppermute(total, 'band', pairs)]
    add x0 -> x4, other arithmetic: none -> 1.14 us  [per_device(): total = total + lax.ppermute(total, 'band', pairs)]
  transfers between devices with their start and end apart: 2 -> 6, of which waited for: 2 -> 3; matrix products, arithmetic and copies ran while one was open for 1% -> 4% of each run, Pallas kernels for 15% -> 21%
where the time goes in v8:
time: 100 us
  Pallas kernels  49.9 us (50%)
  starting transfers between devices  25.5 us (26%)
  waiting for transfers between devices  16.1 us (16%)
  other arithmetic  5.19 us (5%)
  local copies, waits for them, and re-layouts  3.06 us (3%)
    pallas_call x1, Pallas kernels, per_device(): pl.pallas_call(lambda *refs: synth_kernel(dims, *refs), out_shape=jax.Sha...  16.3 us
    all_to_all x2, starting transfers between devices, exchange(): lax.all_to_all(value, 'band', split_axis=0, concat_axis=0, tiled=True)  13.4 us
    pallas_call x1, Pallas kernels, per_device(): pl.pallas_call(lambda *refs: analyze_kernel(dims, *refs), out_shape=jax.S...  12.8 us
    ppermute x4, starting transfers between devices, per_device(): total = total + lax.ppermute(total, 'band', pairs)  12.2 us
    pallas_call x1, Pallas kernels, per_device(): pl.pallas_call(lambda *refs: table_kernel(blocks, *refs), out_shape=[jax....  11.4 us
    all_to_all x2, waiting for transfers between devices, exchange(): lax.all_to_all(value, 'band', split_axis=0, concat_axis=0, tiled=True)  11 us
    pallas_call x1, Pallas kernels, per_device(): pl.pallas_call(lambda *refs: grid_kernel(grid_dims, *refs), out_shape=jax...  6.97 us
    ppermute x4, waiting for transfers between devices, per_device(): total = total + lax.ppermute(total, 'band', pairs)  5.08 us
  transfers between devices with their start and end apart: 6, of which 3 were waited for; matrix products, arithmetic and copies ran while one was open for 4% of the time, Pallas kernels for 21%

profile of v8, /device:TPU:0, one launch (start us, length us, event | category | flops | bytes accessed | tf_op | source)
XLA Modules:
  0.0 100.2 jit_solution(15825002019697154335)
XLA Ops:
  0.0 0.8 iota_add_fusion.1
  0.8 0.2 convert_reduce_fusion.1
  1.0 0.8 multiply_sine_fusion
  1.8 0.6 select_reduce_fusion.1.refs_0_
  2.4 16.3 %synth.1 = f32[16,96,128]{2,1,0:T(8,128)} custom-call(s32[32]{0:T(128)} %select_reduce_fusion.1.refs_0_, f32[1024]{0:T(1024)} %constant.49.clone.refs_1_, f32[6,32,512]{2,1,0:T(8,128)} %bitcast.7, f32[8,512]{1,0:T(8,128)} %constant.47.clone.refs_3_.refs_2_, bf16[128,1024]{1,0:T(8,128)(2,1)} %constant.48.clone.refs_4_, s32[1,1024]{1,0:T(1,128)} %bitcast.5), custom_call_target="tpu_custom_call" | custom-call | flops 15000000512 | bytes 1048576 | tf_op jit(solution)/shard_map/synth/pallas_call | solution.py:637
  18.8 0.0 copy-start.3
  18.8 0.0 copy-start.4
  18.8 8.5 %all-to-all-start = ((f32[16,96,128]{2,1,0:T(8,128)}), f32[16,96,128]{2,1,0:T(8,128)S(1)}, u32[]{:S(2)}, u32[]{:S(2)}) async-start(f32[16,96,128]{2,1,0:T(8,128)} %synth.1), calls=%async_computation | async-start | bytes 1572864 | tf_op jit(solution)/shard_map/all_to_all | solution.py:635
  27.3 0.8 multiply_reduce_fusion
  28.1 0.6 broadcast_in_dim.59
  28.7 2.0 %collective-permute-start = (f32[8,128]{1,0:T(8,128)S(1)}, f32[8,128]{1,0:T(8,128)S(1)}, u32[]{:S(2)}, u32[]{:S(2)}) collective-permute-start(f32[8,128]{1,0:T(8,128)S(1)} %broadcast_in_dim.59), channel_id=1, source_target_pairs={{0,2},{2,0},{4,6},{6,4},{8,10},{10,8},{12,14},{14,12},{16,18},{18,... | collective-permute-start | bytes 12296 | tf_op jit(solution)/shard_map/ppermute | solution.py:684
  30.7 0.1 lt.47
  30.7 0.5 convert_reduce_fusion
  31.2 0.3 select_reduce_fusion
  31.6 0.1 reshape.191
  31.7 2.5 %trig.1.refs_4_ = bf16[4,2,2,512,256]{4,3,2,1,0:T(8,128)(2,1)S(1)} custom-call(), custom_call_target="tpu_custom_call" | custom-call | flops 4000000000 | bytes 1048576 | tf_op jit(solution)/shard_map/trig/pallas_call | solution.py:666
  34.1 1.9 %copy-done.5 = bf16[4,2,2,512,256]{4,3,2,1,0:T(8,128)(2,1)} copy-done((bf16[4,2,2,512,256]{4,3,2,1,0:T(8,128)(2,1)}, bf16[4,2,2,512,256]{4,3,2,1,0:T(8,128)(2,1)S(1)}, u32[]{:S(2)}) %copy-start.5) | copy-done | bytes 4194328
  36.1 11.0 %all-to-all-done.refs_0_ = f32[16,96,128]{2,1,0:T(8,128)S(1)} async-done(((f32[16,96,128]{2,1,0:T(8,128)}), f32[16,96,128]{2,1,0:T(8,128)S(1)}, u32[]{:S(2)}, u32[]{:S(2)}) %all-to-all-start) | async-done | bytes 786464 | tf_op jit(solution)/shard_map/all_to_all | solution.py:635
  47.0 0.1 broadcast_in_dim.58.refs_3_
  47.1 0.1 broadcast_in_dim.36.refs_1_
  47.3 7.0 %grid.1 = f32[16,96,128]{2,1,0:T(8,128)} custom-call(f32[16,96,128]{2,1,0:T(8,128)S(1)} %all-to-all-done.refs_0_, s32[512,128]{1,0:T(8,128)S(1)} %broadcast_in_dim.36.refs_1_, f32[64,2048]{1,0:T(8,128)S(1)} %bitcast.4, f32[64,128]{1,0:T(8,128)S(1)} %broadcast_in_dim.58.refs_3_, bf16[4,2,2,512,256]{4,3,2,1,0:T(8,128)(2,1)} %copy-done.5), custom_call_target="tpu_custom_call" | custom-call | flops 8000000000 | bytes 1048576 | tf_op jit(solution)/shard_map/grid/pallas_call | solution.py:691
  54.2 4.9 %all-to-all-start.1 = ((f32[16,96,128]{2,1,0:T(8,128)}), f32[16,96,128]{2,1,0:T(8,128)S(1)}, u32[]{:S(2)}, u32[]{:S(2)}) async-start(f32[16,96,128]{2,1,0:T(8,128)} %grid.1), calls=%async_computation.1 | async-start | bytes 1572864 | tf_op jit(solution)/shard_map/all_to_all | solution.py:635
  59.2 0.6 broadcast_add_fusion
  59.7 2.0 %collective-permute-start.1 = (f32[8,128]{1,0:T(8,128)S(1)}, f32[8,128]{1,0:T(8,128)S(1)}, u32[]{:S(2)}, u32[]{:S(2)}) collective-permute-start(f32[8,128]{1,0:T(8,128)S(1)} %broadcast_add_fusion), channel_id=1, source_target_pairs={{0,4},{2,6},{4,0},{6,2},{8,12},{10,14},{12,8},{14,10},{16,20},{18,... | collective-permute-start | bytes 12296 | tf_op jit(solution)/shard_map/ppermute | solution.py:684
  61.7 1.7 %collective-permute-done.1 = f32[8,128]{1,0:T(8,128)S(1)} collective-permute-done((f32[8,128]{1,0:T(8,128)S(1)}, f32[8,128]{1,0:T(8,128)S(1)}, u32[]{:S(2)}, u32[]{:S(2)}) %collective-permute-start.1) | collective-permute-done | bytes 4128 | tf_op jit(solution)/shard_map/ppermute | solution.py:684
  63.4 0.6 fusion.2
  64.0 3.6 %collective-permute-start.2 = (f32[8,128]{1,0:T(8,128)S(1)}, f32[8,128]{1,0:T(8,128)S(1)}, u32[]{:S(2)}, u32[]{:S(2)}) collective-permute-start(f32[8,128]{1,0:T(8,128)S(1)} %fusion.2), channel_id=1, source_target_pairs={{0,8},{2,10},{4,12},{6,14},{8,0},{10,2},{12,4},{14,6},{16,24},{18,... | collective-permute-start | bytes 12296 | tf_op jit(solution)/shard_map/ppermute | solution.py:684
  67.5 3.4 %collective-permute-done.2 = f32[8,128]{1,0:T(8,128)S(1)} collective-permute-done((f32[8,128]{1,0:T(8,128)S(1)}, f32[8,128]{1,0:T(8,128)S(1)}, u32[]{:S(2)}, u32[]{:S(2)}) %collective-permute-start.2) | collective-permute-done | bytes 4128 | tf_op jit(solution)/shard_map/ppermute | solution.py:684
  70.9 4.6 %collective-permute-start.3 = (f32[8,128]{1,0:T(8,128)S(1)}, f32[8,128]{1,0:T(8,128)S(1)}, u32[]{:S(2)}, u32[]{:S(2)}) collective-permute-start(f32[8,128]{1,0:T(8,128)S(1)} %add.54), channel_id=1, source_target_pairs={{0,16},{2,18},{4,20},{6,22},{8,24},{10,26},{12,28},{14,30},{16,0},... | collective-permute-start | bytes 12296 | tf_op jit(solution)/shard_map/ppermute | solution.py:684
  75.6 11.4 %table.1 = (bf16[4,8,512,1024]{3,2,1,0:T(8,128)(2,1)}, f32[32,512]{1,0:T(8,128)S(1)}) custom-call(s32[32]{0:T(128)S(1)} %copy-done.2, f32[1024]{0:T(1024)S(1)} %copy-done.4, f32[8,512]{1,0:T(8,128)S(1)} %copy-done.3), custom_call_target="tpu_custom_call" | custom-call | flops 12000000000 | bytes 1048576 | tf_op jit(solution)/shard_map/table/pallas_call | solution.py:711
  87.0 0.2 broadcast_in_dim.60.refs_3_
  87.2 12.8 %analyze.1 = f32[6,32,512]{2,1,0:T(8,128)} custom-call(s32[32]{0:T(128)S(1)} %copy-done.2, f32[16,96,128]{2,1,0:T(8,128)S(1)} %all-to-all-done.1.refs_1_, f32[8,128]{1,0:T(8,128)S(1)} %add.55.refs_2_, s32[1024,128]{1,0:T(8,128)S(1)} %broadcast_in_dim.60.refs_3_, s32[1,1024]{1,0:T(1,128)S(1)} %bitcast.6, f32[32,512]{1,0:T(8,128)S(1)} %get-tuple-element.11.refs_5_, ...), custom_call_target="tpu_custom_call" | custom-call | flops 8999999488 | bytes 1048576 | tf_op jit(solution)/shard_map/analyze/pallas_call | solution.py:726
  (18 shorter events, 0.1 us)
Async XLA Ops:
  0.0 30.7 %copy-start.6 = (s32[512]{0:T(512)S(1)}, s32[512]{0:T(512)}, u32[]{:S(2)}) copy-start(s32[512]{0:T(512)} %param.10) | copy-start | bytes 6148
  0.0 27.3 %copy-start = (f32[1,64,2048]{2,1,0:T(8,128)S(1)}, f32[1,64,2048]{2,1,0:T(8,128)}, u32[]{:S(2)}) copy-start(f32[1,64,2048]{2,1,0:T(8,128)} %param.8) | copy-start | bytes 1572868
  18.8 56.8 %copy-start.2 = (s32[32]{0:T(128)S(1)}, s32[32]{0:T(128)}, u32[]{:S(2)}) copy-start(s32[32]{0:T(128)} %select_reduce_fusion.1.refs_0_) | copy-start | bytes 388
  18.8 56.8 %copy-start.3 = (f32[8,512]{1,0:T(8,128)S(1)}, f32[8,512]{1,0:T(8,128)}, u32[]{:S(2)}) copy-start(f32[8,512]{1,0:T(8,128)} %constant.47.clone.refs_3_.refs_2_) | copy-start | bytes 49156
  18.8 56.8 %copy-start.4 = (f32[1024]{0:T(1024)S(1)}, f32[1024]{0:T(1024)}, u32[]{:S(2)}) copy-start(f32[1024]{0:T(1024)} %constant.49.clone.refs_1_) | copy-start | bytes 12292
  18.8 28.2 %all-to-all-start = ((f32[16,96,128]{2,1,0:T(8,128)}), f32[16,96,128]{2,1,0:T(8,128)S(1)}, u32[]{:S(2)}, u32[]{:S(2)}) async-start(f32[16,96,128]{2,1,0:T(8,128)} %synth.1), calls=%async_computation | async-start | bytes 1572864 | tf_op jit(solution)/shard_map/all_to_all | solution.py:635
  28.7 30.5 %collective-permute-start = (f32[8,128]{1,0:T(8,128)S(1)}, f32[8,128]{1,0:T(8,128)S(1)}, u32[]{:S(2)}, u32[]{:S(2)}) collective-permute-start(f32[8,128]{1,0:T(8,128)S(1)} %broadcast_in_dim.59), channel_id=1, source_target_pairs={{0,2},{2,0},{4,6},{6,4},{8,10},{10,8},{12,14},{14,12},{16,18},{18,... | collective-permute-start | bytes 12296 | tf_op jit(solution)/shard_map/ppermute | solution.py:684
  34.1 1.9 %copy-start.5 = (bf16[4,2,2,512,256]{4,3,2,1,0:T(8,128)(2,1)}, bf16[4,2,2,512,256]{4,3,2,1,0:T(8,128)(2,1)S(1)}, u32[]{:S(2)}) copy-start(bf16[4,2,2,512,256]{4,3,2,1,0:T(8,128)(2,1)S(1)} %trig.1.refs_4_) | copy-start | bytes 12582916
  47.2 39.8 %copy-start.1 = (s32[1024]{0:T(1024)S(1)}, s32[1024]{0:T(1024)}, u32[]{:S(2)}) copy-start(s32[1024]{0:T(1024)} %param.9) | copy-start | bytes 12292
  54.2 32.8 %all-to-all-start.1 = ((f32[16,96,128]{2,1,0:T(8,128)}), f32[16,96,128]{2,1,0:T(8,128)S(1)}, u32[]{:S(2)}, u32[]{:S(2)}) async-start(f32[16,96,128]{2,1,0:T(8,128)} %grid.1), calls=%async_computation.1 | async-start | bytes 1572864 | tf_op jit(solution)/shard_map/all_to_all | solution.py:635
  59.7 3.7 %collective-permute-start.1 = (f32[8,128]{1,0:T(8,128)S(1)}, f32[8,128]{1,0:T(8,128)S(1)}, u32[]{:S(2)}, u32[]{:S(2)}) collective-permute-start(f32[8,128]{1,0:T(8,128)S(1)} %broadcast_add_fusion), channel_id=1, source_target_pairs={{0,4},{2,6},{4,0},{6,2},{8,12},{10,14},{12,8},{14,10},{16,20},{18,... | collective-permute-start | bytes 12296 | tf_op jit(solution)/shard_map/ppermute | solution.py:684
  64.0 6.9 %collective-permute-start.2 = (f32[8,128]{1,0:T(8,128)S(1)}, f32[8,128]{1,0:T(8,128)S(1)}, u32[]{:S(2)}, u32[]{:S(2)}) collective-permute-start(f32[8,128]{1,0:T(8,128)S(1)} %fusion.2), channel_id=1, source_target_pairs={{0,8},{2,10},{4,12},{6,14},{8,0},{10,2},{12,4},{14,6},{16,24},{18,... | collective-permute-start | bytes 12296 | tf_op jit(solution)/shard_map/ppermute | solution.py:684
  70.9 16.1 %collective-permute-start.3 = (f32[8,128]{1,0:T(8,128)S(1)}, f32[8,128]{1,0:T(8,128)S(1)}, u32[]{:S(2)}, u32[]{:S(2)}) collective-permute-start(f32[8,128]{1,0:T(8,128)S(1)} %add.54), channel_id=1, source_target_pairs={{0,16},{2,18},{4,20},{6,22},{8,24},{10,26},{12,28},{14,30},{16,0},... | collective-permute-start | bytes 12296 | tf_op jit(solution)/shard_map/ppermute | solution.py:684

commit v9 on v7

--- a/solution.py
+++ b/solution.py
@@ -336,7 +336,7 @@
 
 def analyze_kernel(
     dims, total_row, slots_ref, data_ref, column_ref, latitude_ref, within_ref, table_ref,
-    out_ref, chunk_ref, weight_ref, stack_ref, result_ref, fold_ref, coeff_ref, raw_ref, sems,
+    out_ref, chunk_ref, weight_ref, stack_ref, result_ref, fold_ref, coeff_ref, sems,
 ):
     bands, row_count, modes, blocks, tiles = dims
     chunks = DEG // CHUNK
@@ -405,34 +405,26 @@
         here = pl.ds(pl.multiple_of(block * BLK, BLK), BLK)
         result_ref[block] = jnp.zeros((DEG, LANES), F32)
 
-        def product(step, which):
-            full = dot(chunk_ref[block, step], weight_ref[block])
-            raw_ref[which] = full[:, :LANES] + full[:, LANES:]
-
-        def pick(step, which):
-            picked = jnp.where(keep, raw_ref[which], 0.0).reshape(CHUNK, BLK, LANES)
-            to = pl.ds(pl.multiple_of(step * CHUNK, CHUNK), CHUNK)
+        def some_chunks(step, count):
+            for k in range(count):
+                copy_in(block, step + k).wait()
+            values = chunk_ref[block, pl.ds(step, count)].reshape(count * CHUNK * BLK, 2 * HALF)
+            full = dot(values, weight_ref[block])
+            full = (full[:, :LANES] + full[:, LANES:]).reshape(count, CHUNK * BLK, LANES)
+            picked = jnp.where(keep[None], full, 0.0).reshape(count * CHUNK, BLK, LANES)
+            to = pl.ds(pl.multiple_of(step * CHUNK, CHUNK), count * CHUNK)
             result_ref[block, to, :] = jnp.sum(picked, axis=1)
 
         def lone_chunk(unused, inner):
-            copy_in(block, first).wait()
-            product(first, 1)
+            some_chunks(first, 1)
             return inner
 
         def two_chunks(pair, inner):
-            step = 2 * pair
-            copy_in(block, step).wait()
-            copy_in(block, step + 1).wait()
-            product(step, 0)
-            pick(jnp.maximum(step - 1, 0), 1)
-            product(step + 1, 1)
-            pick(step, 0)
+            some_chunks(2 * pair, 2)
             return inner
 
-        raw_ref[1] = jnp.zeros((CHUNK * BLK, LANES), F32)
         lax.fori_loop(0, first & 1, lone_chunk, 0)
         lax.fori_loop((first + 1) // 2, chunks // 2, two_chunks, 0)
-        pick(chunks - 1, 1)
         return unused
 
     lax.fori_loop(0, blocks, one_block, 0)
@@ -734,7 +726,6 @@
             pltpu.VMEM((blocks, DEG, LANES), F32),
             pltpu.VMEM((NLAT, HALF), BF),
             pltpu.VMEM((blocks, CHAN, BLK, DEG), F32),
-            pltpu.VMEM((2, CHUNK * BLK, LANES), F32),
             pltpu.SemaphoreType.DMA((blocks, chunks)),
         ],
         compiler_params=params,

time: 91.5 us -> 91.6 us (level); the launches traced: 90.9 us -> 92.2 us
  Pallas kernels: 49 us -> 50.8 us
where the time goes in v9:
time: 91.6 us; the launch traced here: 92.2 us
  Pallas kernels  50.8 us (55%)
  waiting for transfers between devices  22.1 us (24%)
  starting transfers between devices  13.9 us (15%)
  other arithmetic  2.57 us (3%)
  local copies, waits for them, and re-layouts  2.5 us (3%)
    all_to_all x2, waiting for transfers between devices, exchange(): lax.all_to_all(value, 'band', split_axis=0, concat_axis=0, tiled=True)  22.1 us
    pallas_call x1, Pallas kernels, per_device(): pl.pallas_call(lambda *refs: synth_kernel(dims, *refs), out_shape=jax.Sha...  16.8 us
    all_to_all x2, starting transfers between devices, exchange(): lax.all_to_all(value, 'band', split_axis=0, concat_axis=0, tiled=True)  13.9 us
    pallas_call x1, Pallas kernels, per_device(): pl.pallas_call(lambda *refs: analyze_kernel(dims, chunk_rows, *refs), out...  12.8 us
    pallas_call x1, Pallas kernels, per_device(): pl.pallas_call(lambda *refs: table_kernel(blocks, *refs), out_shape=[jax....  11.8 us
    pallas_call x1, Pallas kernels, per_device(): pl.pallas_call(lambda *refs: grid_kernel(grid_dims, *refs), out_shape=jax...  6.98 us
    pallas_call x1, Pallas kernels, per_device(): pl.pallas_call(trig_kernel, out_shape=jax.ShapeDtypeStruct(trig_shape, BF...  2.47 us
    unnamed x14, local copies, waits for them, and re-layouts  1.96 us
  transfers between devices with their start and end apart: 2, of which 2 were waited for; matrix products, arithmetic and copies ran while one was open for 1% of the time, Pallas kernels for 15%

profile of v9, /device:TPU:0, one launch (start us, length us, event | category | flops | bytes accessed | tf_op | source)
XLA Modules:
  0.0 92.2 jit_solution(1747652509181664434)
XLA Ops:
  0.0 0.0 copy-start
  0.0 0.8 iota_add_fusion.1
  0.8 0.2 convert_reduce_fusion.1
  1.0 0.6 select_reduce_fusion.1.refs_0_
  1.6 16.8 %synth.1 = f32[16,96,128]{2,1,0:T(8,128)} custom-call(s32[32]{0:T(128)} %select_reduce_fusion.1.refs_0_, f32[1024]{0:T(1024)} %constant.47.clone.refs_1_, f32[6,32,512]{2,1,0:T(8,128)} %bitcast.7, f32[8,512]{1,0:T(8,128)} %constant.45.clone.refs_3_.refs_2_, bf16[128,1024]{1,0:T(8,128)(2,1)} %constant.46.clone.refs_4_, s32[1,1024]{1,0:T(1,128)} %bitcast.4), custom_call_target="tpu_custom_call" | custom-call | flops 15000000512 | bytes 1048576 | tf_op jit(solution)/shard_map/synth/pallas_call | solution.py:635
  18.4 0.0 copy-start.1
  18.4 0.0 copy-start.3
  18.4 0.0 copy-start.4
  18.5 8.9 %all-to-all-start = ((f32[16,96,128]{2,1,0:T(8,128)}), f32[16,96,128]{2,1,0:T(8,128)S(1)}, u32[]{:S(2)}, u32[]{:S(2)}) async-start(f32[16,96,128]{2,1,0:T(8,128)} %synth.1), calls=%async_computation | async-start | bytes 1572864 | tf_op jit(solution)/shard_map/all_to_all | solution.py:633
  27.4 0.0 copy-done.6
  27.4 0.1 lt.46
  27.5 0.5 convert_reduce_fusion
  28.0 0.3 select_reduce_fusion
  28.3 0.1 reshape.188
  28.4 0.0 copy-done
  28.4 0.1 multiply_sine_fusion
  28.5 2.5 %trig.1.refs_4_ = bf16[4,2,2,512,256]{4,3,2,1,0:T(8,128)(2,1)S(1)} custom-call(), custom_call_target="tpu_custom_call" | custom-call | flops 4000000000 | bytes 1048576 | tf_op jit(solution)/shard_map/trig/pallas_call | solution.py:665
  31.0 0.0 copy-start.5
  31.0 1.9 %copy-done.5 = bf16[4,2,2,512,256]{4,3,2,1,0:T(8,128)(2,1)} copy-done((bf16[4,2,2,512,256]{4,3,2,1,0:T(8,128)(2,1)}, bf16[4,2,2,512,256]{4,3,2,1,0:T(8,128)(2,1)S(1)}, u32[]{:S(2)}) %copy-start.5) | copy-done | bytes 4194328
  32.9 14.2 %all-to-all-done.refs_0_ = f32[16,96,128]{2,1,0:T(8,128)S(1)} async-done(((f32[16,96,128]{2,1,0:T(8,128)}), f32[16,96,128]{2,1,0:T(8,128)S(1)}, u32[]{:S(2)}, u32[]{:S(2)}) %all-to-all-start) | async-done | bytes 786464 | tf_op jit(solution)/shard_map/all_to_all | solution.py:633
  47.1 0.1 broadcast_in_dim.54.refs_3_
  47.2 0.1 broadcast_in_dim.34.refs_1_
  47.4 0.0 copy-done.2
  47.4 7.0 %grid.1 = f32[16,104,128]{2,1,0:T(8,128)} custom-call(f32[16,96,128]{2,1,0:T(8,128)S(1)} %all-to-all-done.refs_0_, s32[512,128]{1,0:T(8,128)S(1)} %broadcast_in_dim.34.refs_1_, f32[64,2048]{1,0:T(8,128)S(1)} %bitcast.6, f32[64,128]{1,0:T(8,128)S(1)} %broadcast_in_dim.54.refs_3_, bf16[4,2,2,512,256]{4,3,2,1,0:T(8,128)(2,1)} %copy-done.5), custom_call_target="tpu_custom_call" | custom-call | flops 8000000000 | bytes 1048576 | tf_op jit(solution)/shard_map/grid/pallas_call | solution.py:682
  54.4 4.9 %all-to-all-start.1 = ((f32[16,104,128]{2,1,0:T(8,128)}), f32[16,104,128]{2,1,0:T(8,128)S(1)}, u32[]{:S(2)}, u32[]{:S(2)}) async-start(f32[16,104,128]{2,1,0:T(8,128)} %grid.1), calls=%async_computation.1 | async-start | bytes 1703936 | tf_op jit(solution)/shard_map/all_to_all | solution.py:633
  59.3 0.0 copy-done.1
  59.3 0.0 copy-done.3
  59.3 0.0 copy-done.4
  59.3 11.8 %table.1 = (bf16[4,8,512,1024]{3,2,1,0:T(8,128)(2,1)}, f32[32,512]{1,0:T(8,128)S(1)}) custom-call(s32[32]{0:T(128)S(1)} %copy-done.1, f32[1024]{0:T(1024)S(1)} %copy-done.4, f32[8,512]{1,0:T(8,128)S(1)} %copy-done.3), custom_call_target="tpu_custom_call" | custom-call | flops 12000000000 | bytes 1048576 | tf_op jit(solution)/shard_map/table/pallas_call | solution.py:702
  71.1 7.9 %all-to-all-done.1.refs_1_ = f32[16,104,128]{2,1,0:T(8,128)S(1)} async-done(((f32[16,104,128]{2,1,0:T(8,128)}), f32[16,104,128]{2,1,0:T(8,128)S(1)}, u32[]{:S(2)}, u32[]{:S(2)}) %all-to-all-start.1) | async-done | bytes 852000 | tf_op jit(solution)/shard_map/all_to_all | solution.py:633
  79.0 0.2 broadcast_in_dim.55.refs_2_
  79.2 12.8 %analyze.1 = f32[6,32,512]{2,1,0:T(8,128)} custom-call(s32[32]{0:T(128)S(1)} %copy-done.1, f32[16,104,128]{2,1,0:T(8,128)S(1)} %all-to-all-done.1.refs_1_, s32[1024,128]{1,0:T(8,128)S(1)} %broadcast_in_dim.55.refs_2_, s32[1,1024]{1,0:T(1,128)S(1)} %bitcast.5, f32[32,512]{1,0:T(8,128)S(1)} %get-tuple-element.7.refs_4_, ...), custom_call_target="tpu_custom_call" | custom-call | flops 8999999488 | bytes 1048576 | tf_op jit(solution)/shard_map/analyze/pallas_call | solution.py:717
  (4 shorter events, 0.0 us)
Async XLA Ops:
  0.0 27.4 %copy-start.6 = (s32[512]{0:T(512)S(1)}, s32[512]{0:T(512)}, u32[]{:S(2)}) copy-start(s32[512]{0:T(512)} %param.10) | copy-start | bytes 6148
  0.0 28.4 %copy-start = (s32[1024]{0:T(1024)S(1)}, s32[1024]{0:T(1024)}, u32[]{:S(2)}) copy-start(s32[1024]{0:T(1024)} %param.9) | copy-start | bytes 12292
  1.6 45.7 %copy-start.2 = (f32[1,64,2048]{2,1,0:T(8,128)S(1)}, f32[1,64,2048]{2,1,0:T(8,128)}, u32[]{:S(2)}) copy-start(f32[1,64,2048]{2,1,0:T(8,128)} %param.8) | copy-start | bytes 1572868
  18.4 40.9 %copy-start.1 = (s32[32]{0:T(128)S(1)}, s32[32]{0:T(128)}, u32[]{:S(2)}) copy-start(s32[32]{0:T(128)} %select_reduce_fusion.1.refs_0_) | copy-start | bytes 388
  18.4 40.9 %copy-start.3 = (f32[8,512]{1,0:T(8,128)S(1)}, f32[8,512]{1,0:T(8,128)}, u32[]{:S(2)}) copy-start(f32[8,512]{1,0:T(8,128)} %constant.45.clone.refs_3_.refs_2_) | copy-start | bytes 49156
  18.4 40.9 %copy-start.4 = (f32[1024]{0:T(1024)S(1)}, f32[1024]{0:T(1024)}, u32[]{:S(2)}) copy-start(f32[1024]{0:T(1024)} %constant.47.clone.refs_1_) | copy-start | bytes 12292
  18.5 28.7 %all-to-all-start = ((f32[16,96,128]{2,1,0:T(8,128)}), f32[16,96,128]{2,1,0:T(8,128)S(1)}, u32[]{:S(2)}, u32[]{:S(2)}) async-start(f32[16,96,128]{2,1,0:T(8,128)} %synth.1), calls=%async_computation | async-start | bytes 1572864 | tf_op jit(solution)/shard_map/all_to_all | solution.py:633
  31.0 1.9 %copy-start.5 = (bf16[4,2,2,512,256]{4,3,2,1,0:T(8,128)(2,1)}, bf16[4,2,2,512,256]{4,3,2,1,0:T(8,128)(2,1)S(1)}, u32[]{:S(2)}) copy-start(bf16[4,2,2,512,256]{4,3,2,1,0:T(8,128)(2,1)S(1)} %trig.1.refs_4_) | copy-start | bytes 12582916
  54.4 24.7 %all-to-all-start.1 = ((f32[16,104,128]{2,1,0:T(8,128)}), f32[16,104,128]{2,1,0:T(8,128)S(1)}, u32[]{:S(2)}, u32[]{:S(2)}) async-start(f32[16,104,128]{2,1,0:T(8,128)} %grid.1), calls=%async_computation.1 | async-start | bytes 1703936 | tf_op jit(solution)/shard_map/all_to_all | solution.py:633

commit v10 on v9

--- a/solution.py
+++ b/solution.py
@@ -213,20 +213,16 @@
             )
 
         def add_products(step, high_ref, low_ref):
-            def high_part(parity, columns):
+            def part(parity, columns):
                 lhs = lhs_ref[step, :, parity * width : (parity + 1) * width]
                 first = dot(lhs, high_ref[parity, :, columns])
-                acc_ref[block, parity, :, columns] += first[:ROWS] + first[ROWS:]
-
-            def low_part(parity, columns):
-                lhs = lhs_ref[step, :ROWS, parity * width : (parity + 1) * width]
-                acc_ref[block, parity, :, columns] += dot(lhs, low_ref[parity, :, columns])
+                second = dot(lhs[:ROWS], low_ref[parity, :, columns])
+                acc_ref[block, parity, :, columns] += first[:ROWS] + first[ROWS:] + second
 
             return [
                 functools.partial(part, parity, slice(at, at + KTILE))
                 for parity in range(2)
                 for at in range(0, HALF, KTILE)
-                for part in (high_part, low_part)
             ]
 
         def two_chunks(guard, pair, carry):
@@ -419,12 +415,19 @@
             some_chunks(first, 1)
             return inner
 
-        def two_chunks(pair, inner):
-            some_chunks(2 * pair, 2)
+        even = (first + 1) // 2
+
+        def two_chunks(unused, inner):
+            some_chunks(2 * even, 2)
             return inner
 
+        def four_chunks(group, inner):
+            some_chunks(4 * group, 4)
+            return inner
+
         lax.fori_loop(0, first & 1, lone_chunk, 0)
-        lax.fori_loop((first + 1) // 2, chunks // 2, two_chunks, 0)
+        lax.fori_loop(0, even & 1, two_chunks, 0)
+        lax.fori_loop((even + 1) // 2, chunks // 4, four_chunks, 0)
         return unused
 
     lax.fori_loop(0, blocks, one_block, 0)

time: 91.6 us -> 90.6 us (0.989)
  Pallas kernels: 50.8 us -> 48.2 us
    pallas_call x1, Pallas kernels: 12.8 us -> 11.8 us  [per_device(): pl.pallas_call(lambda *refs: analyze_kernel(dims, chunk_rows, *refs), out...]
where the time goes in v10:
time: 90.6 us; the launch traced here: 90.3 us
  Pallas kernels  48.2 us (53%)
  waiting for transfers between devices  22.9 us (25%)
  starting transfers between devices  13.8 us (15%)
  other arithmetic  2.57 us (3%)
  local copies, waits for them, and re-layouts  2.5 us (3%)
    all_to_all x2, waiting for transfers between devices, exchange(): lax.all_to_all(value, 'band', split_axis=0, concat_axis=0, tiled=True)  22.9 us
    pallas_call x1, Pallas kernels, per_device(): pl.pallas_call(lambda *refs: synth_kernel(dims, *refs), out_shape=jax.Sha...  16 us
    all_to_all x2, starting transfers between devices, exchange(): lax.all_to_all(value, 'band', split_axis=0, concat_axis=0, tiled=True)  13.8 us
    pallas_call x1, Pallas kernels, per_device(): pl.pallas_call(lambda *refs: analyze_kernel(dims, chunk_rows, *refs), out...  11.8 us
    pallas_call x1, Pallas kernels, per_device(): pl.pallas_call(lambda *refs: table_kernel(blocks, *refs), out_shape=[jax....  11 us
    pallas_call x1, Pallas kernels, per_device(): pl.pallas_call(lambda *refs: grid_kernel(grid_dims, *refs), out_shape=jax...  6.98 us
    pallas_call x1, Pallas kernels, per_device(): pl.pallas_call(trig_kernel, out_shape=jax.ShapeDtypeStruct(trig_shape, BF...  2.47 us
    unnamed x14, local copies, waits for them, and re-layouts  1.96 us
  transfers between devices with their start and end apart: 2, of which 2 were waited for; matrix products, arithmetic and copies ran while one was open for 1% of the time, Pallas kernels for 15%

profile of v10, /device:TPU:0, one launch (start us, length us, event | category | flops | bytes accessed | tf_op | source)
XLA Modules:
  0.0 90.3 jit_solution(9733331273805143492)
XLA Ops:
  0.0 0.0 copy-start.6
  0.0 0.8 iota_add_fusion.1
  0.8 0.2 convert_reduce_fusion.1
  1.0 0.6 select_reduce_fusion.1.refs_0_
  1.6 16.0 %synth.1 = f32[16,96,128]{2,1,0:T(8,128)} custom-call(s32[32]{0:T(128)} %select_reduce_fusion.1.refs_0_, f32[1024]{0:T(1024)} %constant.47.clone.refs_1_, f32[6,32,512]{2,1,0:T(8,128)} %bitcast.7, f32[8,512]{1,0:T(8,128)} %constant.45.clone.refs_3_.refs_2_, bf16[128,1024]{1,0:T(8,128)(2,1)} %constant.46.clone.refs_4_, s32[1,1024]{1,0:T(1,128)} %bitcast.4), custom_call_target="tpu_custom_call" | custom-call | flops 15000000512 | bytes 1048576 | tf_op jit(solution)/shard_map/synth/pallas_call | solution.py:638
  17.6 0.0 copy-start.1
  17.6 0.0 copy-start.3
  17.6 0.0 copy-start.4
  17.6 8.8 %all-to-all-start = ((f32[16,96,128]{2,1,0:T(8,128)}), f32[16,96,128]{2,1,0:T(8,128)S(1)}, u32[]{:S(2)}, u32[]{:S(2)}) async-start(f32[16,96,128]{2,1,0:T(8,128)} %synth.1), calls=%async_computation | async-start | bytes 1572864 | tf_op jit(solution)/shard_map/all_to_all | solution.py:636
  26.5 0.0 copy-done.6
  26.5 0.1 lt.46
  26.6 0.5 convert_reduce_fusion
  27.1 0.3 select_reduce_fusion
  27.4 0.1 reshape.188
  27.5 0.0 copy-done
  27.5 0.1 multiply_sine_fusion
  27.6 2.5 %trig.1.refs_4_ = bf16[4,2,2,512,256]{4,3,2,1,0:T(8,128)(2,1)S(1)} custom-call(), custom_call_target="tpu_custom_call" | custom-call | flops 4000000000 | bytes 1048576 | tf_op jit(solution)/shard_map/trig/pallas_call | solution.py:668
  30.1 0.0 copy-start.5
  30.1 1.9 %copy-done.5 = bf16[4,2,2,512,256]{4,3,2,1,0:T(8,128)(2,1)} copy-done((bf16[4,2,2,512,256]{4,3,2,1,0:T(8,128)(2,1)}, bf16[4,2,2,512,256]{4,3,2,1,0:T(8,128)(2,1)S(1)}, u32[]{:S(2)}) %copy-start.5) | copy-done | bytes 4194328
  32.0 14.2 %all-to-all-done.refs_0_ = f32[16,96,128]{2,1,0:T(8,128)S(1)} async-done(((f32[16,96,128]{2,1,0:T(8,128)}), f32[16,96,128]{2,1,0:T(8,128)S(1)}, u32[]{:S(2)}, u32[]{:S(2)}) %all-to-all-start) | async-done | bytes 786464 | tf_op jit(solution)/shard_map/all_to_all | solution.py:636
  46.2 0.1 broadcast_in_dim.54.refs_3_
  46.3 0.1 broadcast_in_dim.34.refs_1_
  46.5 0.0 copy-done.2
  46.5 7.0 %grid.1 = f32[16,104,128]{2,1,0:T(8,128)} custom-call(f32[16,96,128]{2,1,0:T(8,128)S(1)} %all-to-all-done.refs_0_, s32[512,128]{1,0:T(8,128)S(1)} %broadcast_in_dim.34.refs_1_, f32[64,2048]{1,0:T(8,128)S(1)} %bitcast.6, f32[64,128]{1,0:T(8,128)S(1)} %broadcast_in_dim.54.refs_3_, bf16[4,2,2,512,256]{4,3,2,1,0:T(8,128)(2,1)} %copy-done.5), custom_call_target="tpu_custom_call" | custom-call | flops 8000000000 | bytes 1048576 | tf_op jit(solution)/shard_map/grid/pallas_call | solution.py:685
  53.5 4.9 %all-to-all-start.1 = ((f32[16,104,128]{2,1,0:T(8,128)}), f32[16,104,128]{2,1,0:T(8,128)S(1)}, u32[]{:S(2)}, u32[]{:S(2)}) async-start(f32[16,104,128]{2,1,0:T(8,128)} %grid.1), calls=%async_computation.1 | async-start | bytes 1703936 | tf_op jit(solution)/shard_map/all_to_all | solution.py:636
  58.4 0.0 copy-done.1
  58.4 0.0 copy-done.3
  58.4 0.0 copy-done.4
  58.4 11.0 %table.1 = (bf16[4,8,512,1024]{3,2,1,0:T(8,128)(2,1)}, f32[32,512]{1,0:T(8,128)S(1)}) custom-call(s32[32]{0:T(128)S(1)} %copy-done.1, f32[1024]{0:T(1024)S(1)} %copy-done.4, f32[8,512]{1,0:T(8,128)S(1)} %copy-done.3), custom_call_target="tpu_custom_call" | custom-call | flops 12000000000 | bytes 1048576 | tf_op jit(solution)/shard_map/table/pallas_call | solution.py:705
  69.4 8.7 %all-to-all-done.1.refs_1_ = f32[16,104,128]{2,1,0:T(8,128)S(1)} async-done(((f32[16,104,128]{2,1,0:T(8,128)}), f32[16,104,128]{2,1,0:T(8,128)S(1)}, u32[]{:S(2)}, u32[]{:S(2)}) %all-to-all-start.1) | async-done | bytes 852000 | tf_op jit(solution)/shard_map/all_to_all | solution.py:636
  78.1 0.2 broadcast_in_dim.55.refs_2_
  78.3 11.8 %analyze.1 = f32[6,32,512]{2,1,0:T(8,128)} custom-call(s32[32]{0:T(128)S(1)} %copy-done.1, f32[16,104,128]{2,1,0:T(8,128)S(1)} %all-to-all-done.1.refs_1_, s32[1024,128]{1,0:T(8,128)S(1)} %broadcast_in_dim.55.refs_2_, s32[1,1024]{1,0:T(1,128)S(1)} %bitcast.5, f32[32,512]{1,0:T(8,128)S(1)} %get-tuple-element.7.refs_4_, ...), custom_call_target="tpu_custom_call" | custom-call | flops 8999999488 | bytes 1048576 | tf_op jit(solution)/shard_map/analyze/pallas_call | solution.py:720
  (4 shorter events, 0.0 us)
Async XLA Ops:
  0.0 26.5 %copy-start.6 = (s32[512]{0:T(512)S(1)}, s32[512]{0:T(512)}, u32[]{:S(2)}) copy-start(s32[512]{0:T(512)} %param.10) | copy-start | bytes 6148
  0.0 27.5 %copy-start = (s32[1024]{0:T(1024)S(1)}, s32[1024]{0:T(1024)}, u32[]{:S(2)}) copy-start(s32[1024]{0:T(1024)} %param.9) | copy-start | bytes 12292
  1.6 44.8 %copy-start.2 = (f32[1,64,2048]{2,1,0:T(8,128)S(1)}, f32[1,64,2048]{2,1,0:T(8,128)}, u32[]{:S(2)}) copy-start(f32[1,64,2048]{2,1,0:T(8,128)} %param.8) | copy-start | bytes 1572868
  17.6 40.8 %copy-start.1 = (s32[32]{0:T(128)S(1)}, s32[32]{0:T(128)}, u32[]{:S(2)}) copy-start(s32[32]{0:T(128)} %select_reduce_fusion.1.refs_0_) | copy-start | bytes 388
  17.6 40.8 %copy-start.3 = (f32[8,512]{1,0:T(8,128)S(1)}, f32[8,512]{1,0:T(8,128)}, u32[]{:S(2)}) copy-start(f32[8,512]{1,0:T(8,128)} %constant.45.clone.refs_3_.refs_2_) | copy-start | bytes 49156
  17.6 40.8 %copy-start.4 = (f32[1024]{0:T(1024)S(1)}, f32[1024]{0:T(1024)}, u32[]{:S(2)}) copy-start(f32[1024]{0:T(1024)} %constant.47.clone.refs_1_) | copy-start | bytes 12292
  17.6 28.6 %all-to-all-start = ((f32[16,96,128]{2,1,0:T(8,128)}), f32[16,96,128]{2,1,0:T(8,128)S(1)}, u32[]{:S(2)}, u32[]{:S(2)}) async-start(f32[16,96,128]{2,1,0:T(8,128)} %synth.1), calls=%async_computation | async-start | bytes 1572864 | tf_op jit(solution)/shard_map/all_to_all | solution.py:636
  30.1 1.9 %copy-start.5 = (bf16[4,2,2,512,256]{4,3,2,1,0:T(8,128)(2,1)}, bf16[4,2,2,512,256]{4,3,2,1,0:T(8,128)(2,1)S(1)}, u32[]{:S(2)}) copy-start(bf16[4,2,2,512,256]{4,3,2,1,0:T(8,128)(2,1)S(1)} %trig.1.refs_4_) | copy-start | bytes 12582916
  53.5 24.7 %all-to-all-start.1 = ((f32[16,104,128]{2,1,0:T(8,128)}), f32[16,104,128]{2,1,0:T(8,128)S(1)}, u32[]{:S(2)}, u32[]{:S(2)}) async-start(f32[16,104,128]{2,1,0:T(8,128)} %grid.1), calls=%async_computation.1 | async-start | bytes 1703936 | tf_op jit(solution)/shard_map/all_to_all | solution.py:636

commit v11 on v10

--- a/solution.py
+++ b/solution.py
@@ -151,7 +151,7 @@
 def synth_kernel(
     dims, slots_ref, scalars_in, spec_in, rows_in, spread_in, latitude_in,
     out_ref, scalars_ref, spec_ref, rows_ref, spread_ref, latitude_ref, sems,
-    start_ref, before_ref, within_ref, lhs_ref, high_a, low_a, high_b, low_b, acc_ref, fold_ref, coeff_ref,
+    start_ref, before_ref, within_ref, lhs_ref, high_a, low_a, high_b, low_b, acc_ref, fold_ref, coeff_ref, sent_ref, out_sems,
 ):
     bands, row_count, modes, blocks, tiles = dims
     pairs = (
@@ -254,26 +254,32 @@
     high, low = split_two(acc_ref[...].reshape(blocks * 2 * ROWS, HALF))
     moved = dot(jnp.concatenate([high, low], 0), fold_ref[...])
     moved = moved[: blocks * 2 * ROWS] + moved[blocks * 2 * ROWS :]
+    lanes = []
     for block in range(blocks):
         orders = block_orders(slots_ref, block * BLK)[0][:, :1]
         sign = jnp.tile(1.0 - 2.0 * (orders % 2).astype(F32), (CHAN, 1))
         even = moved[block * 2 * ROWS : block * 2 * ROWS + ROWS]
         odd = moved[block * 2 * ROWS + ROWS : (block + 1) * 2 * ROWS]
-        values = jnp.where(south, sign * (even - odd), even + odd)
-        for d in range(bands):
+        lanes.append(jnp.where(south, sign * (even - odd), even + odd))
+    copies = []
+    for d in range(bands):
+        columns = slice(d * row_count, (d + 1) * row_count)
+        for block in range(blocks):
             parts = []
             for kind in range(2):
                 for field in range(FIELDS):
                     c = field * 2 + kind
-                    parts.append(
-                        values[c * BLK : (c + 1) * BLK, d * row_count : (d + 1) * row_count]
-                    )
+                    parts.append(lanes[block][c * BLK : (c + 1) * BLK, columns])
             if CHAN * row_count < tiles * LANES:
                 parts.append(jnp.zeros((BLK, tiles * LANES - CHAN * row_count), F32))
             joined = jnp.concatenate(parts, 1)
             for t in range(tiles):
                 at = slice((t * blocks + block) * BLK, (t * blocks + block + 1) * BLK)
-                out_ref[d, at, :] = joined[:, t * LANES : (t + 1) * LANES]
+                sent_ref[d, at, :] = joined[:, t * LANES : (t + 1) * LANES]
+        copies.append(pltpu.make_async_copy(sent_ref.at[d], out_ref.at[d], out_sems.at[d]))
+        copies[-1].start()
+    for copy in copies:
+        copy.wait()
 
 
 def table_kernel(
@@ -639,7 +645,7 @@
         lambda *refs: synth_kernel(dims, *refs),
         out_shape=jax.ShapeDtypeStruct((bands, chunk_rows, LANES), F32),
         in_specs=[SMEM] + [HBM] * 5,
-        out_specs=VMEM,
+        out_specs=HBM,
         scratch_shapes=[
             pltpu.SMEM(scalars.shape, F32),
             pltpu.VMEM(coeffs.shape, F32),
@@ -655,6 +661,8 @@
             pltpu.VMEM((blocks, 2, ROWS, HALF), F32),
             pltpu.VMEM((HALF, NLAT), BF),
             pltpu.VMEM((CHAN, BLK, DEG), F32),
+            pltpu.VMEM((bands, chunk_rows, LANES), F32),
+            pltpu.SemaphoreType.DMA((bands,)),
         ],
         compiler_params=pltpu.CompilerParams(vmem_limit_bytes=62 * 2**20),
         cost_estimate=work(15),

time: 90.6 us -> 90 us (level)
  no operation moved by 1% of the time
where the time goes in v11:
time: 90 us; the launch traced here: 89.9 us
  Pallas kernels  47.3 us (53%)
  waiting for transfers between devices  23.3 us (26%)
  starting transfers between devices  13.9 us (15%)
  other arithmetic  2.57 us (3%)
  local copies, waits for them, and re-layouts  2.5 us (3%)
    all_to_all x2, waiting for transfers between devices, exchange(): lax.all_to_all(value, 'band', split_axis=0, concat_axis=0, tiled=True)  23.3 us
    pallas_call x1, Pallas kernels, per_device(): pl.pallas_call(lambda *refs: synth_kernel(dims, *refs), out_shape=jax.Sha...  15.9 us
    all_to_all x2, starting transfers between devices, exchange(): lax.all_to_all(value, 'band', split_axis=0, concat_axis=0, tiled=True)  13.9 us
    pallas_call x1, Pallas kernels, per_device(): pl.pallas_call(lambda *refs: analyze_kernel(dims, chunk_rows, *refs), out...  11.3 us
    pallas_call x1, Pallas kernels, per_device(): pl.pallas_call(lambda *refs: table_kernel(blocks, *refs), out_shape=[jax....  10.7 us
    pallas_call x1, Pallas kernels, per_device(): pl.pallas_call(lambda *refs: grid_kernel(grid_dims, *refs), out_shape=jax...  6.98 us
    pallas_call x1, Pallas kernels, per_device(): pl.pallas_call(trig_kernel, out_shape=jax.ShapeDtypeStruct(trig_shape, BF...  2.47 us
    unnamed x14, local copies, waits for them, and re-layouts  1.96 us
  transfers between devices with their start and end apart: 2, of which 2 were waited for; matrix products, arithmetic and copies ran while one was open for 1% of the time, Pallas kernels for 15%

profile of v11, /device:TPU:0, one launch (start us, length us, event | category | flops | bytes accessed | tf_op | source)
XLA Modules:
  0.0 89.9 jit_solution(14469845613909939298)
XLA Ops:
  0.0 0.0 copy-start.6
  0.0 0.8 iota_add_fusion.1
  0.8 0.2 convert_reduce_fusion.1
  1.0 0.6 select_reduce_fusion.1.refs_0_
  1.6 15.9 %synth.1 = f32[16,96,128]{2,1,0:T(8,128)} custom-call(s32[32]{0:T(128)} %select_reduce_fusion.1.refs_0_, f32[1024]{0:T(1024)} %constant.47.clone.refs_1_, f32[6,32,512]{2,1,0:T(8,128)} %bitcast.7, f32[8,512]{1,0:T(8,128)} %constant.45.clone.refs_3_.refs_2_, bf16[128,1024]{1,0:T(8,128)(2,1)} %constant.46.clone.refs_4_, s32[1,1024]{1,0:T(1,128)} %bitcast.4), custom_call_target="tpu_custom_call" | custom-call | flops 15000000512 | bytes 1048576 | tf_op jit(solution)/shard_map/synth/pallas_call | solution.py:644
  17.6 0.0 copy-start.1
  17.6 0.0 copy-start.3
  17.6 0.0 copy-start.4
  17.6 8.9 %all-to-all-start = ((f32[16,96,128]{2,1,0:T(8,128)}), f32[16,96,128]{2,1,0:T(8,128)S(1)}, u32[]{:S(2)}, u32[]{:S(2)}) async-start(f32[16,96,128]{2,1,0:T(8,128)} %synth.1), calls=%async_computation | async-start | bytes 1572864 | tf_op jit(solution)/shard_map/all_to_all | solution.py:642
  26.5 0.0 copy-done.6
  26.5 0.1 lt.46
  26.6 0.5 convert_reduce_fusion
  27.1 0.3 select_reduce_fusion
  27.4 0.1 reshape.188
  27.5 0.0 copy-done
  27.5 0.1 multiply_sine_fusion
  27.7 2.5 %trig.1.refs_4_ = bf16[4,2,2,512,256]{4,3,2,1,0:T(8,128)(2,1)S(1)} custom-call(), custom_call_target="tpu_custom_call" | custom-call | flops 4000000000 | bytes 1048576 | tf_op jit(solution)/shard_map/trig/pallas_call | solution.py:676
  30.1 0.0 copy-start.5
  30.1 1.9 %copy-done.5 = bf16[4,2,2,512,256]{4,3,2,1,0:T(8,128)(2,1)} copy-done((bf16[4,2,2,512,256]{4,3,2,1,0:T(8,128)(2,1)}, bf16[4,2,2,512,256]{4,3,2,1,0:T(8,128)(2,1)S(1)}, u32[]{:S(2)}) %copy-start.5) | copy-done | bytes 4194328
  32.1 14.2 %all-to-all-done.refs_0_ = f32[16,96,128]{2,1,0:T(8,128)S(1)} async-done(((f32[16,96,128]{2,1,0:T(8,128)}), f32[16,96,128]{2,1,0:T(8,128)S(1)}, u32[]{:S(2)}, u32[]{:S(2)}) %all-to-all-start) | async-done | bytes 786464 | tf_op jit(solution)/shard_map/all_to_all | solution.py:642
  46.3 0.1 broadcast_in_dim.54.refs_3_
  46.4 0.1 broadcast_in_dim.34.refs_1_
  46.5 0.0 copy-done.2
  46.5 7.0 %grid.1 = f32[16,104,128]{2,1,0:T(8,128)} custom-call(f32[16,96,128]{2,1,0:T(8,128)S(1)} %all-to-all-done.refs_0_, s32[512,128]{1,0:T(8,128)S(1)} %broadcast_in_dim.34.refs_1_, f32[64,2048]{1,0:T(8,128)S(1)} %bitcast.6, f32[64,128]{1,0:T(8,128)S(1)} %broadcast_in_dim.54.refs_3_, bf16[4,2,2,512,256]{4,3,2,1,0:T(8,128)(2,1)} %copy-done.5), custom_call_target="tpu_custom_call" | custom-call | flops 8000000000 | bytes 1048576 | tf_op jit(solution)/shard_map/grid/pallas_call | solution.py:693
  53.5 4.9 %all-to-all-start.1 = ((f32[16,104,128]{2,1,0:T(8,128)}), f32[16,104,128]{2,1,0:T(8,128)S(1)}, u32[]{:S(2)}, u32[]{:S(2)}) async-start(f32[16,104,128]{2,1,0:T(8,128)} %grid.1), calls=%async_computation.1 | async-start | bytes 1703936 | tf_op jit(solution)/shard_map/all_to_all | solution.py:642
  58.4 0.0 copy-done.1
  58.4 0.0 copy-done.3
  58.4 0.0 copy-done.4
  58.4 10.7 %table.1 = (bf16[4,8,512,1024]{3,2,1,0:T(8,128)(2,1)}, f32[32,512]{1,0:T(8,128)S(1)}) custom-call(s32[32]{0:T(128)S(1)} %copy-done.1, f32[1024]{0:T(1024)S(1)} %copy-done.4, f32[8,512]{1,0:T(8,128)S(1)} %copy-done.3), custom_call_target="tpu_custom_call" | custom-call | flops 12000000000 | bytes 1048576 | tf_op jit(solution)/shard_map/table/pallas_call | solution.py:713
  69.1 9.0 %all-to-all-done.1.refs_1_ = f32[16,104,128]{2,1,0:T(8,128)S(1)} async-done(((f32[16,104,128]{2,1,0:T(8,128)}), f32[16,104,128]{2,1,0:T(8,128)S(1)}, u32[]{:S(2)}, u32[]{:S(2)}) %all-to-all-start.1) | async-done | bytes 852000 | tf_op jit(solution)/shard_map/all_to_all | solution.py:642
  78.2 0.2 broadcast_in_dim.55.refs_2_
  78.4 11.3 %analyze.1 = f32[6,32,512]{2,1,0:T(8,128)} custom-call(s32[32]{0:T(128)S(1)} %copy-done.1, f32[16,104,128]{2,1,0:T(8,128)S(1)} %all-to-all-done.1.refs_1_, s32[1024,128]{1,0:T(8,128)S(1)} %broadcast_in_dim.55.refs_2_, s32[1,1024]{1,0:T(1,128)S(1)} %bitcast.5, f32[32,512]{1,0:T(8,128)S(1)} %get-tuple-element.7.refs_4_, ...), custom_call_target="tpu_custom_call" | custom-call | flops 8999999488 | bytes 1048576 | tf_op jit(solution)/shard_map/analyze/pallas_call | solution.py:728
  (4 shorter events, 0.0 us)
Async XLA Ops:
  0.0 26.5 %copy-start.6 = (s32[512]{0:T(512)S(1)}, s32[512]{0:T(512)}, u32[]{:S(2)}) copy-start(s32[512]{0:T(512)} %param.10) | copy-start | bytes 6148
  0.0 27.5 %copy-start = (s32[1024]{0:T(1024)S(1)}, s32[1024]{0:T(1024)}, u32[]{:S(2)}) copy-start(s32[1024]{0:T(1024)} %param.9) | copy-start | bytes 12292
  1.6 44.8 %copy-start.2 = (f32[1,64,2048]{2,1,0:T(8,128)S(1)}, f32[1,64,2048]{2,1,0:T(8,128)}, u32[]{:S(2)}) copy-start(f32[1,64,2048]{2,1,0:T(8,128)} %param.8) | copy-start | bytes 1572868
  17.6 40.9 %copy-start.1 = (s32[32]{0:T(128)S(1)}, s32[32]{0:T(128)}, u32[]{:S(2)}) copy-start(s32[32]{0:T(128)} %select_reduce_fusion.1.refs_0_) | copy-start | bytes 388
  17.6 40.9 %copy-start.3 = (f32[8,512]{1,0:T(8,128)S(1)}, f32[8,512]{1,0:T(8,128)}, u32[]{:S(2)}) copy-start(f32[8,512]{1,0:T(8,128)} %constant.45.clone.refs_3_.refs_2_) | copy-start | bytes 49156
  17.6 40.9 %copy-start.4 = (f32[1024]{0:T(1024)S(1)}, f32[1024]{0:T(1024)}, u32[]{:S(2)}) copy-start(f32[1024]{0:T(1024)} %constant.47.clone.refs_1_) | copy-start | bytes 12292
  17.6 28.7 %all-to-all-start = ((f32[16,96,128]{2,1,0:T(8,128)}), f32[16,96,128]{2,1,0:T(8,128)S(1)}, u32[]{:S(2)}, u32[]{:S(2)}) async-start(f32[16,96,128]{2,1,0:T(8,128)} %synth.1), calls=%async_computation | async-start | bytes 1572864 | tf_op jit(solution)/shard_map/all_to_all | solution.py:642
  30.1 1.9 %copy-start.5 = (bf16[4,2,2,512,256]{4,3,2,1,0:T(8,128)(2,1)}, bf16[4,2,2,512,256]{4,3,2,1,0:T(8,128)(2,1)S(1)}, u32[]{:S(2)}) copy-start(bf16[4,2,2,512,256]{4,3,2,1,0:T(8,128)(2,1)S(1)} %trig.1.refs_4_) | copy-start | bytes 12582916
  53.5 24.7 %all-to-all-start.1 = ((f32[16,104,128]{2,1,0:T(8,128)}), f32[16,104,128]{2,1,0:T(8,128)S(1)}, u32[]{:S(2)}, u32[]{:S(2)}) async-start(f32[16,104,128]{2,1,0:T(8,128)} %grid.1), calls=%async_computation.1 | async-start | bytes 1703936 | tf_op jit(solution)/shard_map/all_to_all | solution.py:642

commit v12 on v10

--- a/solution.py
+++ b/solution.py
@@ -220,9 +220,9 @@
                 acc_ref[block, parity, :, columns] += first[:ROWS] + first[ROWS:] + second
 
             return [
-                functools.partial(part, parity, slice(at, at + KTILE))
+                functools.partial(part, parity, slice(at, at + 2 * KTILE))
                 for parity in range(2)
-                for at in range(0, HALF, KTILE)
+                for at in range(0, HALF, 2 * KTILE)
             ]
 
         def two_chunks(guard, pair, carry):

time: 90.6 us -> 91.1 us (level)
  Pallas kernels: 48.2 us -> 51.8 us
  starting transfers between devices: 13.8 us -> 12.2 us
  waiting for transfers between devices: 22.9 us -> 21.8 us
    all_to_all x2, starting transfers between devices: 13.8 us -> 12.2 us  [exchange(): lax.all_to_all(value, 'band', split_axis=0, concat_axis=0, tiled=True)]
    pallas_call x1, Pallas kernels: 16 us -> 17.2 us  [per_device(): pl.pallas_call(lambda *refs: synth_kernel(dims, *refs), out_shape=jax.Sha...]
    all_to_all x2, waiting for transfers between devices: 22.9 us -> 21.8 us  [exchange(): lax.all_to_all(value, 'band', split_axis=0, concat_axis=0, tiled=True)]
    pallas_call x1, Pallas kernels: 11 us -> 12.2 us  [per_device(): pl.pallas_call(lambda *refs: table_kernel(blocks, *refs), out_shape=[jax....]
    pallas_call x1, Pallas kernels: 11.8 us -> 12.9 us  [per_device(): pl.pallas_call(lambda *refs: analyze_kernel(dims, chunk_rows, *refs), out...]
  transfers between devices with their start and end apart: 2 -> 2, of which waited for: 2 -> 2; matrix products, arithmetic and copies ran while one was open for 1% -> 1% of each run, Pallas kernels for 15% -> 16%
where the time goes in v12:
time: 91.1 us; the launch traced here: 91.2 us
  Pallas kernels  51.8 us (57%)
  waiting for transfers between devices  21.8 us (24%)
  starting transfers between devices  12.2 us (13%)
  other arithmetic  2.57 us (3%)
  local copies, waits for them, and re-layouts  2.5 us (3%)
    all_to_all x2, waiting for transfers between devices, exchange(): lax.all_to_all(value, 'band', split_axis=0, concat_axis=0, tiled=True)  21.8 us
    pallas_call x1, Pallas kernels, per_device(): pl.pallas_call(lambda *refs: synth_kernel(dims, *refs), out_shape=jax.Sha...  17.2 us
    pallas_call x1, Pallas kernels, per_device(): pl.pallas_call(lambda *refs: analyze_kernel(dims, chunk_rows, *refs), out...  12.9 us
    all_to_all x2, starting transfers between devices, exchange(): lax.all_to_all(value, 'band', split_axis=0, concat_axis=0, tiled=True)  12.2 us
    pallas_call x1, Pallas kernels, per_device(): pl.pallas_call(lambda *refs: table_kernel(blocks, *refs), out_shape=[jax....  12.2 us
    pallas_call x1, Pallas kernels, per_device(): pl.pallas_call(lambda *refs: grid_kernel(grid_dims, *refs), out_shape=jax...  6.98 us
    pallas_call x1, Pallas kernels, per_device(): pl.pallas_call(trig_kernel, out_shape=jax.ShapeDtypeStruct(trig_shape, BF...  2.47 us
    unnamed x14, local copies, waits for them, and re-layouts  1.96 us
  transfers between devices with their start and end apart: 2, of which 2 were waited for; matrix products, arithmetic and copies ran while one was open for 1% of the time, Pallas kernels for 16%

profile of v12, /device:TPU:0, one launch (start us, length us, event | category | flops | bytes accessed | tf_op | source)
XLA Modules:
  0.0 91.2 jit_solution(6348121486223261274)
XLA Ops:
  0.0 0.0 copy-start.6
  0.0 0.8 iota_add_fusion.1
  0.8 0.2 convert_reduce_fusion.1
  1.0 0.6 select_reduce_fusion.1.refs_0_
  1.6 17.2 %synth.1 = f32[16,96,128]{2,1,0:T(8,128)} custom-call(s32[32]{0:T(128)} %select_reduce_fusion.1.refs_0_, f32[1024]{0:T(1024)} %constant.47.clone.refs_1_, f32[6,32,512]{2,1,0:T(8,128)} %bitcast.7, f32[8,512]{1,0:T(8,128)} %constant.45.clone.refs_3_.refs_2_, bf16[128,1024]{1,0:T(8,128)(2,1)} %constant.46.clone.refs_4_, s32[1,1024]{1,0:T(1,128)} %bitcast.4), custom_call_target="tpu_custom_call" | custom-call | flops 15000000512 | bytes 1048576 | tf_op jit(solution)/shard_map/synth/pallas_call | solution.py:638
  18.9 0.0 copy-start.1
  18.9 0.0 copy-start.3
  18.9 0.0 copy-start.4
  18.9 7.3 %all-to-all-start = ((f32[16,96,128]{2,1,0:T(8,128)}), f32[16,96,128]{2,1,0:T(8,128)S(1)}, u32[]{:S(2)}, u32[]{:S(2)}) async-start(f32[16,96,128]{2,1,0:T(8,128)} %synth.1), calls=%async_computation | async-start | bytes 1572864 | tf_op jit(solution)/shard_map/all_to_all | solution.py:636
  26.2 0.0 copy-done.6
  26.2 0.1 lt.46
  26.3 0.5 convert_reduce_fusion
  26.8 0.3 select_reduce_fusion
  27.1 0.1 reshape.188
  27.2 0.0 copy-done
  27.2 0.1 multiply_sine_fusion
  27.4 2.5 %trig.1.refs_4_ = bf16[4,2,2,512,256]{4,3,2,1,0:T(8,128)(2,1)S(1)} custom-call(), custom_call_target="tpu_custom_call" | custom-call | flops 4000000000 | bytes 1048576 | tf_op jit(solution)/shard_map/trig/pallas_call | solution.py:668
  29.8 0.0 copy-start.5
  29.9 1.9 %copy-done.5 = bf16[4,2,2,512,256]{4,3,2,1,0:T(8,128)(2,1)} copy-done((bf16[4,2,2,512,256]{4,3,2,1,0:T(8,128)(2,1)}, bf16[4,2,2,512,256]{4,3,2,1,0:T(8,128)(2,1)S(1)}, u32[]{:S(2)}) %copy-start.5) | copy-done | bytes 4194328
  31.8 14.2 %all-to-all-done.refs_0_ = f32[16,96,128]{2,1,0:T(8,128)S(1)} async-done(((f32[16,96,128]{2,1,0:T(8,128)}), f32[16,96,128]{2,1,0:T(8,128)S(1)}, u32[]{:S(2)}, u32[]{:S(2)}) %all-to-all-start) | async-done | bytes 786464 | tf_op jit(solution)/shard_map/all_to_all | solution.py:636
  46.0 0.1 broadcast_in_dim.54.refs_3_
  46.1 0.1 broadcast_in_dim.34.refs_1_
  46.2 0.0 copy-done.2
  46.2 7.0 %grid.1 = f32[16,104,128]{2,1,0:T(8,128)} custom-call(f32[16,96,128]{2,1,0:T(8,128)S(1)} %all-to-all-done.refs_0_, s32[512,128]{1,0:T(8,128)S(1)} %broadcast_in_dim.34.refs_1_, f32[64,2048]{1,0:T(8,128)S(1)} %bitcast.6, f32[64,128]{1,0:T(8,128)S(1)} %broadcast_in_dim.54.refs_3_, bf16[4,2,2,512,256]{4,3,2,1,0:T(8,128)(2,1)} %copy-done.5), custom_call_target="tpu_custom_call" | custom-call | flops 8000000000 | bytes 1048576 | tf_op jit(solution)/shard_map/grid/pallas_call | solution.py:685
  53.2 4.9 %all-to-all-start.1 = ((f32[16,104,128]{2,1,0:T(8,128)}), f32[16,104,128]{2,1,0:T(8,128)S(1)}, u32[]{:S(2)}, u32[]{:S(2)}) async-start(f32[16,104,128]{2,1,0:T(8,128)} %grid.1), calls=%async_computation.1 | async-start | bytes 1703936 | tf_op jit(solution)/shard_map/all_to_all | solution.py:636
  58.1 0.0 copy-done.1
  58.1 0.0 copy-done.3
  58.1 0.0 copy-done.4
  58.1 12.2 %table.1 = (bf16[4,8,512,1024]{3,2,1,0:T(8,128)(2,1)}, f32[32,512]{1,0:T(8,128)S(1)}) custom-call(s32[32]{0:T(128)S(1)} %copy-done.1, f32[1024]{0:T(1024)S(1)} %copy-done.4, f32[8,512]{1,0:T(8,128)S(1)} %copy-done.3), custom_call_target="tpu_custom_call" | custom-call | flops 12000000000 | bytes 1048576 | tf_op jit(solution)/shard_map/table/pallas_call | solution.py:705
  70.3 7.6 %all-to-all-done.1.refs_1_ = f32[16,104,128]{2,1,0:T(8,128)S(1)} async-done(((f32[16,104,128]{2,1,0:T(8,128)}), f32[16,104,128]{2,1,0:T(8,128)S(1)}, u32[]{:S(2)}, u32[]{:S(2)}) %all-to-all-start.1) | async-done | bytes 852000 | tf_op jit(solution)/shard_map/all_to_all | solution.py:636
  77.9 0.2 broadcast_in_dim.55.refs_2_
  78.1 12.9 %analyze.1 = f32[6,32,512]{2,1,0:T(8,128)} custom-call(s32[32]{0:T(128)S(1)} %copy-done.1, f32[16,104,128]{2,1,0:T(8,128)S(1)} %all-to-all-done.1.refs_1_, s32[1024,128]{1,0:T(8,128)S(1)} %broadcast_in_dim.55.refs_2_, s32[1,1024]{1,0:T(1,128)S(1)} %bitcast.5, f32[32,512]{1,0:T(8,128)S(1)} %get-tuple-element.7.refs_4_, ...), custom_call_target="tpu_custom_call" | custom-call | flops 8999999488 | bytes 1048576 | tf_op jit(solution)/shard_map/analyze/pallas_call | solution.py:720
  (4 shorter events, 0.0 us)
Async XLA Ops:
  0.0 26.2 %copy-start.6 = (s32[512]{0:T(512)S(1)}, s32[512]{0:T(512)}, u32[]{:S(2)}) copy-start(s32[512]{0:T(512)} %param.10) | copy-start | bytes 6148
  0.0 27.2 %copy-start = (s32[1024]{0:T(1024)S(1)}, s32[1024]{0:T(1024)}, u32[]{:S(2)}) copy-start(s32[1024]{0:T(1024)} %param.9) | copy-start | bytes 12292
  1.6 44.5 %copy-start.2 = (f32[1,64,2048]{2,1,0:T(8,128)S(1)}, f32[1,64,2048]{2,1,0:T(8,128)}, u32[]{:S(2)}) copy-start(f32[1,64,2048]{2,1,0:T(8,128)} %param.8) | copy-start | bytes 1572868
  18.9 39.2 %copy-start.1 = (s32[32]{0:T(128)S(1)}, s32[32]{0:T(128)}, u32[]{:S(2)}) copy-start(s32[32]{0:T(128)} %select_reduce_fusion.1.refs_0_) | copy-start | bytes 388
  18.9 39.2 %copy-start.3 = (f32[8,512]{1,0:T(8,128)S(1)}, f32[8,512]{1,0:T(8,128)}, u32[]{:S(2)}) copy-start(f32[8,512]{1,0:T(8,128)} %constant.45.clone.refs_3_.refs_2_) | copy-start | bytes 49156
  18.9 39.2 %copy-start.4 = (f32[1024]{0:T(1024)S(1)}, f32[1024]{0:T(1024)}, u32[]{:S(2)}) copy-start(f32[1024]{0:T(1024)} %constant.47.clone.refs_1_) | copy-start | bytes 12292
  18.9 27.1 %all-to-all-start = ((f32[16,96,128]{2,1,0:T(8,128)}), f32[16,96,128]{2,1,0:T(8,128)S(1)}, u32[]{:S(2)}, u32[]{:S(2)}) async-start(f32[16,96,128]{2,1,0:T(8,128)} %synth.1), calls=%async_computation | async-start | bytes 1572864 | tf_op jit(solution)/shard_map/all_to_all | solution.py:636
  29.8 1.9 %copy-start.5 = (bf16[4,2,2,512,256]{4,3,2,1,0:T(8,128)(2,1)}, bf16[4,2,2,512,256]{4,3,2,1,0:T(8,128)(2,1)S(1)}, u32[]{:S(2)}) copy-start(bf16[4,2,2,512,256]{4,3,2,1,0:T(8,128)(2,1)S(1)} %trig.1.refs_4_) | copy-start | bytes 12582916
  53.2 24.7 %all-to-all-start.1 = ((f32[16,104,128]{2,1,0:T(8,128)}), f32[16,104,128]{2,1,0:T(8,128)S(1)}, u32[]{:S(2)}, u32[]{:S(2)}) async-start(f32[16,104,128]{2,1,0:T(8,128)} %grid.1), calls=%async_computation.1 | async-start | bytes 1703936 | tf_op jit(solution)/shard_map/all_to_all | solution.py:636

commit v13 on v12

--- a/solution.py
+++ b/solution.py
@@ -174,6 +174,11 @@
     diagonal = (lane % BLK) == (sub % BLK)
     width = (CHUNK // 2) * BLK
 
+    chunks = DEG // CHUNK
+    high_b[...] = jnp.zeros_like(high_b)
+    low_b[...] = jnp.zeros_like(low_b)
+    lhs_ref[chunks] = jnp.zeros((2 * ROWS, CHUNK * BLK), BF)
+
     def one_block(block, unused):
         orders, first, last = block_orders(slots_ref, block * BLK)
         column = orders[:, :1]
@@ -227,14 +232,11 @@
 
         def two_chunks(guard, pair, carry):
             step = 2 * pair
-            beside = add_products(jnp.maximum(step - 1, 0), high_b, low_b)
+            beside = add_products(jnp.where(step == 0, chunks, step - 1), high_b, low_b)
             carry = recur(step, carry, high_a, low_a, beside, guard)
             beside = add_products(step, high_a, low_a)
             return recur(step + 1, carry, high_b, low_b, beside, guard)
 
-        high_b[...] = jnp.zeros_like(high_b)
-        low_b[...] = jnp.zeros_like(low_b)
-        chunks = DEG // CHUNK
         state = lax.fori_loop(
             0,
             first & 1,
@@ -649,7 +651,7 @@
             pltpu.SemaphoreType.DMA((5,)),
         ]
         + [per_order] * 3
-        + [pltpu.VMEM((chunks, 2 * ROWS, CHUNK * BLK), BF)]
+        + [pltpu.VMEM((chunks + 1, 2 * ROWS, CHUNK * BLK), BF)]
         + [pltpu.VMEM((2, CHUNK // 2 * BLK, HALF), BF)] * 4
         + [
             pltpu.VMEM((blocks, 2, ROWS, HALF), F32),

time: 91.1 us -> 91 us (level)
  Pallas kernels: 51.8 us -> 50.6 us
where the time goes in v13:
time: 91 us; the launch traced here: 90.7 us
  Pallas kernels  50.6 us (56%)
  waiting for transfers between devices  22.2 us (24%)
  starting transfers between devices  12.4 us (14%)
  other arithmetic  2.57 us (3%)
  local copies, waits for them, and re-layouts  2.5 us (3%)
    all_to_all x2, waiting for transfers between devices, exchange(): lax.all_to_all(value, 'band', split_axis=0, concat_axis=0, tiled=True)  22.2 us
    pallas_call x1, Pallas kernels, per_device(): pl.pallas_call(lambda *refs: synth_kernel(dims, *refs), out_shape=jax.Sha...  16.8 us
    pallas_call x1, Pallas kernels, per_device(): pl.pallas_call(lambda *refs: analyze_kernel(dims, chunk_rows, *refs), out...  12.6 us
    all_to_all x2, starting transfers between devices, exchange(): lax.all_to_all(value, 'band', split_axis=0, concat_axis=0, tiled=True)  12.4 us
    pallas_call x1, Pallas kernels, per_device(): pl.pallas_call(lambda *refs: table_kernel(blocks, *refs), out_shape=[jax....  11.7 us
    pallas_call x1, Pallas kernels, per_device(): pl.pallas_call(lambda *refs: grid_kernel(grid_dims, *refs), out_shape=jax...  6.98 us
    pallas_call x1, Pallas kernels, per_device(): pl.pallas_call(trig_kernel, out_shape=jax.ShapeDtypeStruct(trig_shape, BF...  2.47 us
    unnamed x14, local copies, waits for them, and re-layouts  1.96 us
  transfers between devices with their start and end apart: 2, of which 2 were waited for; matrix products, arithmetic and copies ran while one was open for 1% of the time, Pallas kernels for 16%

profile of v13, /device:TPU:0, one launch (start us, length us, event | category | flops | bytes accessed | tf_op | source)
XLA Modules:
  0.0 90.7 jit_solution(4974590686586250192)
XLA Ops:
  0.0 0.0 copy-start.6
  0.0 0.8 iota_add_fusion.1
  0.8 0.2 convert_reduce_fusion.1
  1.0 0.6 select_reduce_fusion.1.refs_0_
  1.6 16.8 %synth.1 = f32[16,96,128]{2,1,0:T(8,128)} custom-call(s32[32]{0:T(128)} %select_reduce_fusion.1.refs_0_, f32[1024]{0:T(1024)} %constant.47.clone.refs_1_, f32[6,32,512]{2,1,0:T(8,128)} %bitcast.7, f32[8,512]{1,0:T(8,128)} %constant.45.clone.refs_3_.refs_2_, bf16[128,1024]{1,0:T(8,128)(2,1)} %constant.46.clone.refs_4_, s32[1,1024]{1,0:T(1,128)} %bitcast.4), custom_call_target="tpu_custom_call" | custom-call | flops 15000000512 | bytes 1048576 | tf_op jit(solution)/shard_map/synth/pallas_call | solution.py:640
  18.5 0.0 copy-start.1
  18.5 0.0 copy-start.3
  18.5 0.0 copy-start.4
  18.5 7.5 %all-to-all-start = ((f32[16,96,128]{2,1,0:T(8,128)}), f32[16,96,128]{2,1,0:T(8,128)S(1)}, u32[]{:S(2)}, u32[]{:S(2)}) async-start(f32[16,96,128]{2,1,0:T(8,128)} %synth.1), calls=%async_computation | async-start | bytes 1572864 | tf_op jit(solution)/shard_map/all_to_all | solution.py:638
  26.0 0.0 copy-done.6
  26.0 0.1 lt.46
  26.1 0.5 convert_reduce_fusion
  26.5 0.3 select_reduce_fusion
  26.9 0.1 reshape.188
  27.0 0.0 copy-done
  27.0 0.1 multiply_sine_fusion
  27.1 2.5 %trig.1.refs_4_ = bf16[4,2,2,512,256]{4,3,2,1,0:T(8,128)(2,1)S(1)} custom-call(), custom_call_target="tpu_custom_call" | custom-call | flops 4000000000 | bytes 1048576 | tf_op jit(solution)/shard_map/trig/pallas_call | solution.py:670
  29.6 0.0 copy-start.5
  29.6 1.9 %copy-done.5 = bf16[4,2,2,512,256]{4,3,2,1,0:T(8,128)(2,1)} copy-done((bf16[4,2,2,512,256]{4,3,2,1,0:T(8,128)(2,1)}, bf16[4,2,2,512,256]{4,3,2,1,0:T(8,128)(2,1)S(1)}, u32[]{:S(2)}) %copy-start.5) | copy-done | bytes 4194328
  31.5 14.2 %all-to-all-done.refs_0_ = f32[16,96,128]{2,1,0:T(8,128)S(1)} async-done(((f32[16,96,128]{2,1,0:T(8,128)}), f32[16,96,128]{2,1,0:T(8,128)S(1)}, u32[]{:S(2)}, u32[]{:S(2)}) %all-to-all-start) | async-done | bytes 786464 | tf_op jit(solution)/shard_map/all_to_all | solution.py:638
  45.7 0.1 broadcast_in_dim.54.refs_3_
  45.8 0.1 broadcast_in_dim.34.refs_1_
  46.0 0.0 copy-done.2
  46.0 7.0 %grid.1 = f32[16,104,128]{2,1,0:T(8,128)} custom-call(f32[16,96,128]{2,1,0:T(8,128)S(1)} %all-to-all-done.refs_0_, s32[512,128]{1,0:T(8,128)S(1)} %broadcast_in_dim.34.refs_1_, f32[64,2048]{1,0:T(8,128)S(1)} %bitcast.6, f32[64,128]{1,0:T(8,128)S(1)} %broadcast_in_dim.54.refs_3_, bf16[4,2,2,512,256]{4,3,2,1,0:T(8,128)(2,1)} %copy-done.5), custom_call_target="tpu_custom_call" | custom-call | flops 8000000000 | bytes 1048576 | tf_op jit(solution)/shard_map/grid/pallas_call | solution.py:687
  53.0 4.9 %all-to-all-start.1 = ((f32[16,104,128]{2,1,0:T(8,128)}), f32[16,104,128]{2,1,0:T(8,128)S(1)}, u32[]{:S(2)}, u32[]{:S(2)}) async-start(f32[16,104,128]{2,1,0:T(8,128)} %grid.1), calls=%async_computation.1 | async-start | bytes 1703936 | tf_op jit(solution)/shard_map/all_to_all | solution.py:638
  57.9 0.0 copy-done.1
  57.9 0.0 copy-done.3
  57.9 0.0 copy-done.4
  57.9 11.7 %table.1 = (bf16[4,8,512,1024]{3,2,1,0:T(8,128)(2,1)}, f32[32,512]{1,0:T(8,128)S(1)}) custom-call(s32[32]{0:T(128)S(1)} %copy-done.1, f32[1024]{0:T(1024)S(1)} %copy-done.4, f32[8,512]{1,0:T(8,128)S(1)} %copy-done.3), custom_call_target="tpu_custom_call" | custom-call | flops 12000000000 | bytes 1048576 | tf_op jit(solution)/shard_map/table/pallas_call | solution.py:707
  69.7 8.0 %all-to-all-done.1.refs_1_ = f32[16,104,128]{2,1,0:T(8,128)S(1)} async-done(((f32[16,104,128]{2,1,0:T(8,128)}), f32[16,104,128]{2,1,0:T(8,128)S(1)}, u32[]{:S(2)}, u32[]{:S(2)}) %all-to-all-start.1) | async-done | bytes 852000 | tf_op jit(solution)/shard_map/all_to_all | solution.py:638
  77.7 0.2 broadcast_in_dim.55.refs_2_
  77.8 12.6 %analyze.1 = f32[6,32,512]{2,1,0:T(8,128)} custom-call(s32[32]{0:T(128)S(1)} %copy-done.1, f32[16,104,128]{2,1,0:T(8,128)S(1)} %all-to-all-done.1.refs_1_, s32[1024,128]{1,0:T(8,128)S(1)} %broadcast_in_dim.55.refs_2_, s32[1,1024]{1,0:T(1,128)S(1)} %bitcast.5, f32[32,512]{1,0:T(8,128)S(1)} %get-tuple-element.7.refs_4_, ...), custom_call_target="tpu_custom_call" | custom-call | flops 8999999488 | bytes 1048576 | tf_op jit(solution)/shard_map/analyze/pallas_call | solution.py:722
  (4 shorter events, 0.0 us)
Async XLA Ops:
  0.0 26.0 %copy-start.6 = (s32[512]{0:T(512)S(1)}, s32[512]{0:T(512)}, u32[]{:S(2)}) copy-start(s32[512]{0:T(512)} %param.10) | copy-start | bytes 6148
  0.0 27.0 %copy-start = (s32[1024]{0:T(1024)S(1)}, s32[1024]{0:T(1024)}, u32[]{:S(2)}) copy-start(s32[1024]{0:T(1024)} %param.9) | copy-start | bytes 12292
  1.6 44.3 %copy-start.2 = (f32[1,64,2048]{2,1,0:T(8,128)S(1)}, f32[1,64,2048]{2,1,0:T(8,128)}, u32[]{:S(2)}) copy-start(f32[1,64,2048]{2,1,0:T(8,128)} %param.8) | copy-start | bytes 1572868
  18.5 39.4 %copy-start.1 = (s32[32]{0:T(128)S(1)}, s32[32]{0:T(128)}, u32[]{:S(2)}) copy-start(s32[32]{0:T(128)} %select_reduce_fusion.1.refs_0_) | copy-start | bytes 388
  18.5 39.4 %copy-start.3 = (f32[8,512]{1,0:T(8,128)S(1)}, f32[8,512]{1,0:T(8,128)}, u32[]{:S(2)}) copy-start(f32[8,512]{1,0:T(8,128)} %constant.45.clone.refs_3_.refs_2_) | copy-start | bytes 49156
  18.5 39.4 %copy-start.4 = (f32[1024]{0:T(1024)S(1)}, f32[1024]{0:T(1024)}, u32[]{:S(2)}) copy-start(f32[1024]{0:T(1024)} %constant.47.clone.refs_1_) | copy-start | bytes 12292
  18.5 27.3 %all-to-all-start = ((f32[16,96,128]{2,1,0:T(8,128)}), f32[16,96,128]{2,1,0:T(8,128)S(1)}, u32[]{:S(2)}, u32[]{:S(2)}) async-start(f32[16,96,128]{2,1,0:T(8,128)} %synth.1), calls=%async_computation | async-start | bytes 1572864 | tf_op jit(solution)/shard_map/all_to_all | solution.py:638
  29.6 1.9 %copy-start.5 = (bf16[4,2,2,512,256]{4,3,2,1,0:T(8,128)(2,1)}, bf16[4,2,2,512,256]{4,3,2,1,0:T(8,128)(2,1)S(1)}, u32[]{:S(2)}) copy-start(bf16[4,2,2,512,256]{4,3,2,1,0:T(8,128)(2,1)S(1)} %trig.1.refs_4_) | copy-start | bytes 12582916
  53.0 24.7 %all-to-all-start.1 = ((f32[16,104,128]{2,1,0:T(8,128)}), f32[16,104,128]{2,1,0:T(8,128)S(1)}, u32[]{:S(2)}, u32[]{:S(2)}) async-start(f32[16,104,128]{2,1,0:T(8,128)} %grid.1), calls=%async_computation.1 | async-start | bytes 1703936 | tf_op jit(solution)/shard_map/all_to_all | solution.py:638

commit v14 on v12

--- a/solution.py
+++ b/solution.py
@@ -534,7 +534,10 @@
         for parity in range(2):
             part = moved[:, parity * half : (parity + 1) * half]
             lhs_ref[parity, :, kind * half : (kind + 1) * half] = part
-    weight_ref[...] = jnp.zeros_like(weight_ref)
+    if group < padded:
+        empty = jnp.zeros((2, padded - group, NLON // 2), BF)
+        weight_ref[:, group:padded, :] = empty
+        weight_ref[:, padded + group :, :] = empty
     flux_scale = math.pi / (2.0 * NLAT * NLON * DEG)
     weight = jnp.tile(sine_ref[...], (1, KTILE // LANES))
     total = jnp.zeros((8, KTILE), F32)

time: 91.1 us -> 90.8 us (level)
  Pallas kernels: 51.8 us -> 47.4 us
  starting transfers between devices: 12.2 us -> 14.1 us
  waiting for transfers between devices: 21.8 us -> 23.3 us
    all_to_all x2, starting transfers between devices: 12.2 us -> 14.1 us  [exchange(): lax.all_to_all(value, 'band', split_axis=0, concat_axis=0, tiled=True)]
    pallas_call x1, Pallas kernels: 17.2 us -> 15.7 us  [per_device(): pl.pallas_call(lambda *refs: synth_kernel(dims, *refs), out_shape=jax.Sha...]
    all_to_all x2, waiting for transfers between devices: 21.8 us -> 23.3 us  [exchange(): lax.all_to_all(value, 'band', split_axis=0, concat_axis=0, tiled=True)]
    pallas_call x1, Pallas kernels: 12.2 us -> 10.7 us  [per_device(): pl.pallas_call(lambda *refs: table_kernel(blocks, *refs), out_shape=[jax....]
    pallas_call x1, Pallas kernels: 12.9 us -> 11.6 us  [per_device(): pl.pallas_call(lambda *refs: analyze_kernel(dims, chunk_rows, *refs), out...]
  transfers between devices with their start and end apart: 2 -> 2, of which waited for: 2 -> 2; matrix products, arithmetic and copies ran while one was open for 1% -> 1% of each run, Pallas kernels for 16% -> 15%
where the time goes in v14:
time: 90.8 us; the launch traced here: 90.1 us
  Pallas kernels  47.4 us (52%)
  waiting for transfers between devices  23.3 us (26%)
  starting transfers between devices  14.1 us (16%)
  other arithmetic  2.57 us (3%)
  local copies, waits for them, and re-layouts  2.5 us (3%)
    all_to_all x2, waiting for transfers between devices, exchange(): lax.all_to_all(value, 'band', split_axis=0, concat_axis=0, tiled=True)  23.3 us
    pallas_call x1, Pallas kernels, per_device(): pl.pallas_call(lambda *refs: synth_kernel(dims, *refs), out_shape=jax.Sha...  15.7 us
    all_to_all x2, starting transfers between devices, exchange(): lax.all_to_all(value, 'band', split_axis=0, concat_axis=0, tiled=True)  14.1 us
    pallas_call x1, Pallas kernels, per_device(): pl.pallas_call(lambda *refs: analyze_kernel(dims, chunk_rows, *refs), out...  11.6 us
    pallas_call x1, Pallas kernels, per_device(): pl.pallas_call(lambda *refs: table_kernel(blocks, *refs), out_shape=[jax....  10.7 us
    pallas_call x1, Pallas kernels, per_device(): pl.pallas_call(lambda *refs: grid_kernel(grid_dims, *refs), out_shape=jax...  6.98 us
    pallas_call x1, Pallas kernels, per_device(): pl.pallas_call(trig_kernel, out_shape=jax.ShapeDtypeStruct(trig_shape, BF...  2.47 us
    unnamed x14, local copies, waits for them, and re-layouts  1.96 us
  transfers between devices with their start and end apart: 2, of which 2 were waited for; matrix products, arithmetic and copies ran while one was open for 1% of the time, Pallas kernels for 15%

profile of v14, /device:TPU:0, one launch (start us, length us, event | category | flops | bytes accessed | tf_op | source)
XLA Modules:
  0.0 90.1 jit_solution(6348121486223261274)
XLA Ops:
  0.0 0.0 copy-start.6
  0.0 0.8 iota_add_fusion.1
  0.8 0.2 convert_reduce_fusion.1
  1.0 0.6 select_reduce_fusion.1.refs_0_
  1.6 15.7 %synth.1 = f32[16,96,128]{2,1,0:T(8,128)} custom-call(s32[32]{0:T(128)} %select_reduce_fusion.1.refs_0_, f32[1024]{0:T(1024)} %constant.47.clone.refs_1_, f32[6,32,512]{2,1,0:T(8,128)} %bitcast.7, f32[8,512]{1,0:T(8,128)} %constant.45.clone.refs_3_.refs_2_, bf16[128,1024]{1,0:T(8,128)(2,1)} %constant.46.clone.refs_4_, s32[1,1024]{1,0:T(1,128)} %bitcast.4), custom_call_target="tpu_custom_call" | custom-call | flops 15000000512 | bytes 1048576 | tf_op jit(solution)/shard_map/synth/pallas_call | solution.py:641
  17.4 0.0 copy-start.1
  17.4 0.0 copy-start.3
  17.4 0.0 copy-start.4
  17.4 9.1 %all-to-all-start = ((f32[16,96,128]{2,1,0:T(8,128)}), f32[16,96,128]{2,1,0:T(8,128)S(1)}, u32[]{:S(2)}, u32[]{:S(2)}) async-start(f32[16,96,128]{2,1,0:T(8,128)} %synth.1), calls=%async_computation | async-start | bytes 1572864 | tf_op jit(solution)/shard_map/all_to_all | solution.py:639
  26.5 0.0 copy-done.6
  26.5 0.1 lt.46
  26.6 0.5 convert_reduce_fusion
  27.1 0.3 select_reduce_fusion
  27.4 0.1 reshape.188
  27.5 0.0 copy-done
  27.5 0.1 multiply_sine_fusion
  27.7 2.5 %trig.1.refs_4_ = bf16[4,2,2,512,256]{4,3,2,1,0:T(8,128)(2,1)S(1)} custom-call(), custom_call_target="tpu_custom_call" | custom-call | flops 4000000000 | bytes 1048576 | tf_op jit(solution)/shard_map/trig/pallas_call | solution.py:671
  30.1 0.0 copy-start.5
  30.1 1.9 %copy-done.5 = bf16[4,2,2,512,256]{4,3,2,1,0:T(8,128)(2,1)} copy-done((bf16[4,2,2,512,256]{4,3,2,1,0:T(8,128)(2,1)}, bf16[4,2,2,512,256]{4,3,2,1,0:T(8,128)(2,1)S(1)}, u32[]{:S(2)}) %copy-start.5) | copy-done | bytes 4194328
  32.1 14.2 %all-to-all-done.refs_0_ = f32[16,96,128]{2,1,0:T(8,128)S(1)} async-done(((f32[16,96,128]{2,1,0:T(8,128)}), f32[16,96,128]{2,1,0:T(8,128)S(1)}, u32[]{:S(2)}, u32[]{:S(2)}) %all-to-all-start) | async-done | bytes 786464 | tf_op jit(solution)/shard_map/all_to_all | solution.py:639
  46.3 0.1 broadcast_in_dim.54.refs_3_
  46.3 0.1 broadcast_in_dim.34.refs_1_
  46.5 0.0 copy-done.2
  46.5 7.0 %grid.1 = f32[16,104,128]{2,1,0:T(8,128)} custom-call(f32[16,96,128]{2,1,0:T(8,128)S(1)} %all-to-all-done.refs_0_, s32[512,128]{1,0:T(8,128)S(1)} %broadcast_in_dim.34.refs_1_, f32[64,2048]{1,0:T(8,128)S(1)} %bitcast.6, f32[64,128]{1,0:T(8,128)S(1)} %broadcast_in_dim.54.refs_3_, bf16[4,2,2,512,256]{4,3,2,1,0:T(8,128)(2,1)} %copy-done.5), custom_call_target="tpu_custom_call" | custom-call | flops 8000000000 | bytes 1048576 | tf_op jit(solution)/shard_map/grid/pallas_call | solution.py:688
  53.5 4.9 %all-to-all-start.1 = ((f32[16,104,128]{2,1,0:T(8,128)}), f32[16,104,128]{2,1,0:T(8,128)S(1)}, u32[]{:S(2)}, u32[]{:S(2)}) async-start(f32[16,104,128]{2,1,0:T(8,128)} %grid.1), calls=%async_computation.1 | async-start | bytes 1703936 | tf_op jit(solution)/shard_map/all_to_all | solution.py:639
  58.4 0.0 copy-done.1
  58.4 0.0 copy-done.3
  58.4 0.0 copy-done.4
  58.4 10.7 %table.1 = (bf16[4,8,512,1024]{3,2,1,0:T(8,128)(2,1)}, f32[32,512]{1,0:T(8,128)S(1)}) custom-call(s32[32]{0:T(128)S(1)} %copy-done.1, f32[1024]{0:T(1024)S(1)} %copy-done.4, f32[8,512]{1,0:T(8,128)S(1)} %copy-done.3), custom_call_target="tpu_custom_call" | custom-call | flops 12000000000 | bytes 1048576 | tf_op jit(solution)/shard_map/table/pallas_call | solution.py:708
  69.1 9.1 %all-to-all-done.1.refs_1_ = f32[16,104,128]{2,1,0:T(8,128)S(1)} async-done(((f32[16,104,128]{2,1,0:T(8,128)}), f32[16,104,128]{2,1,0:T(8,128)S(1)}, u32[]{:S(2)}, u32[]{:S(2)}) %all-to-all-start.1) | async-done | bytes 852000 | tf_op jit(solution)/shard_map/all_to_all | solution.py:639
  78.2 0.2 broadcast_in_dim.55.refs_2_
  78.4 11.6 %analyze.1 = f32[6,32,512]{2,1,0:T(8,128)} custom-call(s32[32]{0:T(128)S(1)} %copy-done.1, f32[16,104,128]{2,1,0:T(8,128)S(1)} %all-to-all-done.1.refs_1_, s32[1024,128]{1,0:T(8,128)S(1)} %broadcast_in_dim.55.refs_2_, s32[1,1024]{1,0:T(1,128)S(1)} %bitcast.5, f32[32,512]{1,0:T(8,128)S(1)} %get-tuple-element.7.refs_4_, ...), custom_call_target="tpu_custom_call" | custom-call | flops 8999999488 | bytes 1048576 | tf_op jit(solution)/shard_map/analyze/pallas_call | solution.py:723
  (4 shorter events, 0.0 us)
Async XLA Ops:
  0.0 26.5 %copy-start.6 = (s32[512]{0:T(512)S(1)}, s32[512]{0:T(512)}, u32[]{:S(2)}) copy-start(s32[512]{0:T(512)} %param.10) | copy-start | bytes 6148
  0.0 27.5 %copy-start = (s32[1024]{0:T(1024)S(1)}, s32[1024]{0:T(1024)}, u32[]{:S(2)}) copy-start(s32[1024]{0:T(1024)} %param.9) | copy-start | bytes 12292
  1.6 44.8 %copy-start.2 = (f32[1,64,2048]{2,1,0:T(8,128)S(1)}, f32[1,64,2048]{2,1,0:T(8,128)}, u32[]{:S(2)}) copy-start(f32[1,64,2048]{2,1,0:T(8,128)} %param.8) | copy-start | bytes 1572868
  17.4 41.0 %copy-start.1 = (s32[32]{0:T(128)S(1)}, s32[32]{0:T(128)}, u32[]{:S(2)}) copy-start(s32[32]{0:T(128)} %select_reduce_fusion.1.refs_0_) | copy-start | bytes 388
  17.4 41.0 %copy-start.3 = (f32[8,512]{1,0:T(8,128)S(1)}, f32[8,512]{1,0:T(8,128)}, u32[]{:S(2)}) copy-start(f32[8,512]{1,0:T(8,128)} %constant.45.clone.refs_3_.refs_2_) | copy-start | bytes 49156
  17.4 41.0 %copy-start.4 = (f32[1024]{0:T(1024)S(1)}, f32[1024]{0:T(1024)}, u32[]{:S(2)}) copy-start(f32[1024]{0:T(1024)} %constant.47.clone.refs_1_) | copy-start | bytes 12292
  17.4 28.9 %all-to-all-start = ((f32[16,96,128]{2,1,0:T(8,128)}), f32[16,96,128]{2,1,0:T(8,128)S(1)}, u32[]{:S(2)}, u32[]{:S(2)}) async-start(f32[16,96,128]{2,1,0:T(8,128)} %synth.1), calls=%async_computation | async-start | bytes 1572864 | tf_op jit(solution)/shard_map/all_to_all | solution.py:639
  30.1 1.9 %copy-start.5 = (bf16[4,2,2,512,256]{4,3,2,1,0:T(8,128)(2,1)}, bf16[4,2,2,512,256]{4,3,2,1,0:T(8,128)(2,1)S(1)}, u32[]{:S(2)}) copy-start(bf16[4,2,2,512,256]{4,3,2,1,0:T(8,128)(2,1)S(1)} %trig.1.refs_4_) | copy-start | bytes 12582916
  53.5 24.7 %all-to-all-start.1 = ((f32[16,104,128]{2,1,0:T(8,128)}), f32[16,104,128]{2,1,0:T(8,128)S(1)}, u32[]{:S(2)}, u32[]{:S(2)}) async-start(f32[16,104,128]{2,1,0:T(8,128)} %grid.1), calls=%async_computation.1 | async-start | bytes 1703936 | tf_op jit(solution)/shard_map/all_to_all | solution.py:639
